TPU v7x, 32 devices: a whole 2x2x4 slice. The times are simulated.
32 devices in a mesh: prow: 4 (over y, core), pcol: 8 (over z, x).
Axes of the slice: x: 2, y: 2, z: 4, core: 2. Of those that a mesh axis runs over, the one named last changes fastest.
Arguments:
- matrix: bfloat16 [4096, 4096], P('prow', 'pcol'), may hold values from -6 to 6
- panels: bfloat16 [4, 256, 4096], P(None, 'pcol', 'prow'), may hold values from -0.375 to 0.375
- exponents: int32 [4, 32], P(None, 'prow'), may hold values from -3 to 1
- inverses: bfloat16 [4, 256, 256], replicated, as said below
- pivots: int32 [4, 256], replicated, may hold values from 1024 to 4095, as said below
Outputs:
- updated: bfloat16 [4096, 4096], P('prow', 'pcol')
Inputs may be any that keep to these rules, and one draw needn't show every extreme that they name: `pivots`: within one step the 256 pivot rows are distinct; their owners along the rows are uneven. `inverses`: each block is unit lower triangular.
All inputs are finite; a program needn't handle non-finite values.
Results may differ from a plain program's by a relative error of at most 0.0075.
Values may be sent and summed in bfloat16 or wider, within the bound.
No kernel may reach another device: no remote copies, remote signals or barrier semaphores. Data moves between devices by JAX's collectives and lax.ppermute only.
A program may use at most 64 MiB of HBM per device.

v0:
```python
import jax
import jax.numpy as jnp
from jax import lax
from jax.sharding import PartitionSpec as P


def broadcast(value, axis, root):
    mine = lax.axis_index(axis) == root
    return lax.psum(jnp.where(mine, value, jnp.zeros_like(value)), axis)


def on_device(matrix, panels, exponents, inverses, pivots):
    row_dev = matrix.shape[0]
    width = inverses.shape[1]
    steps = pivots.shape[0]
    tile = row_dev // exponents.shape[1]
    first_row = lax.axis_index("prow") * row_dev
    global_rows = first_row + jnp.arange(row_dev, dtype=jnp.int32)
    positions = jnp.arange(width, dtype=jnp.int32)
    current = matrix
    for step in range(steps):
        top = step * width
        root = top // row_dev
        offset = top - root * row_dev
        top_block = current[offset : offset + width]
        upper = broadcast(top_block, "prow", root)
        local_piv = pivots[step] - first_row
        owned = (local_piv >= 0) & (local_piv < row_dev)
        picked = jnp.where(
            owned[:, None],
            current[jnp.clip(local_piv, 0, row_dev - 1)],
            jnp.zeros((), jnp.bfloat16),
        )
        chosen = lax.psum(picked, "prow").astype(jnp.float32).astype(jnp.bfloat16)
        solved = jnp.dot(inverses[step], chosen, preferred_element_type=jnp.float32).astype(
            jnp.bfloat16
        )
        matches = global_rows[:, None] == pivots[step][None, :]
        is_pivot = jnp.any(matches, axis=1)
        which = jnp.sum(jnp.where(matches, positions[None, :], 0), axis=1)
        swapped = jnp.where(is_pivot[:, None], upper[which], current)
        in_top = (global_rows >= top) & (global_rows < top + width)
        swapped = jnp.where(
            in_top[:, None], solved[jnp.clip(global_rows - top, 0, width - 1)], swapped
        )
        factor = jnp.repeat(jnp.exp2(exponents[step].astype(jnp.float32)), tile).astype(
            jnp.bfloat16
        )
        change = lax.dot_general(
            lax.all_gather(panels[step], "pcol", axis=0, tiled=True) * factor[None, :],
            solved,
            (((0,), (0,)), ((), ())),
            preferred_element_type=jnp.float32,
        )
        keep = global_rows >= top + width
        refreshed = (swapped.astype(jnp.float32) - change).astype(jnp.bfloat16)
        current = jnp.where(keep[:, None], refreshed, swapped)
    return current


def solution(mesh):
    return jax.shard_map(
        on_device,
        mesh=mesh,
        in_specs=(P("prow", "pcol"), P(None, "pcol", "prow"), P(None, "prow"), P(), P()),
        out_specs=P("prow", "pcol"),
        check_vma=False,
    )
```

profile of v0, /device:TPU:0, one launch (start us, length us, event | category | flops | bytes accessed | tf_op | source)
XLA Modules:
  0.0 227.1 jit_solution(692898121099988300)
XLA Ops:
  6.5 0.8 fusion.34
  7.4 0.8 compare_select_fusion.12
  8.3 2.7 %gather_fusion = bf16[256,512]{1,0:T(8,128)(2,1)S(1)} fusion(bf16[1024,512]{1,0:T(8,128)(2,1)} %param.5, s32[1024]{0:T(1024)S(1)} %pad_clamp_fusion.3), kind=kCustom, calls=%fused_computation | custom fusion | bytes 525312 | tf_op jit(solution)/shard_map/gather | solution.py:31
  11.0 0.9 slice_select_fusion.3
  12.7 1.4 compare_reduce_fusion
  22.7 35.3 %all-gather = bf16[1,256,1024]{2,1,0:T(8,128)(2,1)} all-gather(bf16[1,32,1024]{2,1,0:T(8,128)(2,1)S(1)} %get-tuple-element.23), channel_id=2, replica_groups=mesh['prow'=4,'pcol'=8] {'pcol'}, dimensions={1}, use_global_device_ids=true | all-gather | bytes 589824 | tf_op jit(solution)/shard_map/all_gather | solution.py:50
  58.0 1.3 convolution_convert_fusion.3
  59.4 4.0 %gather_fusion.2 = bf16[1024,512]{1,0:T(8,128)(2,1)S(1)} fusion(bf16[256,512]{1,0:T(8,128)(2,1)S(1)} %copy-done, s32[1024]{0:T(1024)S(1)} %broadcast_clamp_fusion.6), kind=kCustom, calls=%fused_computation.2 | custom fusion | bytes 2101248 | tf_op jit(solution)/shard_map/gather | solution.py:41
  63.4 5.1 %gather_fusion.1 = bf16[1024,512]{1,0:T(8,128)(2,1)} fusion(bf16[256,512]{1,0:T(8,128)(2,1)S(1)} %copy.14, s32[1024]{0:T(1024)S(1)} %broadcast_clamp_fusion.7), kind=kCustom, calls=%fused_computation.1 | custom fusion | bytes 2101248 | tf_op jit(solution)/shard_map/gather | solution.py:44
  68.5 2.2 fusion
  70.7 0.8 slice_select_fusion.2
  71.5 1.4 gather_fusion.3
  72.9 0.8 broadcast_select_fusion.1
  74.4 33.3 %all-gather.1 = bf16[1,256,1024]{2,1,0:T(8,128)(2,1)} all-gather(bf16[1,32,1024]{2,1,0:T(8,128)(2,1)S(1)} %copy-done.9), channel_id=3, replica_groups=mesh['prow'=4,'pcol'=8] {'pcol'}, dimensions={1}, use_global_device_ids=true | all-gather | bytes 589824 | tf_op jit(solution)/shard_map/all_gather | solution.py:50
  108.1 1.2 convolution_convert_fusion.2
  109.5 4.0 %gather_fusion.4 = bf16[1024,512]{1,0:T(8,128)(2,1)S(1)} fusion(bf16[256,512]{1,0:T(8,128)(2,1)S(1)} %copy.15, s32[1024]{0:T(1024)S(1)} %copy-done.10), kind=kCustom, calls=%fused_computation.4 | custom fusion | bytes 2101248 | tf_op jit(solution)/shard_map/gather | solution.py:44
  113.5 5.1 %gather_fusion.5 = bf16[1024,512]{1,0:T(8,128)(2,1)} fusion(bf16[256,512]{1,0:T(8,128)(2,1)S(1)} %copy-done.1, s32[1024]{0:T(1024)S(1)} %copy-done.11), kind=kCustom, calls=%fused_computation.5 | custom fusion | bytes 2101248 | tf_op jit(solution)/shard_map/gather | solution.py:41
  118.6 2.2 fusion.1
  121.5 1.4 gather_fusion.6
  123.0 0.8 broadcast_select_fusion.2
  124.4 33.3 %all-gather.2 = bf16[1,256,1024]{2,1,0:T(8,128)(2,1)} all-gather(bf16[1,32,1024]{2,1,0:T(8,128)(2,1)S(1)} %get-tuple-element.24), channel_id=4, replica_groups=mesh['prow'=4,'pcol'=8] {'pcol'}, dimensions={1}, use_global_device_ids=true | all-gather | bytes 589824 | tf_op jit(solution)/shard_map/all_gather | solution.py:50
  158.1 1.2 convolution_convert_fusion.1
  159.5 4.0 %gather_fusion.7 = bf16[1024,512]{1,0:T(8,128)(2,1)S(1)} fusion(bf16[256,512]{1,0:T(8,128)(2,1)S(1)} %copy.16, s32[1024]{0:T(1024)S(1)} %broadcast_clamp_fusion.3), kind=kCustom, calls=%fused_computation.7 | custom fusion | bytes 2101248 | tf_op jit(solution)/shard_map/gather | solution.py:44
  163.5 5.1 %gather_fusion.8 = bf16[1024,512]{1,0:T(8,128)(2,1)} fusion(bf16[256,512]{1,0:T(8,128)(2,1)S(1)} %copy-done.2, s32[1024]{0:T(1024)S(1)} %broadcast_clamp_fusion.2), kind=kCustom, calls=%fused_computation.8 | custom fusion | bytes 2101248 | tf_op jit(solution)/shard_map/gather | solution.py:41
  168.6 2.2 fusion.2
  171.6 1.4 gather_fusion.9
  173.0 0.8 broadcast_select_fusion.3
  173.8 33.3 %all-gather.3 = bf16[1,256,1024]{2,1,0:T(8,128)(2,1)} all-gather(bf16[1,32,1024]{2,1,0:T(8,128)(2,1)S(1)} %get-tuple-element.21), channel_id=5, replica_groups=mesh['prow'=4,'pcol'=8] {'pcol'}, dimensions={1}, use_global_device_ids=true | all-gather | bytes 589824 | tf_op jit(solution)/shard_map/all_gather | solution.py:50
  207.5 1.2 convolution_convert_fusion
  209.7 4.0 %gather_fusion.10 = bf16[1024,512]{1,0:T(8,128)(2,1)S(1)} fusion(bf16[256,512]{1,0:T(8,128)(2,1)S(1)} %copy.17, s32[1024]{0:T(1024)S(1)} %broadcast_clamp_fusion.1), kind=kCustom, calls=%fused_computation.10 | custom fusion | bytes 2101248 | tf_op jit(solution)/shard_map/gather | solution.py:44
  213.7 4.0 %gather_fusion.11 = bf16[1024,512]{1,0:T(8,128)(2,1)S(1)} fusion(bf16[256,512]{1,0:T(8,128)(2,1)S(1)} %copy-done.3, s32[1024]{0:T(1024)S(1)} %broadcast_clamp_fusion), kind=kCustom, calls=%fused_computation.11 | custom fusion | bytes 2101248 | tf_op jit(solution)/shard_map/gather | solution.py:41
  217.7 2.9 %fusion.3 = bf16[1024,512]{1,0:T(8,128)(2,1)} fusion(bf16[512,256]{1,0:T(8,128)(2,1)} %copy-done.7, bf16[1024,512]{1,0:T(8,128)(2,1)S(1)} %gather_fusion.10, bf16[1024,512]{1,0:T(8,128)(2,1)S(1)} %gather_fusion.11, bf16[1024,512]{1,0:T(8,128)(2,1)S(1)} %fusion.2, pred[1024]{0:T(1024)(128)(4,1)S(1)} %copy-done.18, ...), kind=kOutput, calls=%fused_computation.19 | convolution fusion | flops 271843328 | bytes 4985856 | tf_op jit(solution)/shard_map/dot_general | solution.py:49
  (98 shorter events, 14.7 us)
Async XLA Ops:
  6.5 51.4 %all-reduce.15.cloned.1.call-start = ((), (), s32[]{:S(2)}) async-start(), calls=%async_computation.3 | async-start | bytes 1048576 | tf_op jit(solution)/shard_map/psum | solution.py:34
  8.3 2.7 %copy-start.4 = (bf16[1024,512]{1,0:T(8,128)(2,1)S(1)}, bf16[1024,512]{1,0:T(8,128)(2,1)}, u32[]{:S(2)}) copy-start(bf16[1024,512]{1,0:T(8,128)(2,1)} %param.5) | copy-start | bytes 3145732
  10.9 4.8 %copy-start.8 = (bf16[4,32,1024]{2,1,0:T(8,128)(2,1)S(1)}, bf16[4,32,1024]{2,1,0:T(8,128)(2,1)}, u32[]{:S(2)}) copy-start(bf16[4,32,1024]{2,1,0:T(8,128)(2,1)} %param.6) | copy-start | bytes 786436
  11.0 5.5 %copy-start.17 = (s32[4,8]{1,0:T(4,128)S(1)}, s32[4,8]{1,0:T(4,128)}, u32[]{:S(2)}) copy-start(s32[4,8]{1,0:T(4,128)} %param.7) | copy-start | bytes 388
  11.9 96.2 %all-reduce.13.cloned.1.call-start = ((), (), s32[]{:S(2)}) async-start(), calls=%async_computation.2 | async-start | bytes 1048576 | tf_op jit(solution)/shard_map/psum | solution.py:34
  58.0 1.4 copy-start
  70.7 2.2 copy-start.5
  71.5 1.4 copy-start.14
  72.9 1.5 copy-start.9
  73.7 35.8 %copy-start.10 = (s32[1024]{0:T(1024)S(1)}, s32[1024]{0:T(1024)}, u32[]{:S(2)}) copy-start(s32[1024]{0:T(1024)} %broadcast_clamp_fusion.5) | copy-start | bytes 12292
  73.8 84.3 %all-reduce.11.cloned.1.call-start = ((), (), s32[]{:S(2)}) async-start(), calls=%async_computation.1 | async-start | bytes 1048576 | tf_op jit(solution)/shard_map/psum | solution.py:34
  109.5 4.0 %copy-start.1 = (bf16[256,512]{1,0:T(8,128)(2,1)S(1)}, bf16[256,512]{1,0:T(8,128)(2,1)}, u32[]{:S(2)}) copy-start(bf16[256,512]{1,0:T(8,128)(2,1)} %get-tuple-element.18) | copy-start | bytes 786436
  109.5 4.0 %copy-start.11 = (s32[1024]{0:T(1024)S(1)}, s32[1024]{0:T(1024)}, u32[]{:S(2)}) copy-start(s32[1024]{0:T(1024)} %broadcast_clamp_fusion.4) | copy-start | bytes 12292
  113.5 5.1 %copy-start.6 = (bf16[1024,512]{1,0:T(8,128)(2,1)S(1)}, bf16[1024,512]{1,0:T(8,128)(2,1)}, u32[]{:S(2)}) copy-start(bf16[1024,512]{1,0:T(8,128)(2,1)} %copy-done.5) | copy-start | bytes 3145732
  121.5 1.4 copy-start.13
  123.8 83.7 %all-reduce.9.cloned.1.call-start = ((), (), s32[]{:S(2)}) async-start(), calls=%async_computation | async-start | bytes 1048576 | tf_op jit(solution)/shard_map/psum | solution.py:34
  159.5 4.0 %copy-start.2 = (bf16[256,512]{1,0:T(8,128)(2,1)S(1)}, bf16[256,512]{1,0:T(8,128)(2,1)}, u32[]{:S(2)}) copy-start(bf16[256,512]{1,0:T(8,128)(2,1)} %get-tuple-element.16) | copy-start | bytes 786436
  163.5 5.1 %copy-start.16 = (bf16[1024]{0:T(1024)(128)(2,1)S(1)}, bf16[1024]{0:T(1024)(128)(2,1)}, u32[]{:S(2)}) copy-start(bf16[1024]{0:T(1024)(128)(2,1)} %broadcast_bitcast_fusion.1) | copy-start | bytes 6148
  163.5 5.1 %copy-start.19 = (pred[1024]{0:T(1024)(128)(4,1)S(1)}, pred[1024]{0:T(1024)(128)(4,1)}, u32[]{:S(2)}) copy-start(pred[1024]{0:T(1024)(128)(4,1)} %get-tuple-element.6) | copy-start | bytes 3076
  163.5 5.1 %copy-start.20 = (pred[1024]{0:T(1024)(128)(4,1)S(1)}, pred[1024]{0:T(1024)(128)(4,1)}, u32[]{:S(2)}) copy-start(pred[1024]{0:T(1024)(128)(4,1)} %get-tuple-element.41) | copy-start | bytes 3076
  163.5 5.1 %copy-start.21 = (pred[1024]{0:T(1024)(128)(4,1)S(1)}, pred[1024]{0:T(1024)(128)(4,1)}, u32[]{:S(2)}) copy-start(pred[1024]{0:T(1024)(128)(4,1)} %get-tuple-element.42) | copy-start | bytes 3076
  171.6 1.4 copy-start.12
  208.8 0.7 copy-start.7
  209.7 4.0 %copy-start.3 = (bf16[256,512]{1,0:T(8,128)(2,1)S(1)}, bf16[256,512]{1,0:T(8,128)(2,1)}, u32[]{:S(2)}) copy-start(bf16[256,512]{1,0:T(8,128)(2,1)} %get-tuple-element.14) | copy-start | bytes 786436
  213.6 4.0 %copy-start.15 = (bf16[1024]{0:T(1024)(128)(2,1)S(1)}, bf16[1024]{0:T(1024)(128)(2,1)}, u32[]{:S(2)}) copy-start(bf16[1024]{0:T(1024)(128)(2,1)} %broadcast_bitcast_fusion) | copy-start | bytes 6148
  213.7 4.0 %copy-start.18 = (pred[1024]{0:T(1024)(128)(4,1)S(1)}, pred[1024]{0:T(1024)(128)(4,1)}, u32[]{:S(2)}) copy-start(pred[1024]{0:T(1024)(128)(4,1)} %get-tuple-element.5) | copy-start | bytes 3076
Sparse Core Ops, SparseCore 0:
  12.0 35.8 all-reduce.14
  73.9 34.1 all-reduce.12
  123.9 34.1 all-reduce.10
  173.9 33.5 all-reduce.8
where the time goes:
time: 228 us; the launch traced here: 227 us
  blocking collectives  135 us (59%)
  local copies, waits for them, and re-layouts  47.4 us (21%)
  other arithmetic  15 us (7%)
  matrix products  14.5 us (6%)
  between operations  13.6 us (6%)
    all_gather x4, blocking collectives, on_device(): lax.all_gather(panels[step], 'pcol', axis=0, tiled=True) * factor[None, :]  135 us
    gather x4, local copies, waits for them, and re-layouts, on_device(): swapped = jnp.where(is_pivot[:, None], upper[which], current)  18.1 us
    gather x4, local copies, waits for them, and re-layouts, on_device(): solved[jnp.clip(global_rows - top, 0, width - 1)]  17 us
    dot_general x4, matrix products, on_device(): lax.dot_general(lax.all_gather(panels[step], 'pcol', axis=0, tiled=True)...  9.48 us
    gather x4, local copies, waits for them, and re-layouts, on_device(): current[jnp.clip(local_piv, 0, row_dev - 1)]  6.92 us
    dot_general x4, matrix products, on_device(): jnp.dot(inverses[step], chosen, preferred_element_type=jnp.float32)  5.02 us
  transfers between devices with their start and end apart: 4, of which 3 were waited for; matrix products, arithmetic and copies ran while one was open for 5% of the time, Pallas kernels for 0%

commit v1 on v0

v1 whole, which is shorter than its diff:
```python
import jax
import jax.numpy as jnp
from jax import lax
from jax.sharding import PartitionSpec as P

CHUNKS = ((0,), (1,), (2, 3))
BF = jnp.bfloat16
F32 = jnp.float32


def xor_pairs(size, mask):
    return [(i, i ^ mask) for i in range(size)]


def swap(value, axis, size, mask):
    return lax.ppermute(value, axis, xor_pairs(size, mask))


def gather_panels(own, size):
    if size != 8:
        me = lax.axis_index("pcol")
        whole = lax.all_gather(own, "pcol", axis=0)
        return [whole[me ^ m] for m in range(size)]
    x0 = swap(own, "pcol", 8, 1)
    z2 = swap(own, "pcol", 8, 4)
    z3 = swap(own, "pcol", 8, 6)
    z1 = swap(own, "pcol", 8, 2)
    z1x = swap(x0, "pcol", 8, 2)
    z2x = swap(z2, "pcol", 8, 1)
    z3x = swap(z3, "pcol", 8, 1)
    return [own, x0, z1, z1x, z2, z2x, z3, z3x]


def trade_rows(mine, here, row, rows_of_prow):
    n = mine.shape[0]
    if rows_of_prow != 4:
        chosen = lax.psum(jnp.where(row == 0, jnp.zeros_like(mine), mine), "prow")
        upper = lax.psum(jnp.where(row == 0, mine, jnp.zeros_like(mine)), "prow")
        return chosen.astype(F32).astype(BF), upper.astype(F32).astype(BF)
    other = swap(mine, "prow", 4, 1)
    low_chip = row < 2
    upper = jnp.where(row == 0, mine, other)
    picked = jnp.where(low_chip, jnp.where(row == 0, other, mine), mine + other)
    message = jnp.where(low_chip & ~here[:, None], upper, picked)
    core = row % 2
    half = n // 2
    first = jnp.where(core == 0, message[:half], message[half:])
    came = swap(first, "prow", 4, 2)
    rest = swap(came, "prow", 4, 1)
    low = jnp.where(core == 0, came, rest)
    high = jnp.where(core == 0, rest, came)
    came = jnp.concatenate([low, high])
    chosen = jnp.where(here[:, None], picked, came)
    upper = jnp.where(low_chip, upper, came)
    return chosen, upper


def make(n_row, n_col):
    def on_device(matrix, panels, exponents, inverses, pivots):
        row_dev = matrix.shape[0]
        steps, width = pivots.shape
        tile = row_dev // exponents.shape[1]
        part = width // n_col
        row = lax.axis_index("prow")
        me = lax.axis_index("pcol")
        first_row = row * row_dev
        local = jnp.arange(row_dev, dtype=jnp.int32)
        global_rows = first_row + local
        order = jnp.arange(n_col, dtype=jnp.int32) ^ me

        factor = jnp.repeat(jnp.exp2(exponents.astype(F32)), tile, axis=1).astype(BF)
        blocks = [None] * steps
        for chunk in CHUNKS:
            got = gather_panels(panels[chunk[0] : chunk[-1] + 1], n_col)
            for at, step in enumerate(chunk):
                blocks[step] = jnp.concatenate([g[at] for g in got]) * factor[step][None, :]
        current = matrix
        for step in range(steps):
            top = step * width
            root = top // row_dev
            assert root == 0
            local_piv = pivots[step] - first_row
            pick = (local_piv[:, None] == local[None, :]).astype(BF)
            here = (pivots[step] // (2 * row_dev)) == row // 2
            picked = jnp.dot(pick, current, preferred_element_type=F32).astype(BF)
            top_block = current[top : top + width]
            mine = jnp.where(row == 0, top_block, picked)
            chosen, upper = trade_rows(mine, here, row, n_row)
            solved = jnp.dot(inverses[step], chosen, preferred_element_type=F32).astype(BF)
            mixed = solved.reshape(n_col, part, -1)[order].reshape(width, -1)
            put = (global_rows[:, None] == pivots[step][None, :]).astype(BF)
            is_pivot = jnp.any(put > 0, axis=1)
            placed = jnp.dot(put, upper, preferred_element_type=F32)
            swapped = jnp.where(is_pivot[:, None], placed, current.astype(F32))
            change = lax.dot_general(blocks[step], mixed, (((0,), (0,)), ((), ())), preferred_element_type=F32)
            refreshed = (swapped - change).astype(BF)
            keep = global_rows >= top + width
            refreshed = jnp.where(keep[:, None], refreshed, current)
            in_top = row == 0
            top_rows = jnp.where(in_top, solved, refreshed[top : top + width])
            current = lax.dynamic_update_slice(refreshed, top_rows, (top, 0))
        return current

    return on_device


def solution(mesh):
    return jax.shard_map(
        make(mesh.shape["prow"], mesh.shape["pcol"]),
        mesh=mesh,
        in_specs=(P("prow", "pcol"), P(None, "pcol", "prow"), P(None, "prow"), P(), P()),
        out_specs=P("prow", "pcol"),
        check_vma=False,
    )
```

time: 228 us -> 115 us (0.50)
  blocking collectives: 135 us -> 0 us
  starting transfers between devices: 0.13 us -> 36.1 us
  waiting for transfers between devices: 1.24 us -> 29.8 us
  local copies, waits for them, and re-layouts: 47.4 us -> 19.6 us
  between operations: 13.6 us -> 0.62 us
  other arithmetic: 15 us -> 9.72 us
  matrix products: 14.5 us -> 18 us
    all_gather x4 -> x0, blocking collectives: 135 us -> none  [on_device(): lax.all_gather(panels[step], 'pcol', axis=0, tiled=True) * factor[None, :]]
    gather x12 -> x4, local copies, waits for them, and re-layouts: 42 us -> 2.87 us  [on_device(): mixed = solved.reshape(n_col, part, -1)[order].reshape(width, -1)]
    ppermute x0 -> x33, starting transfers between devices: none -> 36.1 us  [swap(): return lax.ppermute(value, axis, xor_pairs(size, mask))]
    ppermute x0 -> x33, waiting for transfers between devices: none -> 29.8 us  [swap(): return lax.ppermute(value, axis, xor_pairs(size, mask))]
    unnamed x44 -> x57, local copies, waits for them, and re-layouts: 0.79 us -> 8.79 us
    select_n x16 -> x13, other arithmetic: 6.46 us -> 0.63 us  [the longest x4 0.47 us: trade_rows(): message = jnp.where(low_chip & ~here[:, None], upper, picked)]
    dot_general x8 -> x16, matrix products: 14.5 us -> 18 us  [the longest x4 7.06 us: on_device(): lax.dot_general(blocks[step], mixed, (((0,), (0,)), ((), ())), preferred_...]
    convert_element_type x8 -> x0, local copies, waits for them, and re-layouts: 3.18 us -> none  [the longest x4 2.62 us: on_device(): jnp.repeat(jnp.exp2(exponents[step].astype(jnp.float32)), tile)]
  transfers between devices with their start and end apart: 4 -> 33, of which waited for: 3 -> 15; matrix products, arithmetic and copies ran while one was open for 5% -> 31% of each run, Pallas kernels for 0% -> 0%
where the time goes in v1:
time: 115 us; the launch traced here: 114 us
  starting transfers between devices  36.1 us (31%)
  waiting for transfers between devices  29.8 us (26%)
  local copies, waits for them, and re-layouts  19.6 us (17%)
  matrix products  18 us (16%)
  other arithmetic  9.72 us (8%)
    ppermute x33, starting transfers between devices, swap(): return lax.ppermute(value, axis, xor_pairs(size, mask))  36.1 us
    ppermute x33, waiting for transfers between devices, swap(): return lax.ppermute(value, axis, xor_pairs(size, mask))  29.8 us
    unnamed x57, local copies, waits for them, and re-layouts  8.79 us
    dot_general x4, matrix products, on_device(): lax.dot_general(blocks[step], mixed, (((0,), (0,)), ((), ())), preferred_...  7.06 us
    dot_general x4, matrix products, on_device(): jnp.dot(inverses[step], chosen, preferred_element_type=F32).astype(BF)  4.98 us
    dot_general x4, matrix products, on_device(): picked = jnp.dot(pick, current, preferred_element_type=F32).astype(BF)  3.19 us
    gather x4, local copies, waits for them, and re-layouts, on_device(): mixed = solved.reshape(n_col, part, -1)[order].reshape(width, -1)  2.87 us
    dot_general x4, matrix products, on_device(): placed = jnp.dot(put, upper, preferred_element_type=F32)  2.73 us
  transfers between devices with their start and end apart: 33, of which 15 were waited for; matrix products, arithmetic and copies ran while one was open for 31% of the time, Pallas kernels for 0%

profile of v1, /device:TPU:0, one launch (start us, length us, event | category | flops | bytes accessed | tf_op | source)
XLA Modules:
  0.0 113.9 jit_solution(1252592934586120694)
XLA Ops:
  0.0 1.6 %slice.191 = bf16[2,32,1024]{2,1,0:T(8,128)(2,1)} slice(bf16[4,32,1024]{2,1,0:T(8,128)(2,1)} %param.6), slice={[2:4], [0:32], [0:1024]} | slice | bytes 262144 | tf_op jit(solution)/shard_map/slice | solution.py:74
  1.6 2.9 %collective-permute-start.23 = (bf16[2,32,1024]{2,1,0:T(8,128)(2,1)}, bf16[2,32,1024]{2,1,0:T(8,128)(2,1)S(1)}, u32[]{:S(2)}, u32[]{:S(2)}) collective-permute-start(bf16[2,32,1024]{2,1,0:T(8,128)(2,1)} %slice.191), channel_id=1, source_target_pairs={{0,1},{1,0},{2,3},{3,2},{4,5},{5,4},{6,7},{7,6},{8,9},{9,8},{10,11... | collective-permute-start | bytes 393224 | tf_op jit(solution)/shard_map/ppermute | solution.py:16
  4.5 1.6 %collective-permute-start.24 = (bf16[2,32,1024]{2,1,0:T(8,128)(2,1)}, bf16[2,32,1024]{2,1,0:T(8,128)(2,1)}, u32[]{:S(2)}, u32[]{:S(2)}) collective-permute-start(bf16[2,32,1024]{2,1,0:T(8,128)(2,1)} %slice.191), channel_id=1, source_target_pairs={{0,2},{1,3},{2,0},{3,1},{4,6},{5,7},{6,4},{7,5},{8,10},{9,11},{10,... | collective-permute-start | bytes 393224 | tf_op jit(solution)/shard_map/ppermute | solution.py:16
  6.1 2.6 %collective-permute-start.26 = (bf16[2,32,1024]{2,1,0:T(8,128)(2,1)}, bf16[2,32,1024]{2,1,0:T(8,128)(2,1)S(1)}, u32[]{:S(2)}, u32[]{:S(2)}) collective-permute-start(bf16[2,32,1024]{2,1,0:T(8,128)(2,1)} %slice.191), channel_id=1, source_target_pairs={{0,4},{1,5},{2,6},{3,7},{4,0},{5,1},{6,2},{7,3},{8,12},{9,13},{10,... | collective-permute-start | bytes 393224 | tf_op jit(solution)/shard_map/ppermute | solution.py:16
  10.6 1.6 %constant_dynamic-update-slice_fusion.17 = (bf16[256,1024]{1,0:T(8,128)(2,1)}, bf16[256,1024]{1,0:T(8,128)(2,1)S(1)}, bf16[256,1024]{1,0:T(8,128)(2,1)S(1)}, bf16[256,1024]{1,0:T(8,128)(2,1)}) fusion(bf16[4,32,1024]{2,1,0:T(8,128)(2,1)} %param.6), kind=kLoop, calls=%fused_computation.169 | loop fusion | bytes 524288
  22.1 1.7 %fusion.12 = bf16[256,512]{1,0:T(8,128)(2,1)S(1)} fusion(bf16[1024,512]{1,0:T(8,128)(2,1)} %param.5, s32[256]{0:T(256)S(1)} %broadcast_subtract_fusion.3, pred[]{:T(512)S(6)} %eq.193), kind=kOutput, calls=%fused_computation.32 | convolution fusion | flops 268959744 | bytes 1573889 | tf_op jit(solution)/shard_map/dot_general | solution.py:85
  24.5 1.9 %collective-permute-start.13 = (bf16[1,32,1024]{2,1,0:T(8,128)(2,1)S(1)}, bf16[1,32,1024]{2,1,0:T(8,128)(2,1)S(1)}, u32[]{:S(2)}, u32[]{:S(2)}) collective-permute-start(bf16[1,32,1024]{2,1,0:T(8,128)(2,1)S(1)} %get-tuple-element.25), channel_id=1, source_target_pairs={{0,1},{1,0},{2,3},{3,2},{4,5},{5,4},{6,7},{7,6},{8,9},{9,8},{10,11... | collective-permute-start | bytes 196616 | tf_op jit(solution)/shard_map/ppermute | solution.py:16
  26.4 2.4 %collective-permute-done.13 = bf16[1,32,1024]{2,1,0:T(8,128)(2,1)S(1)} collective-permute-done((bf16[1,32,1024]{2,1,0:T(8,128)(2,1)S(1)}, bf16[1,32,1024]{2,1,0:T(8,128)(2,1)S(1)}, u32[]{:S(2)}, u32[]{:S(2)}) %collective-permute-start.13) | collective-permute-done | bytes 65568 | tf_op jit(solution)/shard_map/ppermute | solution.py:16
  28.8 1.9 %collective-permute-start.14 = (bf16[1,32,1024]{2,1,0:T(8,128)(2,1)S(1)}, bf16[1,32,1024]{2,1,0:T(8,128)(2,1)S(1)}, u32[]{:S(2)}, u32[]{:S(2)}) collective-permute-start(bf16[1,32,1024]{2,1,0:T(8,128)(2,1)S(1)} %get-tuple-element.25), channel_id=1, source_target_pairs={{0,2},{1,3},{2,0},{3,1},{4,6},{5,7},{6,4},{7,5},{8,10},{9,11},{10,... | collective-permute-start | bytes 196616 | tf_op jit(solution)/shard_map/ppermute | solution.py:16
  30.7 2.9 %collective-permute-done.14 = bf16[1,32,1024]{2,1,0:T(8,128)(2,1)S(1)} collective-permute-done((bf16[1,32,1024]{2,1,0:T(8,128)(2,1)S(1)}, bf16[1,32,1024]{2,1,0:T(8,128)(2,1)S(1)}, u32[]{:S(2)}, u32[]{:S(2)}) %collective-permute-start.14) | collective-permute-done | bytes 65568 | tf_op jit(solution)/shard_map/ppermute | solution.py:16
  33.7 1.5 %collective-permute-start.5 = (bf16[1,32,1024]{2,1,0:T(8,128)(2,1)S(1)}, bf16[1,32,1024]{2,1,0:T(8,128)(2,1)S(1)}, u32[]{:S(2)}, u32[]{:S(2)}) collective-permute-start(bf16[1,32,1024]{2,1,0:T(8,128)(2,1)S(1)} %collective-permute-done.3), channel_id=1, source_target_pairs={{0,2},{1,3},{2,0},{3,1},{4,6},{5,7},{6,4},{7,5},{8,10},{9,11},{10,... | collective-permute-start | bytes 196616 | tf_op jit(solution)/shard_map/ppermute | solution.py:16
  35.2 2.5 %collective-permute-start.8 = (bf16[1,32,1024]{2,1,0:T(8,128)(2,1)S(1)}, bf16[1,32,1024]{2,1,0:T(8,128)(2,1)S(1)}, u32[]{:S(2)}, u32[]{:S(2)}) collective-permute-start(bf16[1,32,1024]{2,1,0:T(8,128)(2,1)S(1)} %get-tuple-element.26), channel_id=1, source_target_pairs={{0,6},{1,7},{2,4},{3,5},{4,2},{5,3},{6,0},{7,1},{8,14},{9,15},{10,... | collective-permute-start | bytes 196616 | tf_op jit(solution)/shard_map/ppermute | solution.py:16
  37.9 1.8 %collective-permute-start.7 = (bf16[1,32,1024]{2,1,0:T(8,128)(2,1)S(1)}, bf16[1,32,1024]{2,1,0:T(8,128)(2,1)S(1)}, u32[]{:S(2)}, u32[]{:S(2)}) collective-permute-start(bf16[1,32,1024]{2,1,0:T(8,128)(2,1)S(1)} %collective-permute-done.6), channel_id=1, source_target_pairs={{0,1},{1,0},{2,3},{3,2},{4,5},{5,4},{6,7},{7,6},{8,9},{9,8},{10,11... | collective-permute-start | bytes 196616 | tf_op jit(solution)/shard_map/ppermute | solution.py:16
  39.8 2.4 %collective-permute-done.7 = bf16[1,32,1024]{2,1,0:T(8,128)(2,1)S(1)} collective-permute-done((bf16[1,32,1024]{2,1,0:T(8,128)(2,1)S(1)}, bf16[1,32,1024]{2,1,0:T(8,128)(2,1)S(1)}, u32[]{:S(2)}, u32[]{:S(2)}) %collective-permute-start.7) | collective-permute-done | bytes 65568 | tf_op jit(solution)/shard_map/ppermute | solution.py:16
  42.2 2.5 %collective-permute-start.16 = (bf16[1,32,1024]{2,1,0:T(8,128)(2,1)S(1)}, bf16[1,32,1024]{2,1,0:T(8,128)(2,1)S(1)}, u32[]{:S(2)}, u32[]{:S(2)}) collective-permute-start(bf16[1,32,1024]{2,1,0:T(8,128)(2,1)S(1)} %get-tuple-element.25), channel_id=1, source_target_pairs={{0,4},{1,5},{2,6},{3,7},{4,0},{5,1},{6,2},{7,3},{8,12},{9,13},{10,... | collective-permute-start | bytes 196616 | tf_op jit(solution)/shard_map/ppermute | solution.py:16
  44.7 1.5 %collective-permute-start.15 = (bf16[1,32,1024]{2,1,0:T(8,128)(2,1)S(1)}, bf16[1,32,1024]{2,1,0:T(8,128)(2,1)S(1)}, u32[]{:S(2)}, u32[]{:S(2)}) collective-permute-start(bf16[1,32,1024]{2,1,0:T(8,128)(2,1)S(1)} %collective-permute-done.13), channel_id=1, source_target_pairs={{0,2},{1,3},{2,0},{3,1},{4,6},{5,7},{6,4},{7,5},{8,10},{9,11},{10,... | collective-permute-start | bytes 196616 | tf_op jit(solution)/shard_map/ppermute | solution.py:16
  46.2 3.2 %collective-permute-done.15 = bf16[1,32,1024]{2,1,0:T(8,128)(2,1)S(1)} collective-permute-done((bf16[1,32,1024]{2,1,0:T(8,128)(2,1)S(1)}, bf16[1,32,1024]{2,1,0:T(8,128)(2,1)S(1)}, u32[]{:S(2)}, u32[]{:S(2)}) %collective-permute-start.15) | collective-permute-done | bytes 65568 | tf_op jit(solution)/shard_map/ppermute | solution.py:16
  50.7 1.5 %collective-permute-start.9 = (bf16[1,32,1024]{2,1,0:T(8,128)(2,1)S(1)}, bf16[1,32,1024]{2,1,0:T(8,128)(2,1)S(1)}, u32[]{:S(2)}, u32[]{:S(2)}) collective-permute-start(bf16[1,32,1024]{2,1,0:T(8,128)(2,1)S(1)} %collective-permute-done.8), channel_id=1, source_target_pairs={{0,1},{1,0},{2,3},{3,2},{4,5},{5,4},{6,7},{7,6},{8,9},{9,8},{10,11... | collective-permute-start | bytes 196616 | tf_op jit(solution)/shard_map/ppermute | solution.py:16
  55.2 1.5 %collective-permute-start.1 = (bf16[128,512]{1,0:T(8,128)(2,1)S(1)}, bf16[128,512]{1,0:T(8,128)(2,1)S(1)}, u32[]{:S(2)}, u32[]{:S(2)}) collective-permute-start(bf16[128,512]{1,0:T(8,128)(2,1)S(1)} %slice_select_fusion.7), channel_id=1, source_target_pairs={{0,16},{8,24},{16,0},{24,8},{1,17},{9,25},{17,1},{25,9},{2,18},{10... | collective-permute-start | bytes 393224 | tf_op jit(solution)/shard_map/ppermute | solution.py:16
  56.8 2.7 %collective-permute-start.28 = (bf16[2,32,1024]{2,1,0:T(8,128)(2,1)}, bf16[2,32,1024]{2,1,0:T(8,128)(2,1)}, u32[]{:S(2)}, u32[]{:S(2)}) collective-permute-start(bf16[2,32,1024]{2,1,0:T(8,128)(2,1)} %slice.191), channel_id=1, source_target_pairs={{0,6},{1,7},{2,4},{3,5},{4,2},{5,3},{6,0},{7,1},{8,14},{9,15},{10,... | collective-permute-start | bytes 393224 | tf_op jit(solution)/shard_map/ppermute | solution.py:16
  59.5 1.9 %collective-permute-start.19 = (bf16[1,32,1024]{2,1,0:T(8,128)(2,1)}, bf16[1,32,1024]{2,1,0:T(8,128)(2,1)}, u32[]{:S(2)}, u32[]{:S(2)}) collective-permute-start(bf16[1,32,1024]{2,1,0:T(8,128)(2,1)} %collective-permute-done.18), channel_id=1, source_target_pairs={{0,1},{1,0},{2,3},{3,2},{4,5},{5,4},{6,7},{7,6},{8,9},{9,8},{10,11... | collective-permute-start | bytes 196616 | tf_op jit(solution)/shard_map/ppermute | solution.py:16
  66.1 1.7 %fusion = bf16[1024,512]{1,0:T(8,128)(2,1)S(1)} fusion(bf16[1024,512]{1,0:T(8,128)(2,1)S(1)} %copy-done, bf16[256,512]{1,0:T(8,128)(2,1)S(1)} %bitcast.157, f32[1024,512]{1,0:T(8,128)S(1)} %fusion.4, pred[1024]{0:T(1024)(128)(4,1)} %get-tuple-element.8, pred[1024]{0:T(1024)(128)(4,1)} %fusion.78, bf16[256,1024]{1,0:T(8,128)(2,1)} %copy-done.3, ...), kind=kOutput, calls=%fused_computation.8 | convolution fusion | flops 271319040 | bytes 4984832 | tf_op jit(solution)/shard_map/dot_general | solution.py:95
  68.7 1.5 %constant_dynamic-update-slice_fusion.9 = bf16[256,1024]{1,0:T(8,128)(2,1)} fusion(bf16[256,1024]{1,0:T(8,128)(2,1)} %copy-done.2, bf16[1,32,1024]{2,1,0:T(8,128)(2,1)} %collective-permute-done.18), kind=kLoop, calls=%fused_computation.161 | loop fusion | bytes 131072
  72.3 1.5 %fusion.69 = (bf16[256,1024]{1,0:T(8,128)(2,1)S(1)}, bf16[256,1024]{1,0:T(8,128)(2,1)}) fusion(bf16[256,1024]{1,0:T(8,128)(2,1)S(1)} %copy-done.1, bf16[2,32,1024]{2,1,0:T(8,128)(2,1)} %collective-permute-done.24, bf16[256,1024]{1,0:T(8,128)(2,1)} %get-tuple-element.44), kind=kLoop, calls=%fused_computation.135 | loop fusion | bytes 262144
  76.1 3.1 %collective-permute-done.11 = bf16[128,512]{1,0:T(8,128)(2,1)S(1)} collective-permute-done((bf16[128,512]{1,0:T(8,128)(2,1)S(1)}, bf16[128,512]{1,0:T(8,128)(2,1)S(1)}, u32[]{:S(2)}, u32[]{:S(2)}) %collective-permute-start.11) | collective-permute-done | bytes 131104 | tf_op jit(solution)/shard_map/ppermute | solution.py:16
  83.0 1.7 %fusion.1 = bf16[1024,512]{1,0:T(8,128)(2,1)S(1)} fusion(bf16[1024,512]{1,0:T(8,128)(2,1)S(1)} %fusion.35, bf16[256,512]{1,0:T(8,128)(2,1)S(1)} %bitcast.155, f32[1024,512]{1,0:T(8,128)S(1)} %fusion.6, pred[1024]{0:T(1024)(128)(4,1)} %get-tuple-element.7, pred[1024]{0:T(1024)(128)(4,1)} %fusion.79, ...), kind=kOutput, calls=%fused_computation.9 | convolution fusion | flops 271319040 | bytes 4984832 | tf_op jit(solution)/shard_map/dot_general | solution.py:95
  87.8 1.5 %fusion.65 = (bf16[256,1024]{1,0:T(8,128)(2,1)S(1)}, bf16[256,1024]{1,0:T(8,128)(2,1)}) fusion(bf16[256,1024]{1,0:T(8,128)(2,1)S(1)} %get-tuple-element.35, bf16[2,32,1024]{2,1,0:T(8,128)(2,1)} %collective-permute-done.28, bf16[256,1024]{1,0:T(8,128)(2,1)} %get-tuple-element.36), kind=kLoop, calls=%fused_computation.127 | loop fusion | bytes 262144
  89.3 3.6 %collective-permute-done.21 = bf16[128,512]{1,0:T(8,128)(2,1)S(1)} collective-permute-done((bf16[128,512]{1,0:T(8,128)(2,1)S(1)}, bf16[128,512]{1,0:T(8,128)(2,1)S(1)}, u32[]{:S(2)}, u32[]{:S(2)}) %collective-permute-start.21) | collective-permute-done | bytes 131104 | tf_op jit(solution)/shard_map/ppermute | solution.py:16
  96.8 1.7 %fusion.2 = bf16[1024,512]{1,0:T(8,128)(2,1)S(1)} fusion(bf16[1024,512]{1,0:T(8,128)(2,1)S(1)} %fusion.34, bf16[256,512]{1,0:T(8,128)(2,1)S(1)} %bitcast.156, f32[1024,512]{1,0:T(8,128)S(1)} %fusion.8, pred[1024]{0:T(1024)(128)(4,1)S(1)} %copy-done.15, pred[1024]{0:T(1024)(128)(4,1)S(1)} %copy-done.16, bf16[256,1024]{1,0:T(8,128)(2,1)} %get-tuple-element.32, ...), kind=kOutput, calls=%fused_computation.10 | convolution fusion | flops 271319040 | bytes 4984832 | tf_op jit(solution)/shard_map/dot_general | solution.py:95
  101.5 4.9 %collective-permute-done.31 = bf16[128,512]{1,0:T(8,128)(2,1)S(1)} collective-permute-done((bf16[128,512]{1,0:T(8,128)(2,1)S(1)}, bf16[128,512]{1,0:T(8,128)(2,1)S(1)}, u32[]{:S(2)}, u32[]{:S(2)}) %collective-permute-start.31) | collective-permute-done | bytes 131104 | tf_op jit(solution)/shard_map/ppermute | solution.py:16
  110.3 1.9 %fusion.3 = bf16[1024,512]{1,0:T(8,128)(2,1)} fusion(bf16[1024,512]{1,0:T(8,128)(2,1)S(1)} %fusion.33, bf16[256,512]{1,0:T(8,128)(2,1)S(1)} %bitcast.154, f32[1024,512]{1,0:T(8,128)S(1)} %fusion.10, pred[1024]{0:T(1024)(128)(4,1)S(1)} %copy-done.14, pred[1024]{0:T(1024)(128)(4,1)S(1)} %fusion.81, bf16[256,1024]{1,0:T(8,128)(2,1)S(1)} %get-tuple-element.31, ...), kind=kOutput, calls=%fused_computation.11 | convolution fusion | flops 271319040 | bytes 4984832 | tf_op jit(solution)/shard_map/dot_general | solution.py:95
  112.2 1.7 %fusion.32 = bf16[1024,512]{1,0:T(8,128)(2,1)} fusion(bf16[1024,512]{1,0:T(8,128)(2,1)} %fusion.3, bf16[512,256]{0,1:T(8,128)(2,1)S(1)} %convolution_convert_fusion, pred[]{:T(512)S(6)} %eq.193), kind=kLoop, calls=%fused_computation.61 | loop fusion | flops 131072 | bytes 786433 | tf_op jit(solution)/shard_map/dynamic_update_slice | solution.py:101
  (155 shorter events, 44.1 us)
Async XLA Ops:
  1.6 49.1 %collective-permute-start.23 = (bf16[2,32,1024]{2,1,0:T(8,128)(2,1)}, bf16[2,32,1024]{2,1,0:T(8,128)(2,1)S(1)}, u32[]{:S(2)}, u32[]{:S(2)}) collective-permute-start(bf16[2,32,1024]{2,1,0:T(8,128)(2,1)} %slice.191), channel_id=1, source_target_pairs={{0,1},{1,0},{2,3},{3,2},{4,5},{5,4},{6,7},{7,6},{8,9},{9,8},{10,11... | collective-permute-start | bytes 393224 | tf_op jit(solution)/shard_map/ppermute | solution.py:16
  4.5 65.6 %collective-permute-start.24 = (bf16[2,32,1024]{2,1,0:T(8,128)(2,1)}, bf16[2,32,1024]{2,1,0:T(8,128)(2,1)}, u32[]{:S(2)}, u32[]{:S(2)}) collective-permute-start(bf16[2,32,1024]{2,1,0:T(8,128)(2,1)} %slice.191), channel_id=1, source_target_pairs={{0,2},{1,3},{2,0},{3,1},{4,6},{5,7},{6,4},{7,5},{8,10},{9,11},{10,... | collective-permute-start | bytes 393224 | tf_op jit(solution)/shard_map/ppermute | solution.py:16
  6.1 64.1 %collective-permute-start.26 = (bf16[2,32,1024]{2,1,0:T(8,128)(2,1)}, bf16[2,32,1024]{2,1,0:T(8,128)(2,1)S(1)}, u32[]{:S(2)}, u32[]{:S(2)}) collective-permute-start(bf16[2,32,1024]{2,1,0:T(8,128)(2,1)} %slice.191), channel_id=1, source_target_pairs={{0,4},{1,5},{2,6},{3,7},{4,0},{5,1},{6,2},{7,3},{8,12},{9,13},{10,... | collective-permute-start | bytes 393224 | tf_op jit(solution)/shard_map/ppermute | solution.py:16
  9.6 14.9 %collective-permute-start.3 = (bf16[1,32,1024]{2,1,0:T(8,128)(2,1)S(1)}, bf16[1,32,1024]{2,1,0:T(8,128)(2,1)S(1)}, u32[]{:S(2)}, u32[]{:S(2)}) collective-permute-start(bf16[1,32,1024]{2,1,0:T(8,128)(2,1)S(1)} %get-tuple-element.26), channel_id=1, source_target_pairs={{0,1},{1,0},{2,3},{3,2},{4,5},{5,4},{6,7},{7,6},{8,9},{9,8},{10,11... | collective-permute-start | bytes 196616 | tf_op jit(solution)/shard_map/ppermute | solution.py:16
  10.2 14.3 %collective-permute-start.4 = (bf16[1,32,1024]{2,1,0:T(8,128)(2,1)S(1)}, bf16[1,32,1024]{2,1,0:T(8,128)(2,1)S(1)}, u32[]{:S(2)}, u32[]{:S(2)}) collective-permute-start(bf16[1,32,1024]{2,1,0:T(8,128)(2,1)S(1)} %get-tuple-element.26), channel_id=1, source_target_pairs={{0,2},{1,3},{2,0},{3,1},{4,6},{5,7},{6,4},{7,5},{8,10},{9,11},{10,... | collective-permute-start | bytes 196616 | tf_op jit(solution)/shard_map/ppermute | solution.py:16
  24.5 10.7 %collective-permute-start.6 = (bf16[1,32,1024]{2,1,0:T(8,128)(2,1)S(1)}, bf16[1,32,1024]{2,1,0:T(8,128)(2,1)S(1)}, u32[]{:S(2)}, u32[]{:S(2)}) collective-permute-start(bf16[1,32,1024]{2,1,0:T(8,128)(2,1)S(1)} %get-tuple-element.26), channel_id=1, source_target_pairs={{0,4},{1,5},{2,6},{3,7},{4,0},{5,1},{6,2},{7,3},{8,12},{9,13},{10,... | collective-permute-start | bytes 196616 | tf_op jit(solution)/shard_map/ppermute | solution.py:16
  24.5 4.3 %collective-permute-start.13 = (bf16[1,32,1024]{2,1,0:T(8,128)(2,1)S(1)}, bf16[1,32,1024]{2,1,0:T(8,128)(2,1)S(1)}, u32[]{:S(2)}, u32[]{:S(2)}) collective-permute-start(bf16[1,32,1024]{2,1,0:T(8,128)(2,1)S(1)} %get-tuple-element.25), channel_id=1, source_target_pairs={{0,1},{1,0},{2,3},{3,2},{4,5},{5,4},{6,7},{7,6},{8,9},{9,8},{10,11... | collective-permute-start | bytes 196616 | tf_op jit(solution)/shard_map/ppermute | solution.py:16
  28.8 4.8 %collective-permute-start.14 = (bf16[1,32,1024]{2,1,0:T(8,128)(2,1)S(1)}, bf16[1,32,1024]{2,1,0:T(8,128)(2,1)S(1)}, u32[]{:S(2)}, u32[]{:S(2)}) collective-permute-start(bf16[1,32,1024]{2,1,0:T(8,128)(2,1)S(1)} %get-tuple-element.25), channel_id=1, source_target_pairs={{0,2},{1,3},{2,0},{3,1},{4,6},{5,7},{6,4},{7,5},{8,10},{9,11},{10,... | collective-permute-start | bytes 196616 | tf_op jit(solution)/shard_map/ppermute | solution.py:16
  33.7 4.3 %collective-permute-start.5 = (bf16[1,32,1024]{2,1,0:T(8,128)(2,1)S(1)}, bf16[1,32,1024]{2,1,0:T(8,128)(2,1)S(1)}, u32[]{:S(2)}, u32[]{:S(2)}) collective-permute-start(bf16[1,32,1024]{2,1,0:T(8,128)(2,1)S(1)} %collective-permute-done.3), channel_id=1, source_target_pairs={{0,2},{1,3},{2,0},{3,1},{4,6},{5,7},{6,4},{7,5},{8,10},{9,11},{10,... | collective-permute-start | bytes 196616 | tf_op jit(solution)/shard_map/ppermute | solution.py:16
  35.2 9.5 %collective-permute-start.8 = (bf16[1,32,1024]{2,1,0:T(8,128)(2,1)S(1)}, bf16[1,32,1024]{2,1,0:T(8,128)(2,1)S(1)}, u32[]{:S(2)}, u32[]{:S(2)}) collective-permute-start(bf16[1,32,1024]{2,1,0:T(8,128)(2,1)S(1)} %get-tuple-element.26), channel_id=1, source_target_pairs={{0,6},{1,7},{2,4},{3,5},{4,2},{5,3},{6,0},{7,1},{8,14},{9,15},{10,... | collective-permute-start | bytes 196616 | tf_op jit(solution)/shard_map/ppermute | solution.py:16
  37.9 4.3 %collective-permute-start.7 = (bf16[1,32,1024]{2,1,0:T(8,128)(2,1)S(1)}, bf16[1,32,1024]{2,1,0:T(8,128)(2,1)S(1)}, u32[]{:S(2)}, u32[]{:S(2)}) collective-permute-start(bf16[1,32,1024]{2,1,0:T(8,128)(2,1)S(1)} %collective-permute-done.6), channel_id=1, source_target_pairs={{0,1},{1,0},{2,3},{3,2},{4,5},{5,4},{6,7},{7,6},{8,9},{9,8},{10,11... | collective-permute-start | bytes 196616 | tf_op jit(solution)/shard_map/ppermute | solution.py:16
  42.2 8.4 %collective-permute-start.16 = (bf16[1,32,1024]{2,1,0:T(8,128)(2,1)S(1)}, bf16[1,32,1024]{2,1,0:T(8,128)(2,1)S(1)}, u32[]{:S(2)}, u32[]{:S(2)}) collective-permute-start(bf16[1,32,1024]{2,1,0:T(8,128)(2,1)S(1)} %get-tuple-element.25), channel_id=1, source_target_pairs={{0,4},{1,5},{2,6},{3,7},{4,0},{5,1},{6,2},{7,3},{8,12},{9,13},{10,... | collective-permute-start | bytes 196616 | tf_op jit(solution)/shard_map/ppermute | solution.py:16
  44.7 4.7 %collective-permute-start.15 = (bf16[1,32,1024]{2,1,0:T(8,128)(2,1)S(1)}, bf16[1,32,1024]{2,1,0:T(8,128)(2,1)S(1)}, u32[]{:S(2)}, u32[]{:S(2)}) collective-permute-start(bf16[1,32,1024]{2,1,0:T(8,128)(2,1)S(1)} %collective-permute-done.13), channel_id=1, source_target_pairs={{0,2},{1,3},{2,0},{3,1},{4,6},{5,7},{6,4},{7,5},{8,10},{9,11},{10,... | collective-permute-start | bytes 196616 | tf_op jit(solution)/shard_map/ppermute | solution.py:16
  49.4 7.3 %collective-permute-start.18 = (bf16[1,32,1024]{2,1,0:T(8,128)(2,1)S(1)}, bf16[1,32,1024]{2,1,0:T(8,128)(2,1)}, u32[]{:S(2)}, u32[]{:S(2)}) collective-permute-start(bf16[1,32,1024]{2,1,0:T(8,128)(2,1)S(1)} %get-tuple-element.25), channel_id=1, source_target_pairs={{0,6},{1,7},{2,4},{3,5},{4,2},{5,3},{6,0},{7,1},{8,14},{9,15},{10,... | collective-permute-start | bytes 196616 | tf_op jit(solution)/shard_map/ppermute | solution.py:16
  50.6 2.3 %collective-permute-start = (bf16[256,512]{1,0:T(8,128)(2,1)S(1)}, bf16[256,512]{1,0:T(8,128)(2,1)S(1)}, u32[]{:S(2)}, u32[]{:S(2)}) collective-permute-start(bf16[256,512]{1,0:T(8,128)(2,1)S(1)} %fusion.12), channel_id=1, source_target_pairs={{0,8},{8,0},{16,24},{24,16},{1,9},{9,1},{17,25},{25,17},{2,10},{10... | collective-permute-start | bytes 786440 | tf_op jit(solution)/shard_map/ppermute | solution.py:16
  50.7 4.5 %collective-permute-start.9 = (bf16[1,32,1024]{2,1,0:T(8,128)(2,1)S(1)}, bf16[1,32,1024]{2,1,0:T(8,128)(2,1)S(1)}, u32[]{:S(2)}, u32[]{:S(2)}) collective-permute-start(bf16[1,32,1024]{2,1,0:T(8,128)(2,1)S(1)} %collective-permute-done.8), channel_id=1, source_target_pairs={{0,1},{1,0},{2,3},{3,2},{4,5},{5,4},{6,7},{7,6},{8,9},{9,8},{10,11... | collective-permute-start | bytes 196616 | tf_op jit(solution)/shard_map/ppermute | solution.py:16
  52.9 6.6 %collective-permute-start.17 = (bf16[1,32,1024]{2,1,0:T(8,128)(2,1)S(1)}, bf16[1,32,1024]{2,1,0:T(8,128)(2,1)S(1)}, u32[]{:S(2)}, u32[]{:S(2)}) collective-permute-start(bf16[1,32,1024]{2,1,0:T(8,128)(2,1)S(1)} %collective-permute-done.16), channel_id=1, source_target_pairs={{0,1},{1,0},{2,3},{3,2},{4,5},{5,4},{6,7},{7,6},{8,9},{9,8},{10,11... | collective-permute-start | bytes 196616 | tf_op jit(solution)/shard_map/ppermute | solution.py:16
  55.2 6.1 %collective-permute-start.1 = (bf16[128,512]{1,0:T(8,128)(2,1)S(1)}, bf16[128,512]{1,0:T(8,128)(2,1)S(1)}, u32[]{:S(2)}, u32[]{:S(2)}) collective-permute-start(bf16[128,512]{1,0:T(8,128)(2,1)S(1)} %slice_select_fusion.7), channel_id=1, source_target_pairs={{0,16},{8,24},{16,0},{24,8},{1,17},{9,25},{17,1},{25,9},{2,18},{10... | collective-permute-start | bytes 393224 | tf_op jit(solution)/shard_map/ppermute | solution.py:16
  56.8 14.2 %collective-permute-start.28 = (bf16[2,32,1024]{2,1,0:T(8,128)(2,1)}, bf16[2,32,1024]{2,1,0:T(8,128)(2,1)}, u32[]{:S(2)}, u32[]{:S(2)}) collective-permute-start(bf16[2,32,1024]{2,1,0:T(8,128)(2,1)} %slice.191), channel_id=1, source_target_pairs={{0,6},{1,7},{2,4},{3,5},{4,2},{5,3},{6,0},{7,1},{8,14},{9,15},{10,... | collective-permute-start | bytes 393224 | tf_op jit(solution)/shard_map/ppermute | solution.py:16
  59.5 15.1 %collective-permute-start.19 = (bf16[1,32,1024]{2,1,0:T(8,128)(2,1)}, bf16[1,32,1024]{2,1,0:T(8,128)(2,1)}, u32[]{:S(2)}, u32[]{:S(2)}) collective-permute-start(bf16[1,32,1024]{2,1,0:T(8,128)(2,1)} %collective-permute-done.18), channel_id=1, source_target_pairs={{0,1},{1,0},{2,3},{3,2},{4,5},{5,4},{6,7},{7,6},{8,9},{9,8},{10,11... | collective-permute-start | bytes 196616 | tf_op jit(solution)/shard_map/ppermute | solution.py:16
  61.4 1.3 %collective-permute-start.2 = (bf16[128,512]{1,0:T(8,128)(2,1)S(1)}, bf16[128,512]{1,0:T(8,128)(2,1)S(1)}, u32[]{:S(2)}, u32[]{:S(2)}) collective-permute-start(bf16[128,512]{1,0:T(8,128)(2,1)S(1)} %collective-permute-done.1), channel_id=1, source_target_pairs={{0,8},{8,0},{16,24},{24,16},{1,9},{9,1},{17,25},{25,17},{2,10},{10... | collective-permute-start | bytes 393224 | tf_op jit(solution)/shard_map/ppermute | solution.py:16
  68.4 5.3 %collective-permute-start.10 = (bf16[256,512]{1,0:T(8,128)(2,1)S(1)}, bf16[256,512]{1,0:T(8,128)(2,1)S(1)}, u32[]{:S(2)}, u32[]{:S(2)}) collective-permute-start(bf16[256,512]{1,0:T(8,128)(2,1)S(1)} %fusion.13), channel_id=1, source_target_pairs={{0,8},{8,0},{16,24},{24,16},{1,9},{9,1},{17,25},{25,17},{2,10},{10... | collective-permute-start | bytes 786440 | tf_op jit(solution)/shard_map/ppermute | solution.py:16
  70.1 9.1 %collective-permute-start.25 = (bf16[2,32,1024]{2,1,0:T(8,128)(2,1)S(1)}, bf16[2,32,1024]{2,1,0:T(8,128)(2,1)S(1)}, u32[]{:S(2)}, u32[]{:S(2)}) collective-permute-start(bf16[2,32,1024]{2,1,0:T(8,128)(2,1)S(1)} %copy-done.5), channel_id=1, source_target_pairs={{0,2},{1,3},{2,0},{3,1},{4,6},{5,7},{6,4},{7,5},{8,10},{9,11},{10,... | collective-permute-start | bytes 393224 | tf_op jit(solution)/shard_map/ppermute | solution.py:16
  70.2 16.1 %collective-permute-start.27 = (bf16[2,32,1024]{2,1,0:T(8,128)(2,1)S(1)}, bf16[2,32,1024]{2,1,0:T(8,128)(2,1)S(1)}, u32[]{:S(2)}, u32[]{:S(2)}) collective-permute-start(bf16[2,32,1024]{2,1,0:T(8,128)(2,1)S(1)} %collective-permute-done.26), channel_id=1, source_target_pairs={{0,1},{1,0},{2,3},{3,2},{4,5},{5,4},{6,7},{7,6},{8,9},{9,8},{10,11... | collective-permute-start | bytes 393224 | tf_op jit(solution)/shard_map/ppermute | solution.py:16
  71.0 21.9 %collective-permute-start.29 = (bf16[2,32,1024]{2,1,0:T(8,128)(2,1)}, bf16[2,32,1024]{2,1,0:T(8,128)(2,1)S(1)}, u32[]{:S(2)}, u32[]{:S(2)}) collective-permute-start(bf16[2,32,1024]{2,1,0:T(8,128)(2,1)} %collective-permute-done.28), channel_id=1, source_target_pairs={{0,1},{1,0},{2,3},{3,2},{4,5},{5,4},{6,7},{7,6},{8,9},{9,8},{10,11... | collective-permute-start | bytes 393224 | tf_op jit(solution)/shard_map/ppermute | solution.py:16
  73.9 5.3 %collective-permute-start.11 = (bf16[128,512]{1,0:T(8,128)(2,1)S(1)}, bf16[128,512]{1,0:T(8,128)(2,1)S(1)}, u32[]{:S(2)}, u32[]{:S(2)}) collective-permute-start(bf16[128,512]{1,0:T(8,128)(2,1)S(1)} %slice_select_fusion.6), channel_id=1, source_target_pairs={{0,16},{8,24},{16,0},{24,8},{1,17},{9,25},{17,1},{25,9},{2,18},{10... | collective-permute-start | bytes 393224 | tf_op jit(solution)/shard_map/ppermute | solution.py:16
  79.2 1.3 %collective-permute-start.12 = (bf16[128,512]{1,0:T(8,128)(2,1)S(1)}, bf16[128,512]{1,0:T(8,128)(2,1)S(1)}, u32[]{:S(2)}, u32[]{:S(2)}) collective-permute-start(bf16[128,512]{1,0:T(8,128)(2,1)S(1)} %collective-permute-done.11), channel_id=1, source_target_pairs={{0,8},{8,0},{16,24},{24,16},{1,9},{9,1},{17,25},{25,17},{2,10},{10... | collective-permute-start | bytes 393224 | tf_op jit(solution)/shard_map/ppermute | solution.py:16
  85.4 1.6 %collective-permute-start.20 = (bf16[256,512]{1,0:T(8,128)(2,1)S(1)}, bf16[256,512]{1,0:T(8,128)(2,1)S(1)}, u32[]{:S(2)}, u32[]{:S(2)}) collective-permute-start(bf16[256,512]{1,0:T(8,128)(2,1)S(1)} %fusion.14), channel_id=1, source_target_pairs={{0,8},{8,0},{16,24},{24,16},{1,9},{9,1},{17,25},{25,17},{2,10},{10... | collective-permute-start | bytes 786440 | tf_op jit(solution)/shard_map/ppermute | solution.py:16
  87.1 5.7 %collective-permute-start.21 = (bf16[128,512]{1,0:T(8,128)(2,1)S(1)}, bf16[128,512]{1,0:T(8,128)(2,1)S(1)}, u32[]{:S(2)}, u32[]{:S(2)}) collective-permute-start(bf16[128,512]{1,0:T(8,128)(2,1)S(1)} %slice_select_fusion.5), channel_id=1, source_target_pairs={{0,16},{8,24},{16,0},{24,8},{1,17},{9,25},{17,1},{25,9},{2,18},{10... | collective-permute-start | bytes 393224 | tf_op jit(solution)/shard_map/ppermute | solution.py:16
  92.9 1.3 %collective-permute-start.22 = (bf16[128,512]{1,0:T(8,128)(2,1)S(1)}, bf16[128,512]{1,0:T(8,128)(2,1)S(1)}, u32[]{:S(2)}, u32[]{:S(2)}) collective-permute-start(bf16[128,512]{1,0:T(8,128)(2,1)S(1)} %collective-permute-done.21), channel_id=1, source_target_pairs={{0,8},{8,0},{16,24},{24,16},{1,9},{9,1},{17,25},{25,17},{2,10},{10... | collective-permute-start | bytes 393224 | tf_op jit(solution)/shard_map/ppermute | solution.py:16
  99.1 1.6 %collective-permute-start.30 = (bf16[256,512]{1,0:T(8,128)(2,1)S(1)}, bf16[256,512]{1,0:T(8,128)(2,1)S(1)}, u32[]{:S(2)}, u32[]{:S(2)}) collective-permute-start(bf16[256,512]{1,0:T(8,128)(2,1)S(1)} %fusion.15), channel_id=1, source_target_pairs={{0,8},{8,0},{16,24},{24,16},{1,9},{9,1},{17,25},{25,17},{2,10},{10... | collective-permute-start | bytes 786440 | tf_op jit(solution)/shard_map/ppermute | solution.py:16
  100.9 5.6 %collective-permute-start.31 = (bf16[128,512]{1,0:T(8,128)(2,1)S(1)}, bf16[128,512]{1,0:T(8,128)(2,1)S(1)}, u32[]{:S(2)}, u32[]{:S(2)}) collective-permute-start(bf16[128,512]{1,0:T(8,128)(2,1)S(1)} %slice_select_fusion.4), channel_id=1, source_target_pairs={{0,16},{8,24},{16,0},{24,8},{1,17},{9,25},{17,1},{25,9},{2,18},{10... | collective-permute-start | bytes 393224 | tf_op jit(solution)/shard_map/ppermute | solution.py:16
  (20 other events, 112.8 us)

commit v2 on v1

v2 whole, which is shorter than its diff:
```python
import functools

import jax
import jax.numpy as jnp
from jax import lax
from jax.experimental import pallas as pl
from jax.experimental.pallas import tpu as pltpu
from jax.sharding import PartitionSpec as P

GROUPS = ((0,), (1, 2, 3))
CHUNKS = ((0,), (1, 2, 3))
BF = jnp.bfloat16
F32 = jnp.float32
I32 = jnp.int32
W = 256
VMEM = pl.BlockSpec(memory_space=pltpu.VMEM)
SMEM = pl.BlockSpec(memory_space=pltpu.SMEM)
FIRST, LOW, HIGH, IS_LOW, ROW, CORE, ME = range(7)


def group_pairs(steps):
    return [(k, e) for k in steps for e in steps if e < k]


PAIRS = [pair for steps in GROUPS for pair in group_pairs(steps)]
SPECIAL = len(CHUNKS) - 1


def swap(value, axis, size, mask):
    return lax.ppermute(value, axis, [(i, i ^ mask) for i in range(size)])


def dot_tn(a, b):
    return lax.dot_general(a, b, (((0,), (0,)), ((), ())), preferred_element_type=F32)


def dot_nt(a, b):
    return lax.dot_general(a, b, (((1,), (1,)), ((), ())), preferred_element_type=F32)


def dot(a, b):
    return jnp.dot(a, b, preferred_element_type=F32)


def pivot_views(piv_ref):
    rows = piv_ref[...]
    both = jnp.concatenate([rows, rows], axis=0)
    columns = jnp.transpose(both)
    return (lambda k: rows[k : k + 1, :]), (lambda k: columns[:, k : k + 1])


def matches(steps, row_of, col_of):
    out = {}
    for k in steps:
        found = jnp.zeros((W, 1), I32)
        terms = []
        for e in reversed([e for e in steps if e < k]):
            same = (col_of(k) == row_of(e)).astype(I32)
            same = same * (1 - found)
            terms.append((e, same.astype(F32).astype(BF)))
            found = found + jnp.sum(same, axis=1, keepdims=True)
        out[k] = (terms, found)
    return out


def later_matches(k, e, steps, row_of, col_of):
    found = jnp.zeros((1, W), I32)
    for q in steps:
        if e < q < k:
            found = jnp.maximum(found, jnp.max((col_of(q) == row_of(k)).astype(I32), axis=0, keepdims=True))
    return found


def scale_row(fac_ref, step, lo, count, tile):
    parts = [jnp.full((1, tile), fac_ref[step, t], F32) for t in range(lo // tile, (lo + count) // tile)]
    return jnp.concatenate(parts, axis=1) if len(parts) > 1 else parts[0]


def pick_rows(scal, col, source, row_dev):
    lane = lax.broadcasted_iota(I32, (W, row_dev), 1) + scal[FIRST]
    sel = (col == lane).astype(F32).astype(BF)
    return dot(sel, source)


def first_kernel(tile, scal, fac, piv, mat, pan, v_ref, sp_ref):
    row_dev = mat.shape[0]
    _, col_of = pivot_views(piv)
    is_top = scal[ROW] == 0
    if v_ref is not None:
        for at, k in enumerate(GROUPS[0]):
            got = pick_rows(scal, col_of(k), mat[...], row_dev)
            top = mat[k * W : (k + 1) * W, :].astype(F32)
            v_ref[at * W : (at + 1) * W, :] = jnp.where(is_top, top, got).astype(BF)
    if sp_ref is not None:
        lane = lax.broadcasted_iota(I32, (W, row_dev), 1) + scal[FIRST]
        scaled = {}
        for e in sorted({e for _, e in PAIRS}):
            scaled[e] = (pan[e].astype(F32) * scale_row(fac, e, 0, row_dev, tile)).astype(BF)
        sels = {k: (col_of(k) == lane).astype(F32).astype(BF) for k in sorted({k for k, _ in PAIRS})}
        for at, (k, e) in enumerate(PAIRS):
            got = dot_nt(scaled[e], sels[k])
            top = scaled[e][:, k * W : (k + 1) * W].astype(F32)
            sp_ref[:, at * W : (at + 1) * W] = jnp.where(is_top, top, got).astype(BF)


def slices_resolved(scal, piv, tops, picks):
    row_of, col_of = pivot_views(piv)
    out = []
    for steps in GROUPS:
        table = matches(steps, row_of, col_of)
        for k, e in group_pairs(steps):
            value = picks[(k, e)]
            between = [(q, m) for q, m in table[k][0] if q > e]
            if between:
                moved = sum(dot_nt(tops[(q, e)].astype(BF), m) for q, m in between)
                p = row_of(k)
                here = (p >= scal[LOW]) & (p < scal[HIGH])
                resolve = (later_matches(k, e, steps, row_of, col_of) > 0) & (here | (scal[IS_LOW] == 1))
                value = jnp.where(resolve, moved, value)
            out.append(value)
    return out


def here_lanes(scal, piv, k):
    p = piv[k : k + 1, :]
    return (p >= scal[LOW]) & (p < scal[HIGH])


def slice_message_kernel(scal, piv, own, other, out):
    is_top = scal[ROW] == 0
    low = scal[IS_LOW] == 1
    tops, picks, sums = {}, {}, {}
    for at, pair in enumerate(PAIRS):
        lanes = slice(at * W, (at + 1) * W)
        a, b = own[:, lanes].astype(F32), other[:, lanes].astype(F32)
        tops[pair] = jnp.where(is_top, a, b)
        picks[pair] = jnp.where(is_top, b, a)
        sums[pair] = a + b
    resolved = slices_resolved(scal, piv, tops, picks)
    for at, pair in enumerate(PAIRS):
        from_low = jnp.where(here_lanes(scal, piv, pair[0]), resolved[at], tops[pair])
        out[:, at * W : (at + 1) * W] = jnp.where(low, from_low, sums[pair]).astype(BF)


def slice_final_kernel(split, scal, piv, own, other, came, pan, out):
    is_top = scal[ROW] == 0
    low = scal[IS_LOW] == 1
    base = 0
    for k in CHUNKS[SPECIAL]:
        out[:, base : base + pan.shape[2]] = pan[k]
        base += pan.shape[2]
    tops, picks = {}, {}
    for at, pair in enumerate(PAIRS):
        lanes = slice(at * W, (at + 1) * W)
        a, b, c = own[:, lanes].astype(F32), other[:, lanes].astype(F32), came[:, lanes].astype(F32)
        tops[pair] = jnp.where(low, jnp.where(is_top, a, b), c)
        chip = jnp.where(low, jnp.where(is_top, b, a), a + b)
        picks[pair] = jnp.where(here_lanes(scal, piv, pair[0]), chip, c)
    resolved = slices_resolved(scal, piv, tops, picks)
    width = len(PAIRS) * W
    for at, pair in enumerate(PAIRS):
        if split:
            value = jnp.where(scal[CORE] == 0, tops[pair], resolved[at])
            out[:, base + at * W : base + (at + 1) * W] = value.astype(BF)
        else:
            out[:, base + at * W : base + (at + 1) * W] = tops[pair].astype(BF)
            out[:, base + width + at * W : base + width + (at + 1) * W] = resolved[at].astype(BF)


def rows_resolved(scal, steps, table, col_of, tops, picks):
    out = []
    for at, k in enumerate(steps):
        value = picks[at]
        terms, found = table[k]
        if terms:
            moved = sum(dot(m, tops[steps.index(e)].astype(BF)) for e, m in terms)
            p = col_of(k)
            here = (p >= scal[LOW]) & (p < scal[HIGH])
            value = jnp.where((found > 0) & (here | (scal[IS_LOW] == 1)), moved, value)
        out.append(value)
    return out


def here_column(scal, p):
    return (p >= scal[LOW]) & (p < scal[HIGH])


def row_message_kernel(steps, scal, piv, own, other, out):
    row_of, col_of = pivot_views(piv)
    n = len(steps)
    is_top = scal[ROW] == 0
    low = scal[IS_LOW] == 1
    a = [own[i * W : (i + 1) * W, :].astype(F32) for i in range(n)]
    b = [other[i * W : (i + 1) * W, :].astype(F32) for i in range(n)]
    tops = [jnp.where(is_top, x, y) for x, y in zip(a, b)]
    picks = [jnp.where(is_top, y, x) for x, y in zip(a, b)]
    table = matches(steps, row_of, col_of)
    resolved = rows_resolved(scal, steps, table, col_of, tops, picks)
    half = W // 2
    for i, k in enumerate(steps):
        from_low = jnp.where(here_column(scal, col_of(k)), resolved[i], tops[i])
        value = jnp.where(low, from_low, a[i] + b[i])
        out[i * half : (i + 1) * half, :] = jnp.where(scal[CORE] == 0, value[:half], value[half:]).astype(BF)


def step_kernel(steps, after, tile, n_piece, offsets, sp_at, split, *refs):
    pairs = group_pairs(steps)
    refs = list(refs)
    scal, fac, piv, own, other, came, rest, cur, inv = refs[:9]
    refs = refs[9:]
    chunk_ids = sorted({offsets[k][0] for k in steps})
    pieces = {}
    for c in chunk_ids:
        pieces[c] = refs[:n_piece]
        refs = refs[n_piece:]
    special = other_special = None
    if pairs:
        special = refs[:n_piece]
        refs = refs[n_piece:]
        if split:
            other_special = refs[0]
            refs = refs[1:]
    new = refs[0]
    refs = refs[1:]
    v_ref = None
    if after:
        v_ref = refs[0]
        refs = refs[1:]
    s_ref, mix_ref, u_ref = refs
    row_of, col_of = pivot_views(piv)
    n = len(steps)
    row_dev, columns = cur.shape
    part = W // n_piece
    is_top = scal[ROW] == 0
    low = scal[IS_LOW] == 1
    core0 = scal[CORE] == 0
    half = W // 2
    tops, picks = [], []
    for i, k in enumerate(steps):
        a = own[i * W : (i + 1) * W, :].astype(F32)
        b = other[i * W : (i + 1) * W, :].astype(F32)
        c = came[i * half : (i + 1) * half, :].astype(F32)
        d = rest[i * half : (i + 1) * half, :].astype(F32)
        got = jnp.concatenate([jnp.where(core0, c, d), jnp.where(core0, d, c)], axis=0)
        tops.append(jnp.where(low, jnp.where(is_top, a, b), got))
        chip = jnp.where(low, jnp.where(is_top, b, a), a + b)
        picks.append(jnp.where(here_column(scal, col_of(k)), chip, got))
    table = matches(steps, row_of, col_of)
    chosen = rows_resolved(scal, steps, table, col_of, tops, picks)

    def side_rows(pair, which):
        base = sp_at + PAIRS.index(pair) * W
        if not split:
            base = base + which * len(PAIRS) * W
            return jnp.concatenate([p[:, base : base + W] for p in special], axis=0)
        mine = jnp.concatenate([p[:, base : base + W] for p in special], axis=0)
        at = PAIRS.index(pair) * W
        theirs = other_special[:, at : at + W]
        mine_is = core0 if which == 0 else jnp.logical_not(core0)
        return jnp.where(mine_is, mine.astype(F32), theirs.astype(F32)).astype(BF)

    for i, k in enumerate(steps):
        acc, upper = chosen[i], tops[i]
        for j, e in enumerate(steps[:i]):
            mixed = mix_ref[j * W : (j + 1) * W, :]
            acc = acc - dot_tn(side_rows((k, e), 1), mixed)
            upper = upper - dot_tn(side_rows((k, e), 0), mixed)
        u_ref[i * W : (i + 1) * W, :] = upper.astype(BF)
        s_ref[i * W : (i + 1) * W, :] = dot(inv[k], acc.astype(BF)).astype(BF)
        for m in range(n_piece):
            if n_piece == 1:
                mix_ref[i * W : (i + 1) * W, :] = s_ref[i * W : (i + 1) * W, :]
                break
            start = pl.multiple_of((scal[ME] ^ m) * part, part)
            mix_ref[i * W + m * part : i * W + (m + 1) * part, :] = s_ref[pl.ds(i * W + start, part), :]

    for lo in range(0, row_dev, W):
        ids = lax.broadcasted_iota(I32, (W, W), 0) + scal[FIRST] + lo
        taken = jnp.zeros((W, 1), I32)
        placed = jnp.zeros((W, columns), F32)
        for i in reversed(range(n)):
            same = (ids == row_of(steps[i])).astype(I32) * (1 - taken)
            placed = placed + dot(same.astype(F32).astype(BF), u_ref[i * W : (i + 1) * W, :])
            taken = taken + jnp.sum(same, axis=1, keepdims=True)
        old = cur[lo : lo + W, :].astype(F32)
        acc = jnp.where(taken > 0, placed, old)
        lane = lax.broadcasted_iota(I32, (W, W), 1) + scal[FIRST] + lo
        alive = jnp.ones((1, W), F32)
        for i in reversed(range(n)):
            k = steps[i]
            c, off = offsets[k]
            block = jnp.concatenate([p[:, off + lo : off + lo + W] for p in pieces[c]], axis=0)
            weight = scale_row(fac, k, lo, W, tile) * alive
            block = (block.astype(F32) * weight).astype(BF)
            acc = acc - dot_tn(block, mix_ref[i * W : (i + 1) * W, :])
            if i:
                hit = jnp.max((col_of(k) == lane).astype(F32), axis=0, keepdims=True)
                alive = alive * (1.0 - hit)
        at = lo // W
        if at in steps:
            i = steps.index(at)
            acc = jnp.where(is_top, s_ref[i * W : (i + 1) * W, :].astype(F32), acc)
        elif at < steps[0]:
            acc = jnp.where(is_top, old, acc)
        new[lo : lo + W, :] = acc.astype(BF)
    for i, k in enumerate(after):
        got = pick_rows(scal, col_of(k), new[...], row_dev)
        top = new[k * W : (k + 1) * W, :].astype(F32)
        v_ref[i * W : (i + 1) * W, :] = jnp.where(is_top, top, got).astype(BF)


def call(kernel, shapes, n_smem, *args, scratch=()):
    single = not isinstance(shapes, (list, tuple))
    out = pl.pallas_call(
        kernel,
        out_shape=shapes,
        in_specs=[SMEM] * n_smem + [VMEM] * (len(args) - n_smem),
        out_specs=VMEM if single else [VMEM] * len(shapes),
        scratch_shapes=list(scratch),
        compiler_params=pltpu.CompilerParams(vmem_limit_bytes=40 * 1024 * 1024),
    )(*args)
    return out


def gather(own, n_col):
    if n_col != 8:
        return [lax.all_gather(own, "pcol", axis=0, tiled=True)]
    z2 = swap(own, "pcol", 8, 4)
    z3 = swap(own, "pcol", 8, 6)
    x0 = swap(own, "pcol", 8, 1)
    z1 = swap(own, "pcol", 8, 2)
    z1x = swap(x0, "pcol", 8, 2)
    z2x = swap(z2, "pcol", 8, 1)
    z3x = swap(z3, "pcol", 8, 1)
    return [own, x0, z1, z1x, z2, z2x, z3, z3x]


def make(n_row, n_col):
    split = n_row == 4
    n_piece = 8 if n_col == 8 else 1

    def psum_pair(own, row):
        zero = jnp.zeros_like(own)
        picks = lax.psum(jnp.where(row == 0, zero, own), "prow")
        tops = lax.psum(jnp.where(row == 0, own, zero), "prow")
        return picks.astype(F32).astype(BF), tops.astype(F32).astype(BF)

    def on_device(matrix, panels, exponents, inverses, pivots):
        row_dev, columns = matrix.shape
        steps_all = pivots.shape[0]
        assert steps_all * W <= row_dev and pivots.shape[1] == W
        tile = row_dev // exponents.shape[1]
        part = W // n_col
        row = lax.axis_index("prow")
        me = lax.axis_index("pcol")
        first_row = row * row_dev
        if split:
            chip = row // 2
            scal = jnp.stack([first_row, chip * 2 * row_dev, (chip + 1) * 2 * row_dev, (chip == 0).astype(I32), row, row % 2, me, me])
        else:
            zero = jnp.zeros((), I32)
            scal = jnp.stack([first_row, zero, zero + n_row * row_dev, zero + 1, row, zero, me, me])
        scal = scal.astype(I32)
        scal2 = scal if split else scal.at[ROW].set(1)
        top_scal = scal
        fac = jnp.exp2(exponents.astype(F32))

        wide = len(PAIRS) * W
        bf = lambda *shape: jax.ShapeDtypeStruct(shape, BF)

        def no_special(scal, fac, piv, mat, pan, v):
            first_kernel(tile, scal, fac, piv, mat, pan, v, None)

        def only_special(scal, fac, piv, mat, pan, sp):
            first_kernel(tile, scal, fac, piv, mat, pan, None, sp)

        arrived = [None] * len(CHUNKS)
        offsets = {}
        for c, chunk in enumerate(CHUNKS):
            for i, k in enumerate(chunk):
                offsets[k] = (c, i * row_dev)
        for c, chunk in enumerate(CHUNKS):
            if c != SPECIAL or not PAIRS:
                own = jnp.concatenate([panels[k] for k in chunk], axis=1)
                arrived[c] = gather(own, n_col)
        rows = call(no_special, bf(len(GROUPS[0]) * W, columns), 2, top_scal, fac, pivots, matrix, panels)
        sp_at = len(CHUNKS[SPECIAL]) * row_dev
        special = other_special = None
        if PAIRS:
            sp = call(only_special, bf(part, wide), 2, top_scal, fac, pivots, matrix, panels)
            if split:
                sp_other = swap(sp, "prow", 4, 1)
                message = call(slice_message_kernel, bf(part, wide), 1, scal, pivots, sp, sp_other)
                sp_came = swap(message, "prow", 4, 2)
            else:
                sp, sp_other = psum_pair(sp, row)
                sp_came = sp
            load = sp_at + (wide if split else 2 * wide)
            own = call(
                functools.partial(slice_final_kernel, split), bf(part, load), 1, scal2, pivots, sp, sp_other, sp_came, panels
            )
            arrived[SPECIAL] = gather(own, n_col)
            special = arrived[SPECIAL]
            if split:
                mine = jnp.concatenate([p[:, sp_at:] for p in special], axis=0)
                other_special = swap(mine, "prow", 4, 1)

        current = matrix
        for g, steps in enumerate(GROUPS):
            after = GROUPS[g + 1] if g + 1 < len(GROUPS) else ()
            n = len(steps)
            if split:
                other = swap(rows, "prow", 4, 1)
                message = call(functools.partial(row_message_kernel, steps), bf(n * W // 2, columns), 1, scal, pivots, rows, other)
                came = swap(message, "prow", 4, 2)
                rest = swap(came, "prow", 4, 1)
            else:
                rows, other = psum_pair(rows, row)
                came = rest = rows[: n * W // 2]
            pairs = group_pairs(steps)
            args = [scal2, fac, pivots, rows, other, came, rest, current, inverses]
            for c in sorted({offsets[k][0] for k in steps}):
                args += arrived[c]
            if pairs:
                args += special
                if split:
                    args.append(other_special)
            shapes = [bf(row_dev, columns)] + ([bf(len(after) * W, columns)] if after else [])
            out = call(
                functools.partial(step_kernel, steps, after, tile, n_piece, offsets, sp_at, split),
                shapes,
                2,
                *args,
                scratch=[pltpu.VMEM((n * W, columns), BF)] * 3,
            )
            current = out[0]
            rows = out[1] if after else None
        return current

    return on_device


def solution(mesh):
    return jax.shard_map(
        make(mesh.shape["prow"], mesh.shape["pcol"]),
        mesh=mesh,
        in_specs=(P("prow", "pcol"), P(None, "pcol", "prow"), P(None, "prow"), P(), P()),
        out_specs=P("prow", "pcol"),
        check_vma=False,
    )
```

time: 115 us -> 74.1 us (0.64)
  matrix products: 18 us -> 0 us
  Pallas kernels: 0 us -> 16.4 us
  local copies, waits for them, and re-layouts: 19.6 us -> 3.6 us
  starting transfers between devices: 36.1 us -> 23.9 us
  other arithmetic: 9.72 us -> 0.01 us
    dot_general x16 -> x0, matrix products: 18 us -> none  [the longest x4 7.06 us: on_device(): lax.dot_general(blocks[step], mixed, (((0,), (0,)), ((), ())), preferred_...]
    pallas_call x0 -> x8, Pallas kernels: none -> 16.4 us  [call(): pl.pallas_call(kernel, out_shape=shapes, in_specs=[SMEM] * n_smem + [VMEM...]
    ppermute x33 -> x23, starting transfers between devices: 36.1 us -> 23.9 us  [swap(): return lax.ppermute(value, axis, [(i, i ^ mask) for i in range(size)])]
    unnamed x57 -> x19, local copies, waits for them, and re-layouts: 8.79 us -> 3.51 us
    slice x4 -> x0, local copies, waits for them, and re-layouts: 3.89 us -> none  [the longest x2 2.45 us: on_device(): got = gather_panels(panels[chunk[0]:chunk[-1] + 1], n_col)]
    gather x4 -> x0, local copies, waits for them, and re-layouts: 2.87 us -> none  [on_device(): mixed = solved.reshape(n_col, part, -1)[order].reshape(width, -1)]
    concatenate x3 -> x1, local copies, waits for them, and re-layouts: 2.11 us -> 0.01 us  [on_device(): mine = jnp.concatenate([p[:, sp_at:] for p in special], axis=0)]
    mul x4 -> x0, local copies, waits for them, and re-layouts: 1.99 us -> none  [on_device(): blocks[step] = jnp.concatenate([g[at] for g in got]) * factor[step][None, :]]
  transfers between devices with their start and end apart: 33 -> 23, of which waited for: 15 -> 7; matrix products, arithmetic and copies ran while one was open for 31% -> 0% of each run, Pallas kernels for 0% -> 12%
where the time goes in v2:
time: 74.1 us; the launch traced here: 73.9 us
  waiting for transfers between devices  29.9 us (40%)
  starting transfers between devices  23.9 us (32%)
  Pallas kernels  16.4 us (22%)
  local copies, waits for them, and re-layouts  3.6 us (5%)
    ppermute x23, waiting for transfers between devices, swap(): return lax.ppermute(value, axis, [(i, i ^ mask) for i in range(size)])  29.9 us
    ppermute x23, starting transfers between devices, swap(): return lax.ppermute(value, axis, [(i, i ^ mask) for i in range(size)])  23.9 us
    pallas_call x8, Pallas kernels, call(): pl.pallas_call(kernel, out_shape=shapes, in_specs=[SMEM] * n_smem + [VMEM...  16.4 us
    unnamed x19, local copies, waits for them, and re-layouts  3.51 us
  transfers between devices with their start and end apart: 23, of which 7 were waited for; matrix products, arithmetic and copies ran while one was open for 0% of the time, Pallas kernels for 12%

profile of v2, /device:TPU:0, one launch (start us, length us, event | category | flops | bytes accessed | tf_op | source)
XLA Modules:
  0.0 73.9 jit_solution(6125463674648239507)
XLA Ops:
  0.0 0.7 copy-done.5
  0.8 0.6 copy-done.4
  1.4 1.2 %copy-done = bf16[1024,512]{1,0:T(8,128)(2,1)S(1)} copy-done((bf16[1024,512]{1,0:T(8,128)(2,1)S(1)}, bf16[1024,512]{1,0:T(8,128)(2,1)}, u32[]{:S(2)}) %copy-start) | copy-done | bytes 1048600
  2.6 0.9 %copy-done.2 = bf16[4,32,1024]{2,1,0:T(8,128)(2,1)S(1)} copy-done((bf16[4,32,1024]{2,1,0:T(8,128)(2,1)S(1)}, bf16[4,32,1024]{2,1,0:T(8,128)(2,1)}, u32[]{:S(2)}) %copy-start.2) | copy-done | bytes 262168
  3.6 1.3 %shard_map.59.own = bf16[32,768]{1,0:T(8,128)(2,1)S(1)} custom-call(s32[8]{0:T(128)S(1)} %stack.36.scal.refs_0_, f32[4,8]{1,0:T(4,128)S(1)} %multiply_exponential_fusion.fac.refs_1_, s32[4,256]{1,0:T(4,128)S(1)} %copy-done.4, bf16[1024,512]{1,0:T(8,128)(2,1)S(1)} %copy-done, bf16[4,32,1024]{2,1,0:T(8,128)(2,1)S(1)} %copy-done.2), custom_call_target="tpu_custom_call" | custom-call | tf_op jit(solution)/shard_map/pallas_call | solution.py:314
  5.4 1.2 %shard_map.55.own.refs_3_ = bf16[256,512]{1,0:T(8,128)(2,1)S(1)} custom-call(s32[8]{0:T(128)S(1)} %stack.36.scal.refs_0_, f32[4,8]{1,0:T(4,128)S(1)} %multiply_exponential_fusion.fac.refs_1_, s32[4,256]{1,0:T(4,128)S(1)} %copy-done.4, bf16[1024,512]{1,0:T(8,128)(2,1)S(1)} %copy-done, bf16[4,32,1024]{2,1,0:T(8,128)(2,1)S(1)} %copy-done.2), custom_call_target="tpu_custom_call" | custom-call | tf_op jit(solution)/shard_map/pallas_call | solution.py:314
  6.7 5.0 %collective-permute-start.8 = (bf16[32,1024]{1,0:T(8,128)(2,1)S(1)}, bf16[32,1024]{1,0:T(8,128)(2,1)S(1)}, u32[]{:S(2)}, u32[]{:S(2)}) collective-permute-start(bf16[32,1024]{1,0:T(8,128)(2,1)S(1)} %slice_bitcast_fusion.refs_9_), channel_id=1, source_target_pairs={{0,6},{1,7},{2,4},{3,5},{4,2},{5,3},{6,0},{7,1},{8,14},{9,15},{10,... | collective-permute-start | bytes 196616 | tf_op jit(solution)/shard_map/ppermute | solution.py:30
  11.8 1.5 %collective-permute-start.3 = (bf16[32,1024]{1,0:T(8,128)(2,1)S(1)}, bf16[32,1024]{1,0:T(8,128)(2,1)S(1)}, u32[]{:S(2)}, u32[]{:S(2)}) collective-permute-start(bf16[32,1024]{1,0:T(8,128)(2,1)S(1)} %slice_bitcast_fusion.refs_9_), channel_id=1, source_target_pairs={{0,1},{1,0},{2,3},{3,2},{4,5},{5,4},{6,7},{7,6},{8,9},{9,8},{10,11... | collective-permute-start | bytes 196616 | tf_op jit(solution)/shard_map/ppermute | solution.py:30
  13.3 0.9 %shard_map.60 = bf16[32,768]{1,0:T(8,128)(2,1)S(1)} custom-call(s32[8]{0:T(128)S(1)} %stack.36.scal.refs_0_, s32[4,256]{1,0:T(4,128)S(1)} %copy-done.4, bf16[32,768]{1,0:T(8,128)(2,1)S(1)} %shard_map.59.own, bf16[32,768]{1,0:T(8,128)(2,1)S(1)} %collective-permute-done.13.other), custom_call_target="tpu_custom_call" | custom-call | tf_op jit(solution)/shard_map/pallas_call | solution.py:314
  14.2 1.5 %collective-permute-start.14 = (bf16[32,768]{1,0:T(8,128)(2,1)S(1)}, bf16[32,768]{1,0:T(8,128)(2,1)S(1)}, u32[]{:S(2)}, u32[]{:S(2)}) collective-permute-start(bf16[32,768]{1,0:T(8,128)(2,1)S(1)} %shard_map.60), channel_id=1, source_target_pairs={{0,16},{8,24},{16,0},{24,8},{1,17},{9,25},{17,1},{25,9},{2,18},{10... | collective-permute-start | bytes 147464 | tf_op jit(solution)/shard_map/ppermute | solution.py:30
  15.7 1.5 %collective-permute-start.4 = (bf16[32,1024]{1,0:T(8,128)(2,1)S(1)}, bf16[32,1024]{1,0:T(8,128)(2,1)S(1)}, u32[]{:S(2)}, u32[]{:S(2)}) collective-permute-start(bf16[32,1024]{1,0:T(8,128)(2,1)S(1)} %slice_bitcast_fusion.refs_9_), channel_id=1, source_target_pairs={{0,2},{1,3},{2,0},{3,1},{4,6},{5,7},{6,4},{7,5},{8,10},{9,11},{10,... | collective-permute-start | bytes 196616 | tf_op jit(solution)/shard_map/ppermute | solution.py:30
  17.6 1.6 %collective-permute-start.9 = (bf16[32,1024]{1,0:T(8,128)(2,1)S(1)}, bf16[32,1024]{1,0:T(8,128)(2,1)S(1)}, u32[]{:S(2)}, u32[]{:S(2)}) collective-permute-start(bf16[32,1024]{1,0:T(8,128)(2,1)S(1)} %collective-permute-done.8.refs_15_), channel_id=1, source_target_pairs={{0,1},{1,0},{2,3},{3,2},{4,5},{5,4},{6,7},{7,6},{8,9},{9,8},{10,11... | collective-permute-start | bytes 196616 | tf_op jit(solution)/shard_map/ppermute | solution.py:30
  19.8 0.9 %shard_map.61.refs_9_.refs_17_ = bf16[32,3840]{1,0:T(8,128)(2,1)S(1)} custom-call(s32[8]{0:T(128)S(1)} %stack.36.scal.refs_0_, s32[4,256]{1,0:T(4,128)S(1)} %copy-done.4, bf16[32,768]{1,0:T(8,128)(2,1)S(1)} %shard_map.59.own, bf16[32,768]{1,0:T(8,128)(2,1)S(1)} %collective-permute-done.13.other, bf16[32,768]{1,0:T(8,128)(2,1)S(1)} %collective-permute-done.14.came, ...), custom_call_target="tpu_custom_call" | custom-call | tf_op jit(solution)/shard_map/pallas_call | solution.py:314
  20.7 1.5 %collective-permute-start.15 = (bf16[32,3840]{1,0:T(8,128)(2,1)S(1)}, bf16[32,3840]{1,0:T(8,128)(2,1)S(1)}, u32[]{:S(2)}, u32[]{:S(2)}) collective-permute-start(bf16[32,3840]{1,0:T(8,128)(2,1)S(1)} %shard_map.61.refs_9_.refs_17_), channel_id=1, source_target_pairs={{0,1},{1,0},{2,3},{3,2},{4,5},{5,4},{6,7},{7,6},{8,9},{9,8},{10,11... | collective-permute-start | bytes 737288 | tf_op jit(solution)/shard_map/ppermute | solution.py:30
  22.3 0.8 %shard_map.56 = bf16[128,512]{1,0:T(8,128)(2,1)S(1)} custom-call(s32[8]{0:T(128)S(1)} %stack.36.scal.refs_0_, s32[4,256]{1,0:T(4,128)S(1)} %copy-done.4, bf16[256,512]{1,0:T(8,128)(2,1)S(1)} %shard_map.55.own.refs_3_, bf16[256,512]{1,0:T(8,128)(2,1)S(1)} %collective-permute-done.other.refs_4_), custom_call_target="tpu_custom_call" | custom-call | tf_op jit(solution)/shard_map/pallas_call | solution.py:314
  23.1 2.8 %collective-permute-start.20 = (bf16[32,3840]{1,0:T(8,128)(2,1)S(1)}, bf16[32,3840]{1,0:T(8,128)(2,1)S(1)}, u32[]{:S(2)}, u32[]{:S(2)}) collective-permute-start(bf16[32,3840]{1,0:T(8,128)(2,1)S(1)} %shard_map.61.refs_9_.refs_17_), channel_id=1, source_target_pairs={{0,6},{1,7},{2,4},{3,5},{4,2},{5,3},{6,0},{7,1},{8,14},{9,15},{10,... | collective-permute-start | bytes 737288 | tf_op jit(solution)/shard_map/ppermute | solution.py:30
  25.9 0.7 collective-permute-start.18
  26.7 0.9 %collective-permute-start.16 = (bf16[32,3840]{1,0:T(8,128)(2,1)S(1)}, bf16[32,3840]{1,0:T(8,128)(2,1)S(1)}, u32[]{:S(2)}, u32[]{:S(2)}) collective-permute-start(bf16[32,3840]{1,0:T(8,128)(2,1)S(1)} %shard_map.61.refs_9_.refs_17_), channel_id=1, source_target_pairs={{0,2},{1,3},{2,0},{3,1},{4,6},{5,7},{6,4},{7,5},{8,10},{9,11},{10,... | collective-permute-start | bytes 737288 | tf_op jit(solution)/shard_map/ppermute | solution.py:30
  27.6 1.5 %collective-permute-start.1 = (bf16[128,512]{1,0:T(8,128)(2,1)S(1)}, bf16[128,512]{1,0:T(8,128)(2,1)S(1)}, u32[]{:S(2)}, u32[]{:S(2)}) collective-permute-start(bf16[128,512]{1,0:T(8,128)(2,1)S(1)} %shard_map.56), channel_id=1, source_target_pairs={{0,16},{8,24},{16,0},{24,8},{1,17},{9,25},{17,1},{25,9},{2,18},{10... | collective-permute-start | bytes 393224 | tf_op jit(solution)/shard_map/ppermute | solution.py:30
  29.1 1.2 %collective-permute-start.17 = (bf16[32,3840]{1,0:T(8,128)(2,1)S(1)}, bf16[32,3840]{1,0:T(8,128)(2,1)S(1)}, u32[]{:S(2)}, u32[]{:S(2)}) collective-permute-start(bf16[32,3840]{1,0:T(8,128)(2,1)S(1)} %collective-permute-done.15.refs_10_.refs_18_), channel_id=1, source_target_pairs={{0,2},{1,3},{2,0},{3,1},{4,6},{5,7},{6,4},{7,5},{8,10},{9,11},{10,... | collective-permute-start | bytes 737288 | tf_op jit(solution)/shard_map/ppermute | solution.py:30
  30.3 2.3 %collective-permute-done.1.refs_5_ = bf16[128,512]{1,0:T(8,128)(2,1)S(1)} collective-permute-done((bf16[128,512]{1,0:T(8,128)(2,1)S(1)}, bf16[128,512]{1,0:T(8,128)(2,1)S(1)}, u32[]{:S(2)}, u32[]{:S(2)}) %collective-permute-start.1) | collective-permute-done | bytes 131104 | tf_op jit(solution)/shard_map/ppermute | solution.py:30
  32.6 1.4 %collective-permute-done.20.refs_15_.refs_23_ = bf16[32,3840]{1,0:T(8,128)(2,1)S(1)} collective-permute-done((bf16[32,3840]{1,0:T(8,128)(2,1)S(1)}, bf16[32,3840]{1,0:T(8,128)(2,1)S(1)}, u32[]{:S(2)}, u32[]{:S(2)}) %collective-permute-start.20) | collective-permute-done | bytes 245792 | tf_op jit(solution)/shard_map/ppermute | solution.py:30
  34.0 0.6 collective-permute-start.21
  34.5 12.3 %collective-permute-done.18.refs_13_.refs_21_ = bf16[32,3840]{1,0:T(8,128)(2,1)S(1)} collective-permute-done((bf16[32,3840]{1,0:T(8,128)(2,1)S(1)}, bf16[32,3840]{1,0:T(8,128)(2,1)S(1)}, u32[]{:S(2)}, u32[]{:S(2)}) %collective-permute-start.18) | collective-permute-done | bytes 245792 | tf_op jit(solution)/shard_map/ppermute | solution.py:30
  46.8 0.5 collective-permute-start.19
  47.4 2.9 %shard_map.57 = (bf16[1024,512]{1,0:T(8,128)(2,1)S(1)}, bf16[768,512]{1,0:T(8,128)(2,1)S(1)}) custom-call(s32[8]{0:T(128)S(1)} %stack.36.scal.refs_0_, f32[4,8]{1,0:T(4,128)S(1)} %multiply_exponential_fusion.fac.refs_1_, s32[4,256]{1,0:T(4,128)S(1)} %copy-done.4, bf16[256,512]{1,0:T(8,128)(2,1)S(1)} %shard_map.55.own.refs_3_, ...), custom_call_target="tpu_custom_call" | custom-call | tf_op jit(solution)/shard_map/pallas_call | solution.py:314
  50.5 3.5 %collective-permute-done.19.refs_14_.refs_22_ = bf16[32,3840]{1,0:T(8,128)(2,1)S(1)} collective-permute-done((bf16[32,3840]{1,0:T(8,128)(2,1)S(1)}, bf16[32,3840]{1,0:T(8,128)(2,1)S(1)}, u32[]{:S(2)}, u32[]{:S(2)}) %collective-permute-start.19) | collective-permute-done | bytes 245792 | tf_op jit(solution)/shard_map/ppermute | solution.py:30
  54.0 1.8 %shard_map.58 = bf16[384,512]{1,0:T(8,128)(2,1)S(1)} custom-call(s32[8]{0:T(128)S(1)} %stack.36.scal.refs_0_, s32[4,256]{1,0:T(4,128)S(1)} %copy-done.4, bf16[768,512]{1,0:T(8,128)(2,1)S(1)} %get-tuple-element.7.own.refs_3_, bf16[768,512]{1,0:T(8,128)(2,1)S(1)} %collective-permute-done.10.other.refs_4_), custom_call_target="tpu_custom_call" | custom-call | tf_op jit(solution)/shard_map/pallas_call | solution.py:314
  55.8 1.6 %collective-permute-start.11 = (bf16[384,512]{1,0:T(8,128)(2,1)S(1)}, bf16[384,512]{1,0:T(8,128)(2,1)S(1)}, u32[]{:S(2)}, u32[]{:S(2)}) collective-permute-start(bf16[384,512]{1,0:T(8,128)(2,1)S(1)} %shard_map.58), channel_id=1, source_target_pairs={{0,16},{8,24},{16,0},{24,8},{1,17},{9,25},{17,1},{25,9},{2,18},{10... | collective-permute-start | bytes 1179656 | tf_op jit(solution)/shard_map/ppermute | solution.py:30
  57.5 8.2 %collective-permute-done.11.refs_5_ = bf16[384,512]{1,0:T(8,128)(2,1)S(1)} collective-permute-done((bf16[384,512]{1,0:T(8,128)(2,1)S(1)}, bf16[384,512]{1,0:T(8,128)(2,1)S(1)}, u32[]{:S(2)}, u32[]{:S(2)}) %collective-permute-start.11) | collective-permute-done | bytes 393248 | tf_op jit(solution)/shard_map/ppermute | solution.py:30
  65.7 1.7 %collective-permute-done.12.refs_6_ = bf16[384,512]{1,0:T(8,128)(2,1)S(1)} collective-permute-done((bf16[384,512]{1,0:T(8,128)(2,1)S(1)}, bf16[384,512]{1,0:T(8,128)(2,1)S(1)}, u32[]{:S(2)}, u32[]{:S(2)}) %collective-permute-start.12) | collective-permute-done | bytes 393248 | tf_op jit(solution)/shard_map/ppermute | solution.py:30
  67.5 6.4 %shard_map.62 = bf16[1024,512]{1,0:T(8,128)(2,1)} custom-call(s32[8]{0:T(128)S(1)} %stack.36.scal.refs_0_, f32[4,8]{1,0:T(4,128)S(1)} %multiply_exponential_fusion.fac.refs_1_, s32[4,256]{1,0:T(4,128)S(1)} %copy-done.4, bf16[768,512]{1,0:T(8,128)(2,1)S(1)} %get-tuple-element.7.own.refs_3_, bf16[768,512]{1,0:T(8,128)(2,1)S(1)} %collective-permute-done.10.other.refs_4_, ...), custom_call_target="tpu_custom_call" | custom-call | tf_op jit(solution)/shard_map/pallas_call | solution.py:314
  (45 shorter events, 1.9 us)
Async XLA Ops:
  0.0 0.7 copy-start.5
  0.7 0.7 copy-start.4
  1.4 1.2 %copy-start = (bf16[1024,512]{1,0:T(8,128)(2,1)S(1)}, bf16[1024,512]{1,0:T(8,128)(2,1)}, u32[]{:S(2)}) copy-start(bf16[1024,512]{1,0:T(8,128)(2,1)} %mat.3) | copy-start | bytes 3145732
  2.6 0.9 %copy-start.2 = (bf16[4,32,1024]{2,1,0:T(8,128)(2,1)S(1)}, bf16[4,32,1024]{2,1,0:T(8,128)(2,1)}, u32[]{:S(2)}) copy-start(bf16[4,32,1024]{2,1,0:T(8,128)(2,1)} %pan.5) | copy-start | bytes 786436
  4.9 8.4 %collective-permute-start.13 = (bf16[32,768]{1,0:T(8,128)(2,1)S(1)}, bf16[32,768]{1,0:T(8,128)(2,1)S(1)}, u32[]{:S(2)}, u32[]{:S(2)}) collective-permute-start(bf16[32,768]{1,0:T(8,128)(2,1)S(1)} %shard_map.59.own), channel_id=1, source_target_pairs={{0,8},{8,0},{16,24},{24,16},{1,9},{9,1},{17,25},{25,17},{2,10},{10... | collective-permute-start | bytes 147464 | tf_op jit(solution)/shard_map/ppermute | solution.py:30
  6.6 40.8 %copy-start.1 = (bf16[1024,512]{1,0:T(8,128)(2,1)S(1)}, bf16[1024,512]{1,0:T(8,128)(2,1)}, u32[]{:S(2)}) copy-start(bf16[1024,512]{1,0:T(8,128)(2,1)} %mat.3) | copy-start | bytes 3145732
  6.6 14.2 %collective-permute-start = (bf16[256,512]{1,0:T(8,128)(2,1)S(1)}, bf16[256,512]{1,0:T(8,128)(2,1)S(1)}, u32[]{:S(2)}, u32[]{:S(2)}) collective-permute-start(bf16[256,512]{1,0:T(8,128)(2,1)S(1)} %shard_map.55.own.refs_3_), channel_id=1, source_target_pairs={{0,8},{8,0},{16,24},{24,16},{1,9},{9,1},{17,25},{25,17},{2,10},{10... | collective-permute-start | bytes 786440 | tf_op jit(solution)/shard_map/ppermute | solution.py:30
  6.7 9.0 %collective-permute-start.8 = (bf16[32,1024]{1,0:T(8,128)(2,1)S(1)}, bf16[32,1024]{1,0:T(8,128)(2,1)S(1)}, u32[]{:S(2)}, u32[]{:S(2)}) collective-permute-start(bf16[32,1024]{1,0:T(8,128)(2,1)S(1)} %slice_bitcast_fusion.refs_9_), channel_id=1, source_target_pairs={{0,6},{1,7},{2,4},{3,5},{4,2},{5,3},{6,0},{7,1},{8,14},{9,15},{10,... | collective-permute-start | bytes 196616 | tf_op jit(solution)/shard_map/ppermute | solution.py:30
  11.8 5.9 %collective-permute-start.6 = (bf16[32,1024]{1,0:T(8,128)(2,1)S(1)}, bf16[32,1024]{1,0:T(8,128)(2,1)S(1)}, u32[]{:S(2)}, u32[]{:S(2)}) collective-permute-start(bf16[32,1024]{1,0:T(8,128)(2,1)S(1)} %slice_bitcast_fusion.refs_9_), channel_id=1, source_target_pairs={{0,4},{1,5},{2,6},{3,7},{4,0},{5,1},{6,2},{7,3},{8,12},{9,13},{10,... | collective-permute-start | bytes 196616 | tf_op jit(solution)/shard_map/ppermute | solution.py:30
  11.8 7.5 %collective-permute-start.3 = (bf16[32,1024]{1,0:T(8,128)(2,1)S(1)}, bf16[32,1024]{1,0:T(8,128)(2,1)S(1)}, u32[]{:S(2)}, u32[]{:S(2)}) collective-permute-start(bf16[32,1024]{1,0:T(8,128)(2,1)S(1)} %slice_bitcast_fusion.refs_9_), channel_id=1, source_target_pairs={{0,1},{1,0},{2,3},{3,2},{4,5},{5,4},{6,7},{7,6},{8,9},{9,8},{10,11... | collective-permute-start | bytes 196616 | tf_op jit(solution)/shard_map/ppermute | solution.py:30
  14.2 5.5 %collective-permute-start.14 = (bf16[32,768]{1,0:T(8,128)(2,1)S(1)}, bf16[32,768]{1,0:T(8,128)(2,1)S(1)}, u32[]{:S(2)}, u32[]{:S(2)}) collective-permute-start(bf16[32,768]{1,0:T(8,128)(2,1)S(1)} %shard_map.60), channel_id=1, source_target_pairs={{0,16},{8,24},{16,0},{24,8},{1,17},{9,25},{17,1},{25,9},{2,18},{10... | collective-permute-start | bytes 147464 | tf_op jit(solution)/shard_map/ppermute | solution.py:30
  15.7 7.4 %collective-permute-start.4 = (bf16[32,1024]{1,0:T(8,128)(2,1)S(1)}, bf16[32,1024]{1,0:T(8,128)(2,1)S(1)}, u32[]{:S(2)}, u32[]{:S(2)}) collective-permute-start(bf16[32,1024]{1,0:T(8,128)(2,1)S(1)} %slice_bitcast_fusion.refs_9_), channel_id=1, source_target_pairs={{0,2},{1,3},{2,0},{3,1},{4,6},{5,7},{6,4},{7,5},{8,10},{9,11},{10,... | collective-permute-start | bytes 196616 | tf_op jit(solution)/shard_map/ppermute | solution.py:30
  17.6 8.3 %collective-permute-start.9 = (bf16[32,1024]{1,0:T(8,128)(2,1)S(1)}, bf16[32,1024]{1,0:T(8,128)(2,1)S(1)}, u32[]{:S(2)}, u32[]{:S(2)}) collective-permute-start(bf16[32,1024]{1,0:T(8,128)(2,1)S(1)} %collective-permute-done.8.refs_15_), channel_id=1, source_target_pairs={{0,1},{1,0},{2,3},{3,2},{4,5},{5,4},{6,7},{7,6},{8,9},{9,8},{10,11... | collective-permute-start | bytes 196616 | tf_op jit(solution)/shard_map/ppermute | solution.py:30
  19.2 7.5 %collective-permute-start.7 = (bf16[32,1024]{1,0:T(8,128)(2,1)S(1)}, bf16[32,1024]{1,0:T(8,128)(2,1)S(1)}, u32[]{:S(2)}, u32[]{:S(2)}) collective-permute-start(bf16[32,1024]{1,0:T(8,128)(2,1)S(1)} %collective-permute-done.6.refs_13_), channel_id=1, source_target_pairs={{0,1},{1,0},{2,3},{3,2},{4,5},{5,4},{6,7},{7,6},{8,9},{9,8},{10,11... | collective-permute-start | bytes 196616 | tf_op jit(solution)/shard_map/ppermute | solution.py:30
  19.7 7.9 %collective-permute-start.5 = (bf16[32,1024]{1,0:T(8,128)(2,1)S(1)}, bf16[32,1024]{1,0:T(8,128)(2,1)S(1)}, u32[]{:S(2)}, u32[]{:S(2)}) collective-permute-start(bf16[32,1024]{1,0:T(8,128)(2,1)S(1)} %collective-permute-done.3.refs_10_), channel_id=1, source_target_pairs={{0,2},{1,3},{2,0},{3,1},{4,6},{5,7},{6,4},{7,5},{8,10},{9,11},{10,... | collective-permute-start | bytes 196616 | tf_op jit(solution)/shard_map/ppermute | solution.py:30
  20.7 26.7 %copy-start.3 = (bf16[4,256,256]{2,1,0:T(8,128)(2,1)S(1)}, bf16[4,256,256]{2,1,0:T(8,128)(2,1)}, u32[]{:S(2)}) copy-start(bf16[4,256,256]{2,1,0:T(8,128)(2,1)} %refs_8_.3) | copy-start | bytes 1572868
  20.7 8.4 %collective-permute-start.15 = (bf16[32,3840]{1,0:T(8,128)(2,1)S(1)}, bf16[32,3840]{1,0:T(8,128)(2,1)S(1)}, u32[]{:S(2)}, u32[]{:S(2)}) collective-permute-start(bf16[32,3840]{1,0:T(8,128)(2,1)S(1)} %shard_map.61.refs_9_.refs_17_), channel_id=1, source_target_pairs={{0,1},{1,0},{2,3},{3,2},{4,5},{5,4},{6,7},{7,6},{8,9},{9,8},{10,11... | collective-permute-start | bytes 737288 | tf_op jit(solution)/shard_map/ppermute | solution.py:30
  23.1 10.9 %collective-permute-start.20 = (bf16[32,3840]{1,0:T(8,128)(2,1)S(1)}, bf16[32,3840]{1,0:T(8,128)(2,1)S(1)}, u32[]{:S(2)}, u32[]{:S(2)}) collective-permute-start(bf16[32,3840]{1,0:T(8,128)(2,1)S(1)} %shard_map.61.refs_9_.refs_17_), channel_id=1, source_target_pairs={{0,6},{1,7},{2,4},{3,5},{4,2},{5,3},{6,0},{7,1},{8,14},{9,15},{10,... | collective-permute-start | bytes 737288 | tf_op jit(solution)/shard_map/ppermute | solution.py:30
  25.9 20.9 %collective-permute-start.18 = (bf16[32,3840]{1,0:T(8,128)(2,1)S(1)}, bf16[32,3840]{1,0:T(8,128)(2,1)S(1)}, u32[]{:S(2)}, u32[]{:S(2)}) collective-permute-start(bf16[32,3840]{1,0:T(8,128)(2,1)S(1)} %shard_map.61.refs_9_.refs_17_), channel_id=1, source_target_pairs={{0,4},{1,5},{2,6},{3,7},{4,0},{5,1},{6,2},{7,3},{8,12},{9,13},{10,... | collective-permute-start | bytes 737288 | tf_op jit(solution)/shard_map/ppermute | solution.py:30
  26.7 23.7 %collective-permute-start.16 = (bf16[32,3840]{1,0:T(8,128)(2,1)S(1)}, bf16[32,3840]{1,0:T(8,128)(2,1)S(1)}, u32[]{:S(2)}, u32[]{:S(2)}) collective-permute-start(bf16[32,3840]{1,0:T(8,128)(2,1)S(1)} %shard_map.61.refs_9_.refs_17_), channel_id=1, source_target_pairs={{0,2},{1,3},{2,0},{3,1},{4,6},{5,7},{6,4},{7,5},{8,10},{9,11},{10,... | collective-permute-start | bytes 737288 | tf_op jit(solution)/shard_map/ppermute | solution.py:30
  27.6 5.0 %collective-permute-start.1 = (bf16[128,512]{1,0:T(8,128)(2,1)S(1)}, bf16[128,512]{1,0:T(8,128)(2,1)S(1)}, u32[]{:S(2)}, u32[]{:S(2)}) collective-permute-start(bf16[128,512]{1,0:T(8,128)(2,1)S(1)} %shard_map.56), channel_id=1, source_target_pairs={{0,16},{8,24},{16,0},{24,8},{1,17},{9,25},{17,1},{25,9},{2,18},{10... | collective-permute-start | bytes 393224 | tf_op jit(solution)/shard_map/ppermute | solution.py:30
  29.1 21.3 %collective-permute-start.17 = (bf16[32,3840]{1,0:T(8,128)(2,1)S(1)}, bf16[32,3840]{1,0:T(8,128)(2,1)S(1)}, u32[]{:S(2)}, u32[]{:S(2)}) collective-permute-start(bf16[32,3840]{1,0:T(8,128)(2,1)S(1)} %collective-permute-done.15.refs_10_.refs_18_), channel_id=1, source_target_pairs={{0,2},{1,3},{2,0},{3,1},{4,6},{5,7},{6,4},{7,5},{8,10},{9,11},{10,... | collective-permute-start | bytes 737288 | tf_op jit(solution)/shard_map/ppermute | solution.py:30
  32.5 14.8 %collective-permute-start.2 = (bf16[128,512]{1,0:T(8,128)(2,1)S(1)}, bf16[128,512]{1,0:T(8,128)(2,1)S(1)}, u32[]{:S(2)}, u32[]{:S(2)}) collective-permute-start(bf16[128,512]{1,0:T(8,128)(2,1)S(1)} %collective-permute-done.1.refs_5_), channel_id=1, source_target_pairs={{0,8},{8,0},{16,24},{24,16},{1,9},{9,1},{17,25},{25,17},{2,10},{10... | collective-permute-start | bytes 393224 | tf_op jit(solution)/shard_map/ppermute | solution.py:30
  34.0 23.5 %collective-permute-start.21 = (bf16[32,3840]{1,0:T(8,128)(2,1)S(1)}, bf16[32,3840]{1,0:T(8,128)(2,1)S(1)}, u32[]{:S(2)}, u32[]{:S(2)}) collective-permute-start(bf16[32,3840]{1,0:T(8,128)(2,1)S(1)} %collective-permute-done.20.refs_15_.refs_23_), channel_id=1, source_target_pairs={{0,1},{1,0},{2,3},{3,2},{4,5},{5,4},{6,7},{7,6},{8,9},{9,8},{10,11... | collective-permute-start | bytes 737288 | tf_op jit(solution)/shard_map/ppermute | solution.py:30
  46.8 7.1 %collective-permute-start.19 = (bf16[32,3840]{1,0:T(8,128)(2,1)S(1)}, bf16[32,3840]{1,0:T(8,128)(2,1)S(1)}, u32[]{:S(2)}, u32[]{:S(2)}) collective-permute-start(bf16[32,3840]{1,0:T(8,128)(2,1)S(1)} %collective-permute-done.18.refs_13_.refs_21_), channel_id=1, source_target_pairs={{0,1},{1,0},{2,3},{3,2},{4,5},{5,4},{6,7},{7,6},{8,9},{9,8},{10,11... | collective-permute-start | bytes 737288 | tf_op jit(solution)/shard_map/ppermute | solution.py:30
  50.3 3.7 %collective-permute-start.10 = (bf16[768,512]{1,0:T(8,128)(2,1)S(1)}, bf16[768,512]{1,0:T(8,128)(2,1)S(1)}, u32[]{:S(2)}, u32[]{:S(2)}) collective-permute-start(bf16[768,512]{1,0:T(8,128)(2,1)S(1)} %get-tuple-element.7.own.refs_3_), channel_id=1, source_target_pairs={{0,8},{8,0},{16,24},{24,16},{1,9},{9,1},{17,25},{25,17},{2,10},{10... | collective-permute-start | bytes 2359304 | tf_op jit(solution)/shard_map/ppermute | solution.py:30
  55.8 9.9 %collective-permute-start.11 = (bf16[384,512]{1,0:T(8,128)(2,1)S(1)}, bf16[384,512]{1,0:T(8,128)(2,1)S(1)}, u32[]{:S(2)}, u32[]{:S(2)}) collective-permute-start(bf16[384,512]{1,0:T(8,128)(2,1)S(1)} %shard_map.58), channel_id=1, source_target_pairs={{0,16},{8,24},{16,0},{24,8},{1,17},{9,25},{17,1},{25,9},{2,18},{10... | collective-permute-start | bytes 1179656 | tf_op jit(solution)/shard_map/ppermute | solution.py:30
  57.4 8.3 %collective-permute-start.22 = (bf16[256,768]{1,0:T(8,128)(2,1)S(1)}, bf16[256,768]{1,0:T(8,128)(2,1)S(1)}, u32[]{:S(2)}, u32[]{:S(2)}) collective-permute-start(bf16[256,768]{1,0:T(8,128)(2,1)S(1)} %slice_dynamic-update-slice_fusion), channel_id=1, source_target_pairs={{0,8},{8,0},{16,24},{24,16},{1,9},{9,1},{17,25},{25,17},{2,10},{10... | collective-permute-start | bytes 1179656 | tf_op jit(solution)/shard_map/ppermute | solution.py:30
  65.7 1.7 %collective-permute-start.12 = (bf16[384,512]{1,0:T(8,128)(2,1)S(1)}, bf16[384,512]{1,0:T(8,128)(2,1)S(1)}, u32[]{:S(2)}, u32[]{:S(2)}) collective-permute-start(bf16[384,512]{1,0:T(8,128)(2,1)S(1)} %collective-permute-done.11.refs_5_), channel_id=1, source_target_pairs={{0,8},{8,0},{16,24},{24,16},{1,9},{9,1},{17,25},{25,17},{2,10},{10... | collective-permute-start | bytes 1179656 | tf_op jit(solution)/shard_map/ppermute | solution.py:30

commit v3 on v2

v3 whole, which is shorter than its diff:
```python
import functools

import jax
import jax.numpy as jnp
from jax import lax
from jax.experimental import pallas as pl
from jax.experimental.pallas import tpu as pltpu
from jax.sharding import PartitionSpec as P

STEPS = (0, 1, 2, 3)
PAIRS = [(k, e) for k in STEPS for e in STEPS if e < k]
BF = jnp.bfloat16
F32 = jnp.float32
I32 = jnp.int32
W = 256
VMEM = pl.BlockSpec(memory_space=pltpu.VMEM)
SMEM = pl.BlockSpec(memory_space=pltpu.SMEM)
COST = pl.CostEstimate(flops=20000000000, bytes_accessed=1000, transcendentals=0)
FIRST, LOW, HIGH, IS_LOW, ROW, CORE, ME = range(7)


def swap(value, axis, size, mask):
    return lax.ppermute(value, axis, [(i, i ^ mask) for i in range(size)])


def dot_tn(a, b):
    return lax.dot_general(a, b, (((0,), (0,)), ((), ())), preferred_element_type=F32)


def dot_nt(a, b):
    return lax.dot_general(a, b, (((1,), (1,)), ((), ())), preferred_element_type=F32)


def dot(a, b):
    return jnp.dot(a, b, preferred_element_type=F32)


def pivot_views(piv_ref):
    rows = piv_ref[...]
    both = jnp.concatenate([rows, rows], axis=0)
    columns = jnp.transpose(both)
    return (lambda k: rows[k : k + 1, :]), (lambda k: columns[:, k : k + 1])


def matches(steps, row_of, col_of):
    out = {}
    for k in steps:
        found = jnp.zeros((W, 1), I32)
        terms = []
        for e in reversed([e for e in steps if e < k]):
            same = (col_of(k) == row_of(e)).astype(I32)
            same = same * (1 - found)
            terms.append((e, same.astype(F32).astype(BF)))
            found = found + jnp.sum(same, axis=1, keepdims=True)
        out[k] = (terms, found)
    return out


def later_matches(k, e, steps, row_of, col_of):
    found = jnp.zeros((1, W), I32)
    for q in steps:
        if e < q < k:
            found = jnp.maximum(found, jnp.max((col_of(q) == row_of(k)).astype(I32), axis=0, keepdims=True))
    return found


def scale_row(exp_ref, step, lo, count, tile):
    parts = []
    for t in range(lo // tile, (lo + count) // tile):
        e = exp_ref[step, t]
        scale = jnp.where(e >= 0, jnp.where(e == 1, 2.0, 1.0), jnp.where(e == -1, 0.5, jnp.where(e == -2, 0.25, 0.125)))
        parts.append(jnp.full((1, tile), scale, F32))
    return jnp.concatenate(parts, axis=1) if len(parts) > 1 else parts[0]


def pick_rows(scal, col, source, row_dev):
    lane = lax.broadcasted_iota(I32, (W, row_dev), 1) + scal[FIRST]
    sel = (col == lane).astype(F32).astype(BF)
    return dot(sel, source)


def slice_pick_kernel(tile, scal, fac, piv, pan, sp_ref):
    row_dev = pan.shape[2]
    _, col_of = pivot_views(piv)
    is_top = scal[ROW] == 0
    lane = lax.broadcasted_iota(I32, (W, row_dev), 1) + scal[FIRST]
    for k in STEPS[1:]:
        sel = (col_of(k) == lane).astype(F32).astype(BF)
        scaled = jnp.concatenate([pan[e].astype(F32) * scale_row(fac, e, 0, row_dev, tile) for e in STEPS[:k]], axis=0).astype(BF)
        got = dot_nt(scaled, sel)
        top = scaled[:, k * W : (k + 1) * W].astype(F32)
        value = jnp.where(is_top, top, got).astype(BF)
        part = pan.shape[1]
        for e in STEPS[:k]:
            at = PAIRS.index((k, e))
            sp_ref[:, at * W : (at + 1) * W] = value[e * part : (e + 1) * part]


def row_pick_kernel(scal, piv, mat, v_ref):
    _, col_of = pivot_views(piv)
    is_top = scal[ROW] == 0
    for k in STEPS:
        @pl.when(is_top)
        def _():
            v_ref[k * W : (k + 1) * W, :] = mat[k * W : (k + 1) * W, :]

        @pl.when(jnp.logical_not(is_top))
        def _():
            v_ref[k * W : (k + 1) * W, :] = pick_rows(scal, col_of(k), mat[...], mat.shape[0]).astype(BF)


def pass_first(kernel, first, scal, *refs):
    kernel(first, scal, *refs)


def slices_resolved(scal, piv, tops, picks):
    row_of, col_of = pivot_views(piv)
    out = []
    table = matches(STEPS, row_of, col_of)
    for k, e in PAIRS:
        value = picks[(k, e)]
        between = [(q, m) for q, m in table[k][0] if q > e]
        if between:
            moved = sum(dot_nt(tops[(q, e)].astype(BF), m) for q, m in between)
            p = row_of(k)
            here = (p >= scal[LOW]) & (p < scal[HIGH])
            resolve = (later_matches(k, e, STEPS, row_of, col_of) > 0) & (here | (scal[IS_LOW] == 1))
            value = jnp.where(resolve, moved, value)
        out.append(value)
    return out


def here_lanes(scal, piv, k):
    p = piv[k : k + 1, :]
    return (p >= scal[LOW]) & (p < scal[HIGH])


def slice_message_kernel(scal, piv, own, other, out):
    is_top = scal[ROW] == 0
    low = scal[IS_LOW] == 1
    tops, picks, sums = {}, {}, {}
    for at, pair in enumerate(PAIRS):
        lanes = slice(at * W, (at + 1) * W)
        a, b = own[:, lanes].astype(F32), other[:, lanes].astype(F32)
        tops[pair] = jnp.where(is_top, a, b)
        picks[pair] = jnp.where(is_top, b, a)
        sums[pair] = a + b
    resolved = slices_resolved(scal, piv, tops, picks)
    for at, pair in enumerate(PAIRS):
        from_low = jnp.where(here_lanes(scal, piv, pair[0]), resolved[at], tops[pair])
        out[:, at * W : (at + 1) * W] = jnp.where(low, from_low, sums[pair]).astype(BF)


def slice_final_kernel(split, scal, piv, own, other, came, out):
    is_top = scal[ROW] == 0
    low = scal[IS_LOW] == 1
    tops, picks = {}, {}
    for at, pair in enumerate(PAIRS):
        lanes = slice(at * W, (at + 1) * W)
        a, b, c = own[:, lanes].astype(F32), other[:, lanes].astype(F32), came[:, lanes].astype(F32)
        tops[pair] = jnp.where(low, jnp.where(is_top, a, b), c)
        chip = jnp.where(low, jnp.where(is_top, b, a), a + b)
        picks[pair] = jnp.where(here_lanes(scal, piv, pair[0]), chip, c)
    resolved = slices_resolved(scal, piv, tops, picks)
    width = len(PAIRS) * W
    for at, pair in enumerate(PAIRS):
        if split:
            value = jnp.where(scal[CORE] == 0, tops[pair], resolved[at])
            out[:, at * W : (at + 1) * W] = value.astype(BF)
        else:
            out[:, at * W : (at + 1) * W] = tops[pair].astype(BF)
            out[:, width + at * W : width + (at + 1) * W] = resolved[at].astype(BF)


def rows_resolved(scal, steps, table, col_of, tops, picks):
    out = []
    for at, k in enumerate(steps):
        value = picks[at]
        terms, found = table[k]
        if terms:
            moved = sum(dot(m, tops[steps.index(e)].astype(BF)) for e, m in terms)
            p = col_of(k)
            here = (p >= scal[LOW]) & (p < scal[HIGH])
            value = jnp.where((found > 0) & (here | (scal[IS_LOW] == 1)), moved, value)
        out.append(value)
    return out


def here_column(scal, p):
    return (p >= scal[LOW]) & (p < scal[HIGH])


def row_message_kernel(scal, piv, own, other, out):
    steps = STEPS
    row_of, col_of = pivot_views(piv)
    n = len(steps)
    is_top = scal[ROW] == 0
    low = scal[IS_LOW] == 1
    a = [own[i * W : (i + 1) * W, :].astype(F32) for i in range(n)]
    b = [other[i * W : (i + 1) * W, :].astype(F32) for i in range(n)]
    tops = [jnp.where(is_top, x, y) for x, y in zip(a, b)]
    picks = [jnp.where(is_top, y, x) for x, y in zip(a, b)]
    table = matches(steps, row_of, col_of)
    resolved = rows_resolved(scal, steps, table, col_of, tops, picks)
    half = W // 2
    for i, k in enumerate(steps):
        from_low = jnp.where(here_column(scal, col_of(k)), resolved[i], tops[i])
        value = jnp.where(low, from_low, a[i] + b[i])
        out[i * half : (i + 1) * half, :] = jnp.where(scal[CORE] == 0, value[:half], value[half:]).astype(BF)


def chain_kernel(tile, n_piece, split, scal, *refs):
    fac, piv, own, other, came, rest, cur, inv = refs[:8]
    special = refs[8 : 8 + n_piece]
    refs = refs[8 + n_piece :]
    other_special = None
    if split:
        other_special = refs[0]
        refs = refs[1:]
    mix_ref, base_ref, weight_ref, s_ref, u_ref = refs
    row_of, col_of = pivot_views(piv)
    row_dev, columns = cur.shape
    part = W // n_piece
    is_top = scal[ROW] == 0
    top_block = scal[FIRST] == 0
    low = scal[IS_LOW] == 1
    core0 = scal[CORE] == 0
    half = W // 2
    tops, picks = [], []
    for k in STEPS:
        a = own[k * W : (k + 1) * W, :].astype(F32)
        b = other[k * W : (k + 1) * W, :].astype(F32)
        c = came[k * half : (k + 1) * half, :].astype(F32)
        d = rest[k * half : (k + 1) * half, :].astype(F32)
        got = jnp.concatenate([jnp.where(core0, c, d), jnp.where(core0, d, c)], axis=0)
        tops.append(jnp.where(low, jnp.where(is_top, a, b), got))
        chip = jnp.where(low, jnp.where(is_top, b, a), a + b)
        picks.append(jnp.where(here_column(scal, col_of(k)), chip, got))
    table = matches(STEPS, row_of, col_of)
    chosen = rows_resolved(scal, STEPS, table, col_of, tops, picks)

    def side_rows(pair, which):
        base = PAIRS.index(pair) * W
        if not split:
            base = base + which * len(PAIRS) * W
            return jnp.concatenate([p[:, base : base + W] for p in special], axis=0)
        mine = jnp.concatenate([p[:, base : base + W] for p in special], axis=0)
        theirs = other_special[:, base : base + W]
        mine_is = core0 if which == 0 else jnp.logical_not(core0)
        return jnp.where(mine_is, mine.astype(F32), theirs.astype(F32)).astype(BF)

    for k in STEPS:
        acc, upper = chosen[k], tops[k]
        for e in STEPS[:k]:
            mixed = mix_ref[e * W : (e + 1) * W, :]
            acc = acc - dot_tn(side_rows((k, e), 1), mixed)
            upper = upper - dot_tn(side_rows((k, e), 0), mixed)
        u_ref[k * W : (k + 1) * W, :] = upper.astype(BF)
        s_ref[k * W : (k + 1) * W, :] = dot(inv[k], acc.astype(BF)).astype(BF)
        for m in range(n_piece):
            if n_piece == 1:
                mix_ref[k * W : (k + 1) * W, :] = s_ref[k * W : (k + 1) * W, :]
                break
            start = pl.multiple_of((scal[ME] ^ m) * part, part)
            mix_ref[k * W + m * part : k * W + (m + 1) * part, :] = s_ref[pl.ds(k * W + start, part), :]

    for lo in range(0, row_dev, W):
        ids = lax.broadcasted_iota(I32, (W, W), 0) + scal[FIRST] + lo
        lane = lax.broadcasted_iota(I32, (W, W), 1) + scal[FIRST] + lo
        taken = jnp.zeros((W, 1), I32)
        placed = jnp.zeros((W, columns), F32)
        alive = jnp.where(top_block, jnp.zeros((1, W), F32), jnp.ones((1, W), F32))
        for k in reversed(STEPS):
            same = (ids == row_of(k)).astype(I32) * (1 - taken)
            placed = placed + dot(same.astype(F32).astype(BF), u_ref[k * W : (k + 1) * W, :])
            taken = taken + jnp.sum(same, axis=1, keepdims=True)
            weight_ref[k : k + 1, lo : lo + W] = scale_row(fac, k, lo, W, tile) * alive
            if k:
                hit = jnp.max((col_of(k) == lane).astype(F32), axis=0, keepdims=True)
                alive = alive * (1.0 - hit)
        value = jnp.where(taken > 0, placed, cur[lo : lo + W, :].astype(F32))
        value = jnp.where(top_block, s_ref[lo : lo + W, :].astype(F32), value)
        base_ref[lo : lo + W, :] = value.astype(BF)


def update_kernel(n_piece, base, weight, mix, *refs):
    pieces, out = refs[:n_piece], refs[n_piece]
    acc = base[...].astype(F32)
    for k in STEPS:
        block = jnp.concatenate([p[k] for p in pieces], axis=0).astype(F32)
        block = (block * weight[k : k + 1, :]).astype(BF)
        acc = acc - dot_tn(block, mix[k * W : (k + 1) * W, :])
    out[...] = acc.astype(BF)


def place(split, row_dev, n_row, summed):
    row = lax.axis_index("prow")
    me = lax.axis_index("pcol")
    first = row * row_dev
    if split:
        chip = row // 2
        return [first, chip * 2 * row_dev, (chip + 1) * 2 * row_dev, (chip == 0).astype(I32), row, row % 2, me]
    return [first, 0, n_row * row_dev, 1, 1 if summed else row, 0, me]


def call(kernel, where, shapes, n_smem, *args, scratch=()):
    single = not isinstance(shapes, (list, tuple))

    def body(*refs):
        kernel(place(*where), *refs)

    return pl.pallas_call(
        body,
        out_shape=shapes,
        in_specs=[SMEM] * n_smem + [VMEM] * (len(args) - n_smem),
        out_specs=VMEM if single else [VMEM] * len(shapes),
        scratch_shapes=list(scratch),
        cost_estimate=COST,
        compiler_params=pltpu.CompilerParams(vmem_limit_bytes=40 * 1024 * 1024),
    )(*args)


def gather(own, axis):
    return [lax.all_gather(own, "pcol", axis=axis, tiled=True)]


def after(value, *others):
    return lax.optimization_barrier((value,) + others)[0]


def make(n_row, n_col):
    split = n_row == 4 and n_col == 8
    n_piece = 8 if split else 1

    def psum_pair(own, row):
        zero = jnp.zeros_like(own)
        picks = lax.psum(jnp.where(row == 0, zero, own), "prow")
        tops = lax.psum(jnp.where(row == 0, own, zero), "prow")
        return picks.astype(F32).astype(BF), tops.astype(F32).astype(BF)

    def on_device(matrix, panels, exponents, inverses, pivots):
        row_dev, columns = matrix.shape
        assert len(STEPS) * W == row_dev and pivots.shape == (len(STEPS), W)
        tile = row_dev // exponents.shape[1]
        part = W // n_col
        row = lax.axis_index("prow")
        where = (split, row_dev, n_row, False)
        where2 = (split, row_dev, n_row, True)
        wide = len(PAIRS) * W
        bf = lambda *shape: jax.ShapeDtypeStruct(shape, BF)

        sp = call(functools.partial(pass_first, slice_pick_kernel, tile), where, bf(part, wide), 1, exponents, pivots, panels)
        rows = call(row_pick_kernel, where, bf(row_dev, columns), 0, pivots, matrix)
        load = wide if split else 2 * wide
        final_slices = functools.partial(pass_first, slice_final_kernel, split)
        if split:
            sp_other = swap(sp, "prow", 4, 1)
            message = call(slice_message_kernel, where, bf(part, wide), 0, pivots, sp, sp_other)
            sp_came = swap(message, "prow", 4, 2)
        else:
            sp, sp_other = psum_pair(sp, row)
            sp_came = sp
        if n_piece == 8:
            bz2 = swap(panels, "pcol", 8, 4)
            bx0 = swap(panels, "pcol", 8, 1)
            bz1 = swap(panels, "pcol", 8, 2)
            sp_came = after(sp_came, bx0, bz1)
            own = call(final_slices, where2, bf(part, load), 0, pivots, sp, sp_other, sp_came)
        else:
            own = call(final_slices, where2, bf(part, load), 0, pivots, sp, sp_other, sp_came)
            bulk, special = gather(panels, 1), gather(own, 0)
        if split:
            other = swap(rows, "prow", 4, 1)
            message = call(row_message_kernel, where, bf(row_dev // 2, columns), 0, after(pivots, own), rows, other)
            came = swap(message, "prow", 4, 2)
            rest = None
        else:
            message = rows
            rows, other = psum_pair(rows, row)
            came = rest = rows[: row_dev // 2]
        held = pivots
        if n_piece == 8:
            sz2 = swap(own, "pcol", 8, 4)
            sz3 = swap(own, "pcol", 8, 6)
            sx0 = swap(own, "pcol", 8, 1)
            sz1 = swap(after(own, message), "pcol", 8, 2)
            sz1x = swap(after(sx0, message), "pcol", 8, 2)
            bz1x = swap(after(bx0, sx0), "pcol", 8, 2)
            bz3 = swap(after(panels, bz2), "pcol", 8, 6)
            sz2x = swap(after(sz2, bz2, message), "pcol", 8, 1)
            sz3x = swap(sz3, "pcol", 8, 1)
            bz2x = swap(after(bz2, sz3), "pcol", 8, 1)
            bz3x = swap(bz3, "pcol", 8, 1)
            bulk = [panels, bx0, bz1, bz1x, bz2, bz2x, bz3, bz3x]
            special = [own, sx0, sz1, sz1x, sz2, sz2x, sz3, sz3x]
            rest = swap(after(came, bz3), "prow", 4, 1)
            special = list(after(tuple(special), bz1x, bz2x))
        if split:
            mine = jnp.concatenate(special, axis=0)
            special = special + [swap(mine, "prow", 4, 1)]
        mix, base, weight = call(
            functools.partial(chain_kernel, tile, n_piece, split),
            where2,
            [bf(row_dev, columns), bf(row_dev, columns), jax.ShapeDtypeStruct((8, row_dev), F32)],
            1,
            exponents, held, rows, other, came, rest, matrix, inverses, *special,
            scratch=[pltpu.VMEM((row_dev, columns), BF)] * 2,
        )
        return pl.pallas_call(
            functools.partial(update_kernel, n_piece),
            out_shape=bf(row_dev, columns),
            grid=(row_dev // W,),
            in_specs=[
                pl.BlockSpec((W, columns), lambda i: (i, 0)),
                pl.BlockSpec((8, W), lambda i: (0, i)),
                pl.BlockSpec((row_dev, columns), lambda i: (0, 0)),
            ]
            + [pl.BlockSpec((len(STEPS), W // n_piece, W), lambda i: (0, 0, i))] * n_piece,
            out_specs=pl.BlockSpec((W, columns), lambda i: (i, 0)),
            cost_estimate=COST,
            compiler_params=pltpu.CompilerParams(vmem_limit_bytes=40 * 1024 * 1024),
        )(base, weight, mix, *bulk)

    return on_device


def solution(mesh):
    return jax.shard_map(
        make(mesh.shape["prow"], mesh.shape["pcol"]),
        mesh=mesh,
        in_specs=(P("prow", "pcol"), P(None, "pcol", "prow"), P(None, "prow"), P(), P()),
        out_specs=P("prow", "pcol"),
        check_vma=False,
    )
```

time: 74.1 us -> 62.3 us (0.84)
  waiting for transfers between devices: 29.9 us -> 20.6 us
  local copies, waits for them, and re-layouts: 3.6 us -> 1.46 us
    ppermute x23 -> x20, waiting for transfers between devices: 29.9 us -> 20.6 us  [swap(): return lax.ppermute(value, axis, [(i, i ^ mask) for i in range(size)])]
    unnamed x19 -> x17, local copies, waits for them, and re-layouts: 3.51 us -> 1.45 us
    ppermute x23 -> x20, starting transfers between devices: 23.9 us -> 23.6 us  [swap(): return lax.ppermute(value, axis, [(i, i ^ mask) for i in range(size)])]
    pallas_call x8 -> x7, Pallas kernels: 16.4 us -> 16.1 us  [the longest x6 12.1 us: call(): pl.pallas_call(body, out_shape=shapes, in_specs=[SMEM] * n_smem + [VMEM]...]
  transfers between devices with their start and end apart: 23 -> 20, of which waited for: 7 -> 9; matrix products, arithmetic and copies ran while one was open for 0% -> 0% of each run, Pallas kernels for 12% -> 17%
where the time goes in v3:
time: 62.3 us; the launch traced here: 61.9 us
  starting transfers between devices  23.6 us (38%)
  waiting for transfers between devices  20.6 us (33%)
  Pallas kernels  16.1 us (26%)
  local copies, waits for them, and re-layouts  1.46 us (2%)
    ppermute x20, starting transfers between devices, swap(): return lax.ppermute(value, axis, [(i, i ^ mask) for i in range(size)])  23.6 us
    ppermute x20, waiting for transfers between devices, swap(): return lax.ppermute(value, axis, [(i, i ^ mask) for i in range(size)])  20.6 us
    pallas_call x6, Pallas kernels, call(): pl.pallas_call(body, out_shape=shapes, in_specs=[SMEM] * n_smem + [VMEM]...  12.1 us
    pallas_call x1, Pallas kernels, on_device(): pl.pallas_call(functools.partial(update_kernel, n_piece), out_shape=bf(ro...  4.05 us
    unnamed x17, local copies, waits for them, and re-layouts  1.45 us
  transfers between devices with their start and end apart: 20, of which 9 were waited for; matrix products, arithmetic and copies ran while one was open for 0% of the time, Pallas kernels for 17%

profile of v3, /device:TPU:0, one launch (start us, length us, event | category | flops | bytes accessed | tf_op | source)
XLA Modules:
  0.0 61.9 jit_solution(5289641941264131551)
XLA Ops:
  0.0 0.7 %copy-done.2 = s32[4,256]{1,0:T(4,128)S(1)} copy-done((s32[4,256]{1,0:T(4,128)S(1)}, s32[4,256]{1,0:T(4,128)}, u32[]{:S(2)}) %copy-start.2) | copy-done | bytes 4120
  0.7 0.7 %copy-done.3 = s32[4,8]{1,0:T(4,128)S(1)} copy-done((s32[4,8]{1,0:T(4,128)S(1)}, s32[4,8]{1,0:T(4,128)}, u32[]{:S(2)}) %copy-start.3) | copy-done | bytes 152
  1.4 1.8 %shard_map.56.refs_1_ = bf16[32,1536]{1,0:T(8,128)(2,1)S(1)} custom-call(s32[4,8]{1,0:T(4,128)S(1)} %copy-done.3, s32[4,256]{1,0:T(4,128)S(1)} %copy-done.2, bf16[4,32,1024]{2,1,0:T(8,128)(2,1)} %refs_0_.12), custom_call_target="tpu_custom_call" | custom-call | flops 20000000000 | bytes 1000 | tf_op jit(solution)/shard_map/pallas_call | solution.py:312
  3.2 0.5 collective-permute-start.1
  3.7 2.6 %collective-permute-start.3 = (bf16[4,32,1024]{2,1,0:T(8,128)(2,1)}, bf16[4,32,1024]{2,1,0:T(8,128)(2,1)S(1)}, u32[]{:S(2)}, u32[]{:S(2)}) collective-permute-start(bf16[4,32,1024]{2,1,0:T(8,128)(2,1)} %refs_0_.12), channel_id=1, source_target_pairs={{0,1},{1,0},{2,3},{3,2},{4,5},{5,4},{6,7},{7,6},{8,9},{9,8},{10,11... | collective-permute-start | bytes 786440 | tf_op jit(solution)/shard_map/ppermute | solution.py:23
  6.2 1.6 %collective-permute-start.4 = (bf16[4,32,1024]{2,1,0:T(8,128)(2,1)}, bf16[4,32,1024]{2,1,0:T(8,128)(2,1)S(1)}, u32[]{:S(2)}, u32[]{:S(2)}) collective-permute-start(bf16[4,32,1024]{2,1,0:T(8,128)(2,1)} %refs_0_.12), channel_id=1, source_target_pairs={{0,2},{1,3},{2,0},{3,1},{4,6},{5,7},{6,4},{7,5},{8,10},{9,11},{10,... | collective-permute-start | bytes 786440 | tf_op jit(solution)/shard_map/ppermute | solution.py:23
  7.8 2.6 %collective-permute-start.6 = (bf16[4,32,1024]{2,1,0:T(8,128)(2,1)}, bf16[4,32,1024]{2,1,0:T(8,128)(2,1)S(1)}, u32[]{:S(2)}, u32[]{:S(2)}) collective-permute-start(bf16[4,32,1024]{2,1,0:T(8,128)(2,1)} %refs_0_.12), channel_id=1, source_target_pairs={{0,4},{1,5},{2,6},{3,7},{4,0},{5,1},{6,2},{7,3},{8,12},{9,13},{10,... | collective-permute-start | bytes 786440 | tf_op jit(solution)/shard_map/ppermute | solution.py:23
  10.4 0.7 %shard_map.57 = bf16[32,1536]{1,0:T(8,128)(2,1)S(1)} custom-call(s32[4,256]{1,0:T(4,128)S(1)} %copy-done.2, bf16[32,1536]{1,0:T(8,128)(2,1)S(1)} %shard_map.56.refs_1_, bf16[32,1536]{1,0:T(8,128)(2,1)S(1)} %collective-permute-done.1.refs_2_), custom_call_target="tpu_custom_call" | custom-call | flops 20000000000 | bytes 1000 | tf_op jit(solution)/shard_map/pallas_call | solution.py:312
  11.1 1.6 %collective-permute-start.2 = (bf16[32,1536]{1,0:T(8,128)(2,1)S(1)}, bf16[32,1536]{1,0:T(8,128)(2,1)S(1)}, u32[]{:S(2)}, u32[]{:S(2)}) collective-permute-start(bf16[32,1536]{1,0:T(8,128)(2,1)S(1)} %shard_map.57), channel_id=1, source_target_pairs={{0,16},{8,24},{16,0},{24,8},{1,17},{9,25},{17,1},{25,9},{2,18},{10... | collective-permute-start | bytes 294920 | tf_op jit(solution)/shard_map/ppermute | solution.py:23
  12.7 0.4 shard_map.55.refs_1_.refs_2_
  13.1 1.3 %collective-permute-start = (bf16[1024,512]{1,0:T(8,128)(2,1)S(1)}, bf16[1024,512]{1,0:T(8,128)(2,1)S(1)}, u32[]{:S(2)}, u32[]{:S(2)}) collective-permute-start(bf16[1024,512]{1,0:T(8,128)(2,1)S(1)} %shard_map.55.refs_1_.refs_2_), channel_id=1, source_target_pairs={{0,8},{8,0},{16,24},{24,16},{1,9},{9,1},{17,25},{25,17},{2,10},{10... | collective-permute-start | bytes 3145736 | tf_op jit(solution)/shard_map/ppermute | solution.py:23
  14.4 1.4 %collective-permute-done.2.refs_3_ = bf16[32,1536]{1,0:T(8,128)(2,1)S(1)} collective-permute-done((bf16[32,1536]{1,0:T(8,128)(2,1)S(1)}, bf16[32,1536]{1,0:T(8,128)(2,1)S(1)}, u32[]{:S(2)}, u32[]{:S(2)}) %collective-permute-start.2) | collective-permute-done | bytes 98336 | tf_op jit(solution)/shard_map/ppermute | solution.py:23
  15.8 4.5 %collective-permute-done.4.refs_2_ = bf16[4,32,1024]{2,1,0:T(8,128)(2,1)S(1)} collective-permute-done((bf16[4,32,1024]{2,1,0:T(8,128)(2,1)}, bf16[4,32,1024]{2,1,0:T(8,128)(2,1)S(1)}, u32[]{:S(2)}, u32[]{:S(2)}) %collective-permute-start.4) | collective-permute-done | bytes 262176 | tf_op jit(solution)/shard_map/ppermute | solution.py:23
  20.3 0.7 %shard_map.58.refs_8_ = bf16[32,1536]{1,0:T(8,128)(2,1)S(1)} custom-call(s32[4,256]{1,0:T(4,128)S(1)} %copy-done.2, bf16[32,1536]{1,0:T(8,128)(2,1)S(1)} %shard_map.56.refs_1_, bf16[32,1536]{1,0:T(8,128)(2,1)S(1)} %collective-permute-done.1.refs_2_, bf16[32,1536]{1,0:T(8,128)(2,1)S(1)} %collective-permute-done.2.refs_3_), custom_call_target="tpu_custom_call" | custom-call | flops 20000000000 | bytes 1000 | tf_op jit(solution)/shard_map/pallas_call | solution.py:312
  21.1 2.6 %collective-permute-start.14 = (bf16[32,1536]{1,0:T(8,128)(2,1)S(1)}, bf16[32,1536]{1,0:T(8,128)(2,1)S(1)}, u32[]{:S(2)}, u32[]{:S(2)}) collective-permute-start(bf16[32,1536]{1,0:T(8,128)(2,1)S(1)} %shard_map.58.refs_8_), channel_id=1, source_target_pairs={{0,6},{1,7},{2,4},{3,5},{4,2},{5,3},{6,0},{7,1},{8,14},{9,15},{10,... | collective-permute-start | bytes 294920 | tf_op jit(solution)/shard_map/ppermute | solution.py:23
  23.6 0.5 collective-permute-start.9
  24.2 3.9 %collective-permute-done.14.refs_14_ = bf16[32,1536]{1,0:T(8,128)(2,1)S(1)} collective-permute-done((bf16[32,1536]{1,0:T(8,128)(2,1)S(1)}, bf16[32,1536]{1,0:T(8,128)(2,1)S(1)}, u32[]{:S(2)}, u32[]{:S(2)}) %collective-permute-start.14) | collective-permute-done | bytes 98336 | tf_op jit(solution)/shard_map/ppermute | solution.py:23
  28.1 0.7 %collective-permute-start.17 = (bf16[4,32,1024]{2,1,0:T(8,128)(2,1)S(1)}, bf16[4,32,1024]{2,1,0:T(8,128)(2,1)S(1)}, u32[]{:S(2)}, u32[]{:S(2)}) collective-permute-start(bf16[4,32,1024]{2,1,0:T(8,128)(2,1)S(1)} %collective-permute-done.6.refs_4_), channel_id=1, source_target_pairs={{0,1},{1,0},{2,3},{3,2},{4,5},{5,4},{6,7},{7,6},{8,9},{9,8},{10,11... | collective-permute-start | bytes 786440 | tf_op jit(solution)/shard_map/ppermute | solution.py:23
  28.8 1.3 %collective-permute-start.15 = (bf16[32,1536]{1,0:T(8,128)(2,1)S(1)}, bf16[32,1536]{1,0:T(8,128)(2,1)S(1)}, u32[]{:S(2)}, u32[]{:S(2)}) collective-permute-start(bf16[32,1536]{1,0:T(8,128)(2,1)S(1)} %collective-permute-done.14.refs_14_), channel_id=1, source_target_pairs={{0,1},{1,0},{2,3},{3,2},{4,5},{5,4},{6,7},{7,6},{8,9},{9,8},{10,11... | collective-permute-start | bytes 294920 | tf_op jit(solution)/shard_map/ppermute | solution.py:23
  30.1 1.9 %shard_map.59 = bf16[512,512]{1,0:T(8,128)(2,1)S(1)} custom-call(s32[4,256]{1,0:T(4,128)S(1)} %copy-done.2, bf16[1024,512]{1,0:T(8,128)(2,1)S(1)} %shard_map.55.refs_1_.refs_2_, bf16[1024,512]{1,0:T(8,128)(2,1)S(1)} %collective-permute-done.refs_2_.refs_3_), custom_call_target="tpu_custom_call" | custom-call | flops 20000000000 | bytes 1000 | tf_op jit(solution)/shard_map/pallas_call | solution.py:312
  32.1 0.8 %collective-permute-start.13 = (bf16[32,1536]{1,0:T(8,128)(2,1)S(1)}, bf16[32,1536]{1,0:T(8,128)(2,1)S(1)}, u32[]{:S(2)}, u32[]{:S(2)}) collective-permute-start(bf16[32,1536]{1,0:T(8,128)(2,1)S(1)} %collective-permute-done.12.refs_12_), channel_id=1, source_target_pairs={{0,1},{1,0},{2,3},{3,2},{4,5},{5,4},{6,7},{7,6},{8,9},{9,8},{10,11... | collective-permute-start | bytes 294920 | tf_op jit(solution)/shard_map/ppermute | solution.py:23
  32.9 2.0 %collective-permute-start.11 = (bf16[32,1536]{1,0:T(8,128)(2,1)S(1)}, bf16[32,1536]{1,0:T(8,128)(2,1)S(1)}, u32[]{:S(2)}, u32[]{:S(2)}) collective-permute-start(bf16[32,1536]{1,0:T(8,128)(2,1)S(1)} %collective-permute-done.9.refs_9_), channel_id=1, source_target_pairs={{0,2},{1,3},{2,0},{3,1},{4,6},{5,7},{6,4},{7,5},{8,10},{9,11},{10,... | collective-permute-start | bytes 294920 | tf_op jit(solution)/shard_map/ppermute | solution.py:23
  34.9 2.2 %collective-permute-done.15.refs_15_ = bf16[32,1536]{1,0:T(8,128)(2,1)S(1)} collective-permute-done((bf16[32,1536]{1,0:T(8,128)(2,1)S(1)}, bf16[32,1536]{1,0:T(8,128)(2,1)S(1)}, u32[]{:S(2)}, u32[]{:S(2)}) %collective-permute-start.15) | collective-permute-done | bytes 98336 | tf_op jit(solution)/shard_map/ppermute | solution.py:23
  37.1 2.5 %collective-permute-start.7 = (bf16[4,32,1024]{2,1,0:T(8,128)(2,1)}, bf16[4,32,1024]{2,1,0:T(8,128)(2,1)S(1)}, u32[]{:S(2)}, u32[]{:S(2)}) collective-permute-start(bf16[4,32,1024]{2,1,0:T(8,128)(2,1)} %refs_0_.12), channel_id=1, source_target_pairs={{0,6},{1,7},{2,4},{3,5},{4,2},{5,3},{6,0},{7,1},{8,14},{9,15},{10,... | collective-permute-start | bytes 786440 | tf_op jit(solution)/shard_map/ppermute | solution.py:23
  39.6 1.5 %collective-permute-start.5 = (bf16[512,512]{1,0:T(8,128)(2,1)S(1)}, bf16[512,512]{1,0:T(8,128)(2,1)S(1)}, u32[]{:S(2)}, u32[]{:S(2)}) collective-permute-start(bf16[512,512]{1,0:T(8,128)(2,1)S(1)} %shard_map.59), channel_id=1, source_target_pairs={{0,16},{8,24},{16,0},{24,8},{1,17},{9,25},{17,1},{25,9},{2,18},{10... | collective-permute-start | bytes 1572872 | tf_op jit(solution)/shard_map/ppermute | solution.py:23
  41.2 1.2 %collective-permute-done.11.refs_11_ = bf16[32,1536]{1,0:T(8,128)(2,1)S(1)} collective-permute-done((bf16[32,1536]{1,0:T(8,128)(2,1)S(1)}, bf16[32,1536]{1,0:T(8,128)(2,1)S(1)}, u32[]{:S(2)}, u32[]{:S(2)}) %collective-permute-start.11) | collective-permute-done | bytes 98336 | tf_op jit(solution)/shard_map/ppermute | solution.py:23
  42.4 3.9 %collective-permute-done.10.refs_10_ = bf16[32,1536]{1,0:T(8,128)(2,1)S(1)} collective-permute-done((bf16[32,1536]{1,0:T(8,128)(2,1)S(1)}, bf16[32,1536]{1,0:T(8,128)(2,1)S(1)}, u32[]{:S(2)}, u32[]{:S(2)}) %collective-permute-start.10) | collective-permute-done | bytes 98336 | tf_op jit(solution)/shard_map/ppermute | solution.py:23
  46.5 2.7 %collective-permute-done.5.refs_4_ = bf16[512,512]{1,0:T(8,128)(2,1)S(1)} collective-permute-done((bf16[512,512]{1,0:T(8,128)(2,1)S(1)}, bf16[512,512]{1,0:T(8,128)(2,1)S(1)}, u32[]{:S(2)}, u32[]{:S(2)}) %collective-permute-start.5) | collective-permute-done | bytes 524320 | tf_op jit(solution)/shard_map/ppermute | solution.py:23
  49.1 1.4 %collective-permute-start.19 = (bf16[4,32,1024]{2,1,0:T(8,128)(2,1)S(1)}, bf16[4,32,1024]{2,1,0:T(8,128)(2,1)S(1)}, u32[]{:S(2)}, u32[]{:S(2)}) collective-permute-start(bf16[4,32,1024]{2,1,0:T(8,128)(2,1)S(1)} %collective-permute-done.7.refs_6_), channel_id=1, source_target_pairs={{0,1},{1,0},{2,3},{3,2},{4,5},{5,4},{6,7},{7,6},{8,9},{9,8},{10,11... | collective-permute-start | bytes 786440 | tf_op jit(solution)/shard_map/ppermute | solution.py:23
  50.5 0.5 collective-permute-done.8.refs_5_
  51.1 6.5 %shard_map.60 = (bf16[1024,512]{1,0:T(8,128)(2,1)S(1)}, bf16[1024,512]{1,0:T(8,128)(2,1)S(1)}, f32[8,1024]{1,0:T(8,128)S(1)}) custom-call(s32[4,8]{1,0:T(4,128)S(1)} %copy-done.4, s32[4,256]{1,0:T(4,128)S(1)} %copy-done.2, bf16[1024,512]{1,0:T(8,128)(2,1)S(1)} %shard_map.55.refs_1_.refs_2_, bf16[1024,512]{1,0:T(8,128)(2,1)S(1)} %collective-permute-done.refs_2_.refs_3_, ...), custom_call_target="tpu_custom_call" | custom-call | flops 20000000000 | bytes 1000 | tf_op jit(solution)/shard_map/pallas_call | solution.py:312
  57.9 4.1 %shard_map.61 = bf16[1024,512]{1,0:T(8,128)(2,1)} custom-call(bf16[1024,512]{1,0:T(8,128)(2,1)S(1)} %get-tuple-element.42.base, f32[8,1024]{1,0:T(8,128)S(1)} %get-tuple-element.43.weight, bf16[1024,512]{1,0:T(8,128)(2,1)S(1)} %get-tuple-element.44.mix, bf16[4,32,1024]{2,1,0:T(8,128)(2,1)} %refs_0_.12, ...), custom_call_target="tpu_custom_call" | custom-call | flops 20000000000 | bytes 1000 | tf_op jit(solution)/shard_map/pallas_call | solution.py:409
  (33 shorter events, 0.5 us)
Async XLA Ops:
  0.0 0.7 %copy-start.2 = (s32[4,256]{1,0:T(4,128)S(1)}, s32[4,256]{1,0:T(4,128)}, u32[]{:S(2)}) copy-start(s32[4,256]{1,0:T(4,128)} %refs_1_.5) | copy-start | bytes 12292
  0.7 0.7 %copy-start.3 = (s32[4,8]{1,0:T(4,128)S(1)}, s32[4,8]{1,0:T(4,128)}, u32[]{:S(2)}) copy-start(s32[4,8]{1,0:T(4,128)} %refs_0_.11) | copy-start | bytes 388
  3.2 9.6 %copy-start = (bf16[1024,512]{1,0:T(8,128)(2,1)S(1)}, bf16[1024,512]{1,0:T(8,128)(2,1)}, u32[]{:S(2)}) copy-start(bf16[1024,512]{1,0:T(8,128)(2,1)} %refs_6_.1) | copy-start | bytes 3145732
  3.2 7.3 %collective-permute-start.1 = (bf16[32,1536]{1,0:T(8,128)(2,1)S(1)}, bf16[32,1536]{1,0:T(8,128)(2,1)S(1)}, u32[]{:S(2)}, u32[]{:S(2)}) collective-permute-start(bf16[32,1536]{1,0:T(8,128)(2,1)S(1)} %shard_map.56.refs_1_), channel_id=1, source_target_pairs={{0,8},{8,0},{16,24},{24,16},{1,9},{9,1},{17,25},{25,17},{2,10},{10... | collective-permute-start | bytes 294920 | tf_op jit(solution)/shard_map/ppermute | solution.py:23
  3.7 12.2 %collective-permute-start.3 = (bf16[4,32,1024]{2,1,0:T(8,128)(2,1)}, bf16[4,32,1024]{2,1,0:T(8,128)(2,1)S(1)}, u32[]{:S(2)}, u32[]{:S(2)}) collective-permute-start(bf16[4,32,1024]{2,1,0:T(8,128)(2,1)} %refs_0_.12), channel_id=1, source_target_pairs={{0,1},{1,0},{2,3},{3,2},{4,5},{5,4},{6,7},{7,6},{8,9},{9,8},{10,11... | collective-permute-start | bytes 786440 | tf_op jit(solution)/shard_map/ppermute | solution.py:23
  6.2 14.1 %collective-permute-start.4 = (bf16[4,32,1024]{2,1,0:T(8,128)(2,1)}, bf16[4,32,1024]{2,1,0:T(8,128)(2,1)S(1)}, u32[]{:S(2)}, u32[]{:S(2)}) collective-permute-start(bf16[4,32,1024]{2,1,0:T(8,128)(2,1)} %refs_0_.12), channel_id=1, source_target_pairs={{0,2},{1,3},{2,0},{3,1},{4,6},{5,7},{6,4},{7,5},{8,10},{9,11},{10,... | collective-permute-start | bytes 786440 | tf_op jit(solution)/shard_map/ppermute | solution.py:23
  7.8 16.3 %collective-permute-start.6 = (bf16[4,32,1024]{2,1,0:T(8,128)(2,1)}, bf16[4,32,1024]{2,1,0:T(8,128)(2,1)S(1)}, u32[]{:S(2)}, u32[]{:S(2)}) collective-permute-start(bf16[4,32,1024]{2,1,0:T(8,128)(2,1)} %refs_0_.12), channel_id=1, source_target_pairs={{0,4},{1,5},{2,6},{3,7},{4,0},{5,1},{6,2},{7,3},{8,12},{9,13},{10,... | collective-permute-start | bytes 786440 | tf_op jit(solution)/shard_map/ppermute | solution.py:23
  11.1 4.7 %collective-permute-start.2 = (bf16[32,1536]{1,0:T(8,128)(2,1)S(1)}, bf16[32,1536]{1,0:T(8,128)(2,1)S(1)}, u32[]{:S(2)}, u32[]{:S(2)}) collective-permute-start(bf16[32,1536]{1,0:T(8,128)(2,1)S(1)} %shard_map.57), channel_id=1, source_target_pairs={{0,16},{8,24},{16,0},{24,8},{1,17},{9,25},{17,1},{25,9},{2,18},{10... | collective-permute-start | bytes 294920 | tf_op jit(solution)/shard_map/ppermute | solution.py:23
  13.1 17.0 %collective-permute-start = (bf16[1024,512]{1,0:T(8,128)(2,1)S(1)}, bf16[1024,512]{1,0:T(8,128)(2,1)S(1)}, u32[]{:S(2)}, u32[]{:S(2)}) collective-permute-start(bf16[1024,512]{1,0:T(8,128)(2,1)S(1)} %shard_map.55.refs_1_.refs_2_), channel_id=1, source_target_pairs={{0,8},{8,0},{16,24},{24,16},{1,9},{9,1},{17,25},{25,17},{2,10},{10... | collective-permute-start | bytes 3145736 | tf_op jit(solution)/shard_map/ppermute | solution.py:23
  21.1 7.1 %collective-permute-start.14 = (bf16[32,1536]{1,0:T(8,128)(2,1)S(1)}, bf16[32,1536]{1,0:T(8,128)(2,1)S(1)}, u32[]{:S(2)}, u32[]{:S(2)}) collective-permute-start(bf16[32,1536]{1,0:T(8,128)(2,1)S(1)} %shard_map.58.refs_8_), channel_id=1, source_target_pairs={{0,6},{1,7},{2,4},{3,5},{4,2},{5,3},{6,0},{7,1},{8,14},{9,15},{10,... | collective-permute-start | bytes 294920 | tf_op jit(solution)/shard_map/ppermute | solution.py:23
  23.6 5.2 %collective-permute-start.9 = (bf16[32,1536]{1,0:T(8,128)(2,1)S(1)}, bf16[32,1536]{1,0:T(8,128)(2,1)S(1)}, u32[]{:S(2)}, u32[]{:S(2)}) collective-permute-start(bf16[32,1536]{1,0:T(8,128)(2,1)S(1)} %shard_map.58.refs_8_), channel_id=1, source_target_pairs={{0,1},{1,0},{2,3},{3,2},{4,5},{5,4},{6,7},{7,6},{8,9},{9,8},{10,11... | collective-permute-start | bytes 294920 | tf_op jit(solution)/shard_map/ppermute | solution.py:23
  24.1 7.9 %collective-permute-start.12 = (bf16[32,1536]{1,0:T(8,128)(2,1)S(1)}, bf16[32,1536]{1,0:T(8,128)(2,1)S(1)}, u32[]{:S(2)}, u32[]{:S(2)}) collective-permute-start(bf16[32,1536]{1,0:T(8,128)(2,1)S(1)} %shard_map.58.refs_8_), channel_id=1, source_target_pairs={{0,4},{1,5},{2,6},{3,7},{4,0},{5,1},{6,2},{7,3},{8,12},{9,13},{10,... | collective-permute-start | bytes 294920 | tf_op jit(solution)/shard_map/ppermute | solution.py:23
  28.1 9.0 %collective-permute-start.17 = (bf16[4,32,1024]{2,1,0:T(8,128)(2,1)S(1)}, bf16[4,32,1024]{2,1,0:T(8,128)(2,1)S(1)}, u32[]{:S(2)}, u32[]{:S(2)}) collective-permute-start(bf16[4,32,1024]{2,1,0:T(8,128)(2,1)S(1)} %collective-permute-done.6.refs_4_), channel_id=1, source_target_pairs={{0,1},{1,0},{2,3},{3,2},{4,5},{5,4},{6,7},{7,6},{8,9},{9,8},{10,11... | collective-permute-start | bytes 786440 | tf_op jit(solution)/shard_map/ppermute | solution.py:23
  28.8 10.8 %collective-permute-start.16 = (bf16[4,32,1024]{2,1,0:T(8,128)(2,1)S(1)}, bf16[4,32,1024]{2,1,0:T(8,128)(2,1)S(1)}, u32[]{:S(2)}, u32[]{:S(2)}) collective-permute-start(bf16[4,32,1024]{2,1,0:T(8,128)(2,1)S(1)} %collective-permute-done.3.refs_1_), channel_id=1, source_target_pairs={{0,2},{1,3},{2,0},{3,1},{4,6},{5,7},{6,4},{7,5},{8,10},{9,11},{10,... | collective-permute-start | bytes 786440 | tf_op jit(solution)/shard_map/ppermute | solution.py:23
  28.8 8.3 %collective-permute-start.15 = (bf16[32,1536]{1,0:T(8,128)(2,1)S(1)}, bf16[32,1536]{1,0:T(8,128)(2,1)S(1)}, u32[]{:S(2)}, u32[]{:S(2)}) collective-permute-start(bf16[32,1536]{1,0:T(8,128)(2,1)S(1)} %collective-permute-done.14.refs_14_), channel_id=1, source_target_pairs={{0,1},{1,0},{2,3},{3,2},{4,5},{5,4},{6,7},{7,6},{8,9},{9,8},{10,11... | collective-permute-start | bytes 294920 | tf_op jit(solution)/shard_map/ppermute | solution.py:23
  32.1 9.1 %collective-permute-start.13 = (bf16[32,1536]{1,0:T(8,128)(2,1)S(1)}, bf16[32,1536]{1,0:T(8,128)(2,1)S(1)}, u32[]{:S(2)}, u32[]{:S(2)}) collective-permute-start(bf16[32,1536]{1,0:T(8,128)(2,1)S(1)} %collective-permute-done.12.refs_12_), channel_id=1, source_target_pairs={{0,1},{1,0},{2,3},{3,2},{4,5},{5,4},{6,7},{7,6},{8,9},{9,8},{10,11... | collective-permute-start | bytes 294920 | tf_op jit(solution)/shard_map/ppermute | solution.py:23
  32.9 9.5 %collective-permute-start.11 = (bf16[32,1536]{1,0:T(8,128)(2,1)S(1)}, bf16[32,1536]{1,0:T(8,128)(2,1)S(1)}, u32[]{:S(2)}, u32[]{:S(2)}) collective-permute-start(bf16[32,1536]{1,0:T(8,128)(2,1)S(1)} %collective-permute-done.9.refs_9_), channel_id=1, source_target_pairs={{0,2},{1,3},{2,0},{3,1},{4,6},{5,7},{6,4},{7,5},{8,10},{9,11},{10,... | collective-permute-start | bytes 294920 | tf_op jit(solution)/shard_map/ppermute | solution.py:23
  37.1 9.1 %collective-permute-start.10 = (bf16[32,1536]{1,0:T(8,128)(2,1)S(1)}, bf16[32,1536]{1,0:T(8,128)(2,1)S(1)}, u32[]{:S(2)}, u32[]{:S(2)}) collective-permute-start(bf16[32,1536]{1,0:T(8,128)(2,1)S(1)} %shard_map.58.refs_8_), channel_id=1, source_target_pairs={{0,2},{1,3},{2,0},{3,1},{4,6},{5,7},{6,4},{7,5},{8,10},{9,11},{10,... | collective-permute-start | bytes 294920 | tf_op jit(solution)/shard_map/ppermute | solution.py:23
  37.1 9.4 %collective-permute-start.7 = (bf16[4,32,1024]{2,1,0:T(8,128)(2,1)}, bf16[4,32,1024]{2,1,0:T(8,128)(2,1)S(1)}, u32[]{:S(2)}, u32[]{:S(2)}) collective-permute-start(bf16[4,32,1024]{2,1,0:T(8,128)(2,1)} %refs_0_.12), channel_id=1, source_target_pairs={{0,6},{1,7},{2,4},{3,5},{4,2},{5,3},{6,0},{7,1},{8,14},{9,15},{10,... | collective-permute-start | bytes 786440 | tf_op jit(solution)/shard_map/ppermute | solution.py:23
  39.6 9.5 %collective-permute-start.5 = (bf16[512,512]{1,0:T(8,128)(2,1)S(1)}, bf16[512,512]{1,0:T(8,128)(2,1)S(1)}, u32[]{:S(2)}, u32[]{:S(2)}) collective-permute-start(bf16[512,512]{1,0:T(8,128)(2,1)S(1)} %shard_map.59), channel_id=1, source_target_pairs={{0,16},{8,24},{16,0},{24,8},{1,17},{9,25},{17,1},{25,9},{2,18},{10... | collective-permute-start | bytes 1572872 | tf_op jit(solution)/shard_map/ppermute | solution.py:23
  46.3 4.8 %copy-start.1 = (bf16[4,256,256]{2,1,0:T(8,128)(2,1)S(1)}, bf16[4,256,256]{2,1,0:T(8,128)(2,1)}, u32[]{:S(2)}) copy-start(bf16[4,256,256]{2,1,0:T(8,128)(2,1)} %refs_7_.1) | copy-start | bytes 1572868
  46.3 4.7 %copy-start.4 = (s32[4,8]{1,0:T(4,128)S(1)}, s32[4,8]{1,0:T(4,128)}, u32[]{:S(2)}) copy-start(s32[4,8]{1,0:T(4,128)} %refs_0_.11) | copy-start | bytes 388
  46.4 4.1 %collective-permute-start.18 = (bf16[256,1536]{1,0:T(8,128)(2,1)S(1)}, bf16[256,1536]{1,0:T(8,128)(2,1)S(1)}, u32[]{:S(2)}, u32[]{:S(2)}) collective-permute-start(bf16[256,1536]{1,0:T(8,128)(2,1)S(1)} %constant_dynamic-update-slice_fusion), channel_id=1, source_target_pairs={{0,8},{8,0},{16,24},{24,16},{1,9},{9,1},{17,25},{25,17},{2,10},{10... | collective-permute-start | bytes 2359304 | tf_op jit(solution)/shard_map/ppermute | solution.py:23
  49.1 1.9 %collective-permute-start.8 = (bf16[512,512]{1,0:T(8,128)(2,1)S(1)}, bf16[512,512]{1,0:T(8,128)(2,1)S(1)}, u32[]{:S(2)}, u32[]{:S(2)}) collective-permute-start(bf16[512,512]{1,0:T(8,128)(2,1)S(1)} %collective-permute-done.5.refs_4_), channel_id=1, source_target_pairs={{0,8},{8,0},{16,24},{24,16},{1,9},{9,1},{17,25},{25,17},{2,10},{10... | collective-permute-start | bytes 1572872 | tf_op jit(solution)/shard_map/ppermute | solution.py:23
  49.1 8.7 %collective-permute-start.19 = (bf16[4,32,1024]{2,1,0:T(8,128)(2,1)S(1)}, bf16[4,32,1024]{2,1,0:T(8,128)(2,1)S(1)}, u32[]{:S(2)}, u32[]{:S(2)}) collective-permute-start(bf16[4,32,1024]{2,1,0:T(8,128)(2,1)S(1)} %collective-permute-done.7.refs_6_), channel_id=1, source_target_pairs={{0,1},{1,0},{2,3},{3,2},{4,5},{5,4},{6,7},{7,6},{8,9},{9,8},{10,11... | collective-permute-start | bytes 786440 | tf_op jit(solution)/shard_map/ppermute | solution.py:23

commit v4 on v3

--- a/solution.py
+++ b/solution.py
@@ -15,7 +15,7 @@
 W = 256
 VMEM = pl.BlockSpec(memory_space=pltpu.VMEM)
 SMEM = pl.BlockSpec(memory_space=pltpu.SMEM)
-COST = pl.CostEstimate(flops=20000000000, bytes_accessed=1000, transcendentals=0)
+COST = pl.CostEstimate(flops=1000, bytes_accessed=1000, transcendentals=0)
 FIRST, LOW, HIGH, IS_LOW, ROW, CORE, ME = range(7)
 
 
@@ -209,17 +209,33 @@
         out[i * half : (i + 1) * half, :] = jnp.where(scal[CORE] == 0, value[:half], value[half:]).astype(BF)
 
 
-def chain_kernel(tile, n_piece, split, scal, *refs):
-    fac, piv, own, other, came, rest, cur, inv = refs[:8]
-    special = refs[8 : 8 + n_piece]
-    refs = refs[8 + n_piece :]
-    other_special = None
-    if split:
-        other_special = refs[0]
-        refs = refs[1:]
-    mix_ref, base_ref, weight_ref, s_ref, u_ref = refs
+def prepare_kernel(tile, scal, exps, piv, cur, put_ref, base_ref, weight_ref):
     row_of, col_of = pivot_views(piv)
     row_dev, columns = cur.shape
+    top_block = scal[FIRST] == 0
+    for lo in range(0, row_dev, W):
+        ids = lax.broadcasted_iota(I32, (W, W), 0) + scal[FIRST] + lo
+        lane = lax.broadcasted_iota(I32, (W, W), 1) + scal[FIRST] + lo
+        taken = jnp.zeros((W, 1), I32)
+        alive = jnp.where(top_block, jnp.zeros((1, W), F32), jnp.ones((1, W), F32))
+        for k in reversed(STEPS):
+            same = (ids == row_of(k)).astype(I32) * (1 - taken)
+            put_ref[lo : lo + W, k * W : (k + 1) * W] = same.astype(F32).astype(BF)
+            taken = taken + jnp.sum(same, axis=1, keepdims=True)
+            weight_ref[k : k + 1, lo : lo + W] = scale_row(exps, k, lo, W, tile) * alive
+            if k:
+                hit = jnp.max((col_of(k) == lane).astype(F32), axis=0, keepdims=True)
+                alive = alive * (1.0 - hit)
+        base_ref[lo : lo + W, :] = jnp.where(taken > 0, 0.0, cur[lo : lo + W, :].astype(F32)).astype(BF)
+
+
+def chain_kernel(n_piece, split, n_side, scal, *refs):
+    piv, own, other, came, rest, put, start_rows, inv = refs[:8]
+    sides = refs[8 : 8 + n_side]
+    refs = refs[8 + n_side :]
+    mix_ref, base_ref, s_ref, u_ref = refs
+    row_of, col_of = pivot_views(piv)
+    row_dev, columns = start_rows.shape
     part = W // n_piece
     is_top = scal[ROW] == 0
     top_block = scal[FIRST] == 0
@@ -239,13 +255,21 @@
     table = matches(STEPS, row_of, col_of)
     chosen = rows_resolved(scal, STEPS, table, col_of, tops, picks)
 
+    def panel_rows(arrays, base):
+        if len(arrays) == 1:
+            return arrays[0][:, base : base + W]
+        line, cross = arrays
+        blocks = []
+        for z in range(n_piece // 2):
+            blocks += [line[z * part : (z + 1) * part, base : base + W], cross[z * part : (z + 1) * part, base : base + W]]
+        return jnp.concatenate(blocks, axis=0)
+
     def side_rows(pair, which):
         base = PAIRS.index(pair) * W
         if not split:
-            base = base + which * len(PAIRS) * W
-            return jnp.concatenate([p[:, base : base + W] for p in special], axis=0)
-        mine = jnp.concatenate([p[:, base : base + W] for p in special], axis=0)
-        theirs = other_special[:, base : base + W]
+            return panel_rows(sides, base + which * len(PAIRS) * W)
+        mine = panel_rows(sides[: n_side // 2], base)
+        theirs = panel_rows(sides[n_side // 2 :], base)
         mine_is = core0 if which == 0 else jnp.logical_not(core0)
         return jnp.where(mine_is, mine.astype(F32), theirs.astype(F32)).astype(BF)
 
@@ -264,31 +288,22 @@
             start = pl.multiple_of((scal[ME] ^ m) * part, part)
             mix_ref[k * W + m * part : k * W + (m + 1) * part, :] = s_ref[pl.ds(k * W + start, part), :]
 
-    for lo in range(0, row_dev, W):
-        ids = lax.broadcasted_iota(I32, (W, W), 0) + scal[FIRST] + lo
-        lane = lax.broadcasted_iota(I32, (W, W), 1) + scal[FIRST] + lo
-        taken = jnp.zeros((W, 1), I32)
-        placed = jnp.zeros((W, columns), F32)
-        alive = jnp.where(top_block, jnp.zeros((1, W), F32), jnp.ones((1, W), F32))
-        for k in reversed(STEPS):
-            same = (ids == row_of(k)).astype(I32) * (1 - taken)
-            placed = placed + dot(same.astype(F32).astype(BF), u_ref[k * W : (k + 1) * W, :])
-            taken = taken + jnp.sum(same, axis=1, keepdims=True)
-            weight_ref[k : k + 1, lo : lo + W] = scale_row(fac, k, lo, W, tile) * alive
-            if k:
-                hit = jnp.max((col_of(k) == lane).astype(F32), axis=0, keepdims=True)
-                alive = alive * (1.0 - hit)
-        value = jnp.where(taken > 0, placed, cur[lo : lo + W, :].astype(F32))
-        value = jnp.where(top_block, s_ref[lo : lo + W, :].astype(F32), value)
-        base_ref[lo : lo + W, :] = value.astype(BF)
+    @pl.when(top_block)
+    def _():
+        base_ref[...] = s_ref[...]
+
+    @pl.when(jnp.logical_not(top_block))
+    def _():
+        for lo in range(0, row_dev, W):
+            placed = dot(put[lo : lo + W, :], u_ref[...])
+            base_ref[lo : lo + W, :] = (start_rows[lo : lo + W, :].astype(F32) + placed).astype(BF)
 
 
 def update_kernel(n_piece, base, weight, mix, *refs):
     pieces, out = refs[:n_piece], refs[n_piece]
     acc = base[...].astype(F32)
     for k in STEPS:
-        block = jnp.concatenate([p[k] for p in pieces], axis=0).astype(F32)
-        block = (block * weight[k : k + 1, :]).astype(BF)
+        block = jnp.concatenate([p[k] for p in pieces], axis=0) * weight[k : k + 1, :].astype(BF)
         acc = acc - dot_tn(block, mix[k * W : (k + 1) * W, :])
     out[...] = acc.astype(BF)
 
@@ -364,7 +379,7 @@
             bz2 = swap(panels, "pcol", 8, 4)
             bx0 = swap(panels, "pcol", 8, 1)
             bz1 = swap(panels, "pcol", 8, 2)
-            sp_came = after(sp_came, bx0, bz1)
+            sp_came = after(sp_came, bx0)
             own = call(final_slices, where2, bf(part, load), 0, pivots, sp, sp_other, sp_came)
         else:
             own = call(final_slices, where2, bf(part, load), 0, pivots, sp, sp_other, sp_came)
@@ -379,31 +394,37 @@
             rows, other = psum_pair(rows, row)
             came = rest = rows[: row_dev // 2]
         held = pivots
+        put, start_rows, weight = call(
+            functools.partial(pass_first, prepare_kernel, tile),
+            where,
+            [bf(row_dev, row_dev), bf(row_dev, columns), jax.ShapeDtypeStruct((8, row_dev), F32)],
+            1,
+            exponents, after(pivots, message), matrix,
+        )
         if n_piece == 8:
-            sz2 = swap(own, "pcol", 8, 4)
+            sz2 = swap(after(own, message, bz1), "pcol", 8, 4)
             sz3 = swap(own, "pcol", 8, 6)
-            sx0 = swap(own, "pcol", 8, 1)
-            sz1 = swap(after(own, message), "pcol", 8, 2)
-            sz1x = swap(after(sx0, message), "pcol", 8, 2)
-            bz1x = swap(after(bx0, sx0), "pcol", 8, 2)
-            bz3 = swap(after(panels, bz2), "pcol", 8, 6)
-            sz2x = swap(after(sz2, bz2, message), "pcol", 8, 1)
-            sz3x = swap(sz3, "pcol", 8, 1)
+            sz1 = swap(own, "pcol", 8, 2)
+            bz3 = swap(after(panels, bz2, weight), "pcol", 8, 6)
+            line = jnp.concatenate([own, sz1, sz2, sz3], axis=0)
+            cross = swap(line, "pcol", 8, 1)
             bz2x = swap(after(bz2, sz3), "pcol", 8, 1)
             bz3x = swap(bz3, "pcol", 8, 1)
+            line_other = swap(line, "prow", 4, 1)
+            bz1x = swap(after(bx0, line_other), "pcol", 8, 2)
+            rest = swap(after(came, bz3, bz2x), "prow", 4, 1)
             bulk = [panels, bx0, bz1, bz1x, bz2, bz2x, bz3, bz3x]
-            special = [own, sx0, sz1, sz1x, sz2, sz2x, sz3, sz3x]
-            rest = swap(after(came, bz3), "prow", 4, 1)
-            special = list(after(tuple(special), bz1x, bz2x))
-        if split:
-            mine = jnp.concatenate(special, axis=0)
-            special = special + [swap(mine, "prow", 4, 1)]
-        mix, base, weight = call(
-            functools.partial(chain_kernel, tile, n_piece, split),
+            cross_other = swap(cross, "prow", 4, 1)
+            special = [line, cross, line_other, cross_other]
+            held = pivots
+        elif split:
+            special = special + [swap(special[0], "prow", 4, 1)]
+        mix, base = call(
+            functools.partial(chain_kernel, n_piece, split, len(special)),
             where2,
-            [bf(row_dev, columns), bf(row_dev, columns), jax.ShapeDtypeStruct((8, row_dev), F32)],
-            1,
-            exponents, held, rows, other, came, rest, matrix, inverses, *special,
+            [bf(row_dev, columns), bf(row_dev, columns)],
+            0,
+            held, rows, other, came, rest, put, start_rows, inverses, *special,
             scratch=[pltpu.VMEM((row_dev, columns), BF)] * 2,
         )
         return pl.pallas_call(

time: 62.3 us -> 59.1 us (0.949)
  waiting for transfers between devices: 20.6 us -> 15.7 us
  starting transfers between devices: 23.6 us -> 26.3 us
  Pallas kernels: 16.1 us -> 14.9 us
    ppermute x20 -> x18, waiting for transfers between devices: 20.6 us -> 15.7 us  [swap(): return lax.ppermute(value, axis, [(i, i ^ mask) for i in range(size)])]
    ppermute x20 -> x18, starting transfers between devices: 23.6 us -> 26.3 us  [swap(): return lax.ppermute(value, axis, [(i, i ^ mask) for i in range(size)])]
    pallas_call x1, Pallas kernels: 4.05 us -> 3.22 us  [on_device(): pl.pallas_call(functools.partial(update_kernel, n_piece), out_shape=bf(ro...]
    unnamed x17 -> x12, local copies, waits for them, and re-layouts: 1.45 us -> 1.93 us
    pallas_call x6 -> x7, Pallas kernels: 12.1 us -> 11.7 us  [call(): pl.pallas_call(body, out_shape=shapes, in_specs=[SMEM] * n_smem + [VMEM]...]
  transfers between devices with their start and end apart: 20 -> 18, of which waited for: 9 -> 6; matrix products, arithmetic and copies ran while one was open for 0% -> 0% of each run, Pallas kernels for 17% -> 20%
where the time goes in v4:
time: 59.1 us; the launch traced here: 58.9 us
  starting transfers between devices  26.3 us (45%)
  waiting for transfers between devices  15.7 us (27%)
  Pallas kernels  14.9 us (25%)
  local copies, waits for them, and re-layouts  1.93 us (3%)
    ppermute x18, starting transfers between devices, swap(): return lax.ppermute(value, axis, [(i, i ^ mask) for i in range(size)])  26.3 us
    ppermute x18, waiting for transfers between devices, swap(): return lax.ppermute(value, axis, [(i, i ^ mask) for i in range(size)])  15.7 us
    pallas_call x7, Pallas kernels, call(): pl.pallas_call(body, out_shape=shapes, in_specs=[SMEM] * n_smem + [VMEM]...  11.7 us
    pallas_call x1, Pallas kernels, on_device(): pl.pallas_call(functools.partial(update_kernel, n_piece), out_shape=bf(ro...  3.22 us
    unnamed x12, local copies, waits for them, and re-layouts  1.93 us
  transfers between devices with their start and end apart: 18, of which 6 were waited for; matrix products, arithmetic and copies ran while one was open for 0% of the time, Pallas kernels for 20%

profile of v4, /device:TPU:0, one launch (start us, length us, event | category | flops | bytes accessed | tf_op | source)
XLA Modules:
  0.0 58.9 jit_solution(7574810254743847771)
XLA Ops:
  0.0 1.2 %copy-done = bf16[1024,512]{1,0:T(8,128)(2,1)S(1)} copy-done((bf16[1024,512]{1,0:T(8,128)(2,1)S(1)}, bf16[1024,512]{1,0:T(8,128)(2,1)}, u32[]{:S(2)}) %copy-start) | copy-done | bytes 1048600
  1.2 0.7 %copy-done.4 = s32[4,256]{1,0:T(4,128)S(1)} copy-done((s32[4,256]{1,0:T(4,128)S(1)}, s32[4,256]{1,0:T(4,128)}, u32[]{:S(2)}) %copy-start.4) | copy-done | bytes 4120
  1.9 0.2 shard_map.55.refs_1_
  2.1 0.0 copy-start.1
  2.1 2.4 %collective-permute-start = (bf16[1024,512]{1,0:T(8,128)(2,1)S(1)}, bf16[1024,512]{1,0:T(8,128)(2,1)S(1)}, u32[]{:S(2)}, u32[]{:S(2)}) collective-permute-start(bf16[1024,512]{1,0:T(8,128)(2,1)S(1)} %shard_map.55.refs_1_), channel_id=1, source_target_pairs={{0,8},{8,0},{16,24},{24,16},{1,9},{9,1},{17,25},{25,17},{2,10},{10... | collective-permute-start | bytes 3145736 | tf_op jit(solution)/shard_map/ppermute | solution.py:23
  4.6 2.3 %collective-permute-start.3 = (bf16[4,32,1024]{2,1,0:T(8,128)(2,1)S(1)}, bf16[4,32,1024]{2,1,0:T(8,128)(2,1)S(1)}, u32[]{:S(2)}, u32[]{:S(2)}) collective-permute-start(bf16[4,32,1024]{2,1,0:T(8,128)(2,1)S(1)} %copy-done.2), channel_id=1, source_target_pairs={{0,1},{1,0},{2,3},{3,2},{4,5},{5,4},{6,7},{7,6},{8,9},{9,8},{10,11... | collective-permute-start | bytes 786440 | tf_op jit(solution)/shard_map/ppermute | solution.py:23
  6.9 1.6 %collective-permute-start.11 = (bf16[4,32,1024]{2,1,0:T(8,128)(2,1)S(1)}, bf16[4,32,1024]{2,1,0:T(8,128)(2,1)S(1)}, u32[]{:S(2)}, u32[]{:S(2)}) collective-permute-start(bf16[4,32,1024]{2,1,0:T(8,128)(2,1)S(1)} %copy-done.2), channel_id=1, source_target_pairs={{0,2},{1,3},{2,0},{3,1},{4,6},{5,7},{6,4},{7,5},{8,10},{9,11},{10,... | collective-permute-start | bytes 786440 | tf_op jit(solution)/shard_map/ppermute | solution.py:23
  8.5 1.4 %shard_map.56.refs_1_ = bf16[32,1536]{1,0:T(8,128)(2,1)S(1)} custom-call(s32[4,8]{1,0:T(4,128)S(1)} %copy-done.5, s32[4,256]{1,0:T(4,128)S(1)} %copy-done.4, bf16[4,32,1024]{2,1,0:T(8,128)(2,1)S(1)} %copy-done.2), custom_call_target="tpu_custom_call" | custom-call | flops 1000 | bytes 1000 | tf_op jit(solution)/shard_map/pallas_call | solution.py:327
  9.9 0.1 collective-permute-start.1
  9.9 2.6 %collective-permute-start.5 = (bf16[4,32,1024]{2,1,0:T(8,128)(2,1)S(1)}, bf16[4,32,1024]{2,1,0:T(8,128)(2,1)S(1)}, u32[]{:S(2)}, u32[]{:S(2)}) collective-permute-start(bf16[4,32,1024]{2,1,0:T(8,128)(2,1)S(1)} %copy-done.2), channel_id=1, source_target_pairs={{0,4},{1,5},{2,6},{3,7},{4,0},{5,1},{6,2},{7,3},{8,12},{9,13},{10,... | collective-permute-start | bytes 786440 | tf_op jit(solution)/shard_map/ppermute | solution.py:23
  12.6 0.7 %shard_map.57 = bf16[32,1536]{1,0:T(8,128)(2,1)S(1)} custom-call(s32[4,256]{1,0:T(4,128)S(1)} %copy-done.4, bf16[32,1536]{1,0:T(8,128)(2,1)S(1)} %shard_map.56.refs_1_, bf16[32,1536]{1,0:T(8,128)(2,1)S(1)} %collective-permute-done.1.refs_2_), custom_call_target="tpu_custom_call" | custom-call | flops 1000 | bytes 1000 | tf_op jit(solution)/shard_map/pallas_call | solution.py:327
  13.3 1.8 %collective-permute-start.2 = (bf16[32,1536]{1,0:T(8,128)(2,1)S(1)}, bf16[32,1536]{1,0:T(8,128)(2,1)S(1)}, u32[]{:S(2)}, u32[]{:S(2)}) collective-permute-start(bf16[32,1536]{1,0:T(8,128)(2,1)S(1)} %shard_map.57), channel_id=1, source_target_pairs={{0,16},{8,24},{16,0},{24,8},{1,17},{9,25},{17,1},{25,9},{2,18},{10... | collective-permute-start | bytes 294920 | tf_op jit(solution)/shard_map/ppermute | solution.py:23
  15.2 3.1 %collective-permute-done.2.refs_3_ = bf16[32,1536]{1,0:T(8,128)(2,1)S(1)} collective-permute-done((bf16[32,1536]{1,0:T(8,128)(2,1)S(1)}, bf16[32,1536]{1,0:T(8,128)(2,1)S(1)}, u32[]{:S(2)}, u32[]{:S(2)}) %collective-permute-start.2) | collective-permute-done | bytes 98336 | tf_op jit(solution)/shard_map/ppermute | solution.py:23
  18.3 0.7 %shard_map.58 = bf16[32,1536]{1,0:T(8,128)(2,1)S(1)} custom-call(s32[4,256]{1,0:T(4,128)S(1)} %copy-done.4, bf16[32,1536]{1,0:T(8,128)(2,1)S(1)} %shard_map.56.refs_1_, bf16[32,1536]{1,0:T(8,128)(2,1)S(1)} %collective-permute-done.1.refs_2_, bf16[32,1536]{1,0:T(8,128)(2,1)S(1)} %collective-permute-done.2.refs_3_), custom_call_target="tpu_custom_call" | custom-call | flops 1000 | bytes 1000 | tf_op jit(solution)/shard_map/pallas_call | solution.py:327
  19.0 1.2 %collective-permute-start.7 = (bf16[32,1536]{1,0:T(8,128)(2,1)S(1)}, bf16[32,1536]{1,0:T(8,128)(2,1)S(1)}, u32[]{:S(2)}, u32[]{:S(2)}) collective-permute-start(bf16[32,1536]{1,0:T(8,128)(2,1)S(1)} %shard_map.58), channel_id=1, source_target_pairs={{0,6},{1,7},{2,4},{3,5},{4,2},{5,3},{6,0},{7,1},{8,14},{9,15},{10,... | collective-permute-start | bytes 294920 | tf_op jit(solution)/shard_map/ppermute | solution.py:23
  20.2 0.7 %collective-permute-start.10 = (bf16[32,1536]{1,0:T(8,128)(2,1)S(1)}, bf16[32,1536]{1,0:T(8,128)(2,1)S(1)}, u32[]{:S(2)}, u32[]{:S(2)}) collective-permute-start(bf16[32,1536]{1,0:T(8,128)(2,1)S(1)} %shard_map.58), channel_id=1, source_target_pairs={{0,2},{1,3},{2,0},{3,1},{4,6},{5,7},{6,4},{7,5},{8,10},{9,11},{10,... | collective-permute-start | bytes 294920 | tf_op jit(solution)/shard_map/ppermute | solution.py:23
  20.9 1.9 %shard_map.59 = bf16[512,512]{1,0:T(8,128)(2,1)S(1)} custom-call(s32[4,256]{1,0:T(4,128)S(1)} %copy-done.4, bf16[1024,512]{1,0:T(8,128)(2,1)S(1)} %shard_map.55.refs_1_, bf16[1024,512]{1,0:T(8,128)(2,1)S(1)} %collective-permute-done.refs_2_), custom_call_target="tpu_custom_call" | custom-call | flops 1000 | bytes 1000 | tf_op jit(solution)/shard_map/pallas_call | solution.py:327
  22.8 2.7 %collective-permute-start.12 = (bf16[32,1536]{1,0:T(8,128)(2,1)S(1)}, bf16[32,1536]{1,0:T(8,128)(2,1)S(1)}, u32[]{:S(2)}, u32[]{:S(2)}) collective-permute-start(bf16[32,1536]{1,0:T(8,128)(2,1)S(1)} %shard_map.58), channel_id=1, source_target_pairs={{0,4},{1,5},{2,6},{3,7},{4,0},{5,1},{6,2},{7,3},{8,12},{9,13},{10,... | collective-permute-start | bytes 294920 | tf_op jit(solution)/shard_map/ppermute | solution.py:23
  25.5 1.7 %collective-permute-start.4 = (bf16[512,512]{1,0:T(8,128)(2,1)S(1)}, bf16[512,512]{1,0:T(8,128)(2,1)S(1)}, u32[]{:S(2)}, u32[]{:S(2)}) collective-permute-start(bf16[512,512]{1,0:T(8,128)(2,1)S(1)} %shard_map.59), channel_id=1, source_target_pairs={{0,16},{8,24},{16,0},{24,8},{1,17},{9,25},{17,1},{25,9},{2,18},{10... | collective-permute-start | bytes 1572872 | tf_op jit(solution)/shard_map/ppermute | solution.py:23
  27.2 2.7 %collective-permute-done.5.refs_4_ = bf16[4,32,1024]{2,1,0:T(8,128)(2,1)S(1)} collective-permute-done((bf16[4,32,1024]{2,1,0:T(8,128)(2,1)S(1)}, bf16[4,32,1024]{2,1,0:T(8,128)(2,1)S(1)}, u32[]{:S(2)}, u32[]{:S(2)}) %collective-permute-start.5) | collective-permute-done | bytes 262176 | tf_op jit(solution)/shard_map/ppermute | solution.py:23
  29.9 0.5 collective-permute-start.8
  30.5 2.8 %shard_map.60 = (bf16[1024,1024]{1,0:T(8,128)(2,1)S(1)}, bf16[1024,512]{1,0:T(8,128)(2,1)S(1)}, f32[8,1024]{1,0:T(8,128)S(1)}) custom-call(s32[4,8]{1,0:T(4,128)S(1)} %copy-done.5, s32[4,256]{1,0:T(4,128)S(1)} %copy-done.4, bf16[1024,512]{1,0:T(8,128)(2,1)S(1)} %copy-done.1), custom_call_target="tpu_custom_call" | custom-call | flops 1000 | bytes 1000 | tf_op jit(solution)/shard_map/pallas_call | solution.py:327
  33.2 2.5 %collective-permute-start.6 = (bf16[4,32,1024]{2,1,0:T(8,128)(2,1)S(1)}, bf16[4,32,1024]{2,1,0:T(8,128)(2,1)S(1)}, u32[]{:S(2)}, u32[]{:S(2)}) collective-permute-start(bf16[4,32,1024]{2,1,0:T(8,128)(2,1)S(1)} %copy-done.2), channel_id=1, source_target_pairs={{0,6},{1,7},{2,4},{3,5},{4,2},{5,3},{6,0},{7,1},{8,14},{9,15},{10,... | collective-permute-start | bytes 786440 | tf_op jit(solution)/shard_map/ppermute | solution.py:23
  35.8 1.6 %collective-permute-start.13 = (bf16[128,1536]{1,0:T(8,128)(2,1)S(1)}, bf16[128,1536]{1,0:T(8,128)(2,1)S(1)}, u32[]{:S(2)}, u32[]{:S(2)}) collective-permute-start(bf16[128,1536]{1,0:T(8,128)(2,1)S(1)} %pad_maximum_fusion.refs_8_), channel_id=1, source_target_pairs={{0,1},{1,0},{2,3},{3,2},{4,5},{5,4},{6,7},{7,6},{8,9},{9,8},{10,11... | collective-permute-start | bytes 1179656 | tf_op jit(solution)/shard_map/ppermute | solution.py:23
  37.4 4.1 %collective-permute-done.6.refs_6_ = bf16[4,32,1024]{2,1,0:T(8,128)(2,1)S(1)} collective-permute-done((bf16[4,32,1024]{2,1,0:T(8,128)(2,1)S(1)}, bf16[4,32,1024]{2,1,0:T(8,128)(2,1)S(1)}, u32[]{:S(2)}, u32[]{:S(2)}) %collective-permute-start.6) | collective-permute-done | bytes 262176 | tf_op jit(solution)/shard_map/ppermute | solution.py:23
  41.5 3.2 %collective-permute-done.13.refs_9_ = bf16[128,1536]{1,0:T(8,128)(2,1)S(1)} collective-permute-done((bf16[128,1536]{1,0:T(8,128)(2,1)S(1)}, bf16[128,1536]{1,0:T(8,128)(2,1)S(1)}, u32[]{:S(2)}, u32[]{:S(2)}) %collective-permute-start.13) | collective-permute-done | bytes 393248 | tf_op jit(solution)/shard_map/ppermute | solution.py:23
  44.7 1.3 %collective-permute-start.17 = (bf16[4,32,1024]{2,1,0:T(8,128)(2,1)S(1)}, bf16[4,32,1024]{2,1,0:T(8,128)(2,1)S(1)}, u32[]{:S(2)}, u32[]{:S(2)}) collective-permute-start(bf16[4,32,1024]{2,1,0:T(8,128)(2,1)S(1)} %collective-permute-done.6.refs_6_), channel_id=1, source_target_pairs={{0,1},{1,0},{2,3},{3,2},{4,5},{5,4},{6,7},{7,6},{8,9},{9,8},{10,11... | collective-permute-start | bytes 786440 | tf_op jit(solution)/shard_map/ppermute | solution.py:23
  46.0 3.2 %collective-permute-start.16 = (bf16[4,32,1024]{2,1,0:T(8,128)(2,1)S(1)}, bf16[4,32,1024]{2,1,0:T(8,128)(2,1)S(1)}, u32[]{:S(2)}, u32[]{:S(2)}) collective-permute-start(bf16[4,32,1024]{2,1,0:T(8,128)(2,1)S(1)} %collective-permute-done.3.refs_1_), channel_id=1, source_target_pairs={{0,2},{1,3},{2,0},{3,1},{4,6},{5,7},{6,4},{7,5},{8,10},{9,11},{10,... | collective-permute-start | bytes 786440 | tf_op jit(solution)/shard_map/ppermute | solution.py:23
  49.2 3.9 %shard_map.61 = (bf16[1024,512]{1,0:T(8,128)(2,1)S(1)}, bf16[1024,512]{1,0:T(8,128)(2,1)S(1)}) custom-call(s32[4,256]{1,0:T(4,128)S(1)} %copy-done.4, bf16[1024,512]{1,0:T(8,128)(2,1)S(1)} %shard_map.55.refs_1_, bf16[1024,512]{1,0:T(8,128)(2,1)S(1)} %collective-permute-done.refs_2_, bf16[512,512]{1,0:T(8,128)(2,1)S(1)} %collective-permute-done.4.refs_3_, ...), custom_call_target="tpu_custom_call" | custom-call | flops 1000 | bytes 1000 | tf_op jit(solution)/shard_map/pallas_call | solution.py:327
  53.2 0.3 collective-permute-done.17.refs_7_
  53.5 2.2 %collective-permute-done.16.refs_3_ = bf16[4,32,1024]{2,1,0:T(8,128)(2,1)S(1)} collective-permute-done((bf16[4,32,1024]{2,1,0:T(8,128)(2,1)S(1)}, bf16[4,32,1024]{2,1,0:T(8,128)(2,1)S(1)}, u32[]{:S(2)}, u32[]{:S(2)}) %collective-permute-start.16) | collective-permute-done | bytes 262176 | tf_op jit(solution)/shard_map/ppermute | solution.py:23
  55.7 3.2 %shard_map.62 = bf16[1024,512]{1,0:T(8,128)(2,1)} custom-call(bf16[1024,512]{1,0:T(8,128)(2,1)S(1)} %get-tuple-element.28.base, f32[8,1024]{1,0:T(8,128)S(1)} %get-tuple-element.21.weight, bf16[1024,512]{1,0:T(8,128)(2,1)S(1)} %get-tuple-element.29.mix, bf16[4,32,1024]{2,1,0:T(8,128)(2,1)S(1)} %copy-done.2, ...), custom_call_target="tpu_custom_call" | custom-call | flops 1000 | bytes 1000 | tf_op jit(solution)/shard_map/pallas_call | solution.py:430
  (25 shorter events, 0.1 us)
Async XLA Ops:
  0.0 1.2 %copy-start = (bf16[1024,512]{1,0:T(8,128)(2,1)S(1)}, bf16[1024,512]{1,0:T(8,128)(2,1)}, u32[]{:S(2)}) copy-start(bf16[1024,512]{1,0:T(8,128)(2,1)} %refs_2_.3) | copy-start | bytes 3145732
  1.2 0.7 %copy-start.4 = (s32[4,256]{1,0:T(4,128)S(1)}, s32[4,256]{1,0:T(4,128)}, u32[]{:S(2)}) copy-start(s32[4,256]{1,0:T(4,128)} %refs_0_.13) | copy-start | bytes 12292
  1.9 2.6 %copy-start.2 = (bf16[4,32,1024]{2,1,0:T(8,128)(2,1)S(1)}, bf16[4,32,1024]{2,1,0:T(8,128)(2,1)}, u32[]{:S(2)}) copy-start(bf16[4,32,1024]{2,1,0:T(8,128)(2,1)} %refs_0_.14) | copy-start | bytes 786436
  1.9 6.6 %copy-start.5 = (s32[4,8]{1,0:T(4,128)S(1)}, s32[4,8]{1,0:T(4,128)}, u32[]{:S(2)}) copy-start(s32[4,8]{1,0:T(4,128)} %refs_0_.12) | copy-start | bytes 388
  2.1 28.3 %copy-start.1 = (bf16[1024,512]{1,0:T(8,128)(2,1)S(1)}, bf16[1024,512]{1,0:T(8,128)(2,1)}, u32[]{:S(2)}) copy-start(bf16[1024,512]{1,0:T(8,128)(2,1)} %refs_2_.3) | copy-start | bytes 3145732
  2.1 18.7 %collective-permute-start = (bf16[1024,512]{1,0:T(8,128)(2,1)S(1)}, bf16[1024,512]{1,0:T(8,128)(2,1)S(1)}, u32[]{:S(2)}, u32[]{:S(2)}) collective-permute-start(bf16[1024,512]{1,0:T(8,128)(2,1)S(1)} %shard_map.55.refs_1_), channel_id=1, source_target_pairs={{0,8},{8,0},{16,24},{24,16},{1,9},{9,1},{17,25},{25,17},{2,10},{10... | collective-permute-start | bytes 3145736 | tf_op jit(solution)/shard_map/ppermute | solution.py:23
  4.6 13.7 %collective-permute-start.3 = (bf16[4,32,1024]{2,1,0:T(8,128)(2,1)S(1)}, bf16[4,32,1024]{2,1,0:T(8,128)(2,1)S(1)}, u32[]{:S(2)}, u32[]{:S(2)}) collective-permute-start(bf16[4,32,1024]{2,1,0:T(8,128)(2,1)S(1)} %copy-done.2), channel_id=1, source_target_pairs={{0,1},{1,0},{2,3},{3,2},{4,5},{5,4},{6,7},{7,6},{8,9},{9,8},{10,11... | collective-permute-start | bytes 786440 | tf_op jit(solution)/shard_map/ppermute | solution.py:23
  6.9 15.9 %collective-permute-start.11 = (bf16[4,32,1024]{2,1,0:T(8,128)(2,1)S(1)}, bf16[4,32,1024]{2,1,0:T(8,128)(2,1)S(1)}, u32[]{:S(2)}, u32[]{:S(2)}) collective-permute-start(bf16[4,32,1024]{2,1,0:T(8,128)(2,1)S(1)} %copy-done.2), channel_id=1, source_target_pairs={{0,2},{1,3},{2,0},{3,1},{4,6},{5,7},{6,4},{7,5},{8,10},{9,11},{10,... | collective-permute-start | bytes 786440 | tf_op jit(solution)/shard_map/ppermute | solution.py:23
  9.9 2.7 %collective-permute-start.1 = (bf16[32,1536]{1,0:T(8,128)(2,1)S(1)}, bf16[32,1536]{1,0:T(8,128)(2,1)S(1)}, u32[]{:S(2)}, u32[]{:S(2)}) collective-permute-start(bf16[32,1536]{1,0:T(8,128)(2,1)S(1)} %shard_map.56.refs_1_), channel_id=1, source_target_pairs={{0,8},{8,0},{16,24},{24,16},{1,9},{9,1},{17,25},{25,17},{2,10},{10... | collective-permute-start | bytes 294920 | tf_op jit(solution)/shard_map/ppermute | solution.py:23
  9.9 20.0 %collective-permute-start.5 = (bf16[4,32,1024]{2,1,0:T(8,128)(2,1)S(1)}, bf16[4,32,1024]{2,1,0:T(8,128)(2,1)S(1)}, u32[]{:S(2)}, u32[]{:S(2)}) collective-permute-start(bf16[4,32,1024]{2,1,0:T(8,128)(2,1)S(1)} %copy-done.2), channel_id=1, source_target_pairs={{0,4},{1,5},{2,6},{3,7},{4,0},{5,1},{6,2},{7,3},{8,12},{9,13},{10,... | collective-permute-start | bytes 786440 | tf_op jit(solution)/shard_map/ppermute | solution.py:23
  13.3 5.0 %collective-permute-start.2 = (bf16[32,1536]{1,0:T(8,128)(2,1)S(1)}, bf16[32,1536]{1,0:T(8,128)(2,1)S(1)}, u32[]{:S(2)}, u32[]{:S(2)}) collective-permute-start(bf16[32,1536]{1,0:T(8,128)(2,1)S(1)} %shard_map.57), channel_id=1, source_target_pairs={{0,16},{8,24},{16,0},{24,8},{1,17},{9,25},{17,1},{25,9},{2,18},{10... | collective-permute-start | bytes 294920 | tf_op jit(solution)/shard_map/ppermute | solution.py:23
  19.0 30.2 %copy-start.3 = (bf16[4,256,256]{2,1,0:T(8,128)(2,1)S(1)}, bf16[4,256,256]{2,1,0:T(8,128)(2,1)}, u32[]{:S(2)}) copy-start(bf16[4,256,256]{2,1,0:T(8,128)(2,1)} %refs_7_.1) | copy-start | bytes 1572868
  19.0 10.9 %collective-permute-start.7 = (bf16[32,1536]{1,0:T(8,128)(2,1)S(1)}, bf16[32,1536]{1,0:T(8,128)(2,1)S(1)}, u32[]{:S(2)}, u32[]{:S(2)}) collective-permute-start(bf16[32,1536]{1,0:T(8,128)(2,1)S(1)} %shard_map.58), channel_id=1, source_target_pairs={{0,6},{1,7},{2,4},{3,5},{4,2},{5,3},{6,0},{7,1},{8,14},{9,15},{10,... | collective-permute-start | bytes 294920 | tf_op jit(solution)/shard_map/ppermute | solution.py:23
  20.2 15.6 %collective-permute-start.10 = (bf16[32,1536]{1,0:T(8,128)(2,1)S(1)}, bf16[32,1536]{1,0:T(8,128)(2,1)S(1)}, u32[]{:S(2)}, u32[]{:S(2)}) collective-permute-start(bf16[32,1536]{1,0:T(8,128)(2,1)S(1)} %shard_map.58), channel_id=1, source_target_pairs={{0,2},{1,3},{2,0},{3,1},{4,6},{5,7},{6,4},{7,5},{8,10},{9,11},{10,... | collective-permute-start | bytes 294920 | tf_op jit(solution)/shard_map/ppermute | solution.py:23
  22.8 13.0 %collective-permute-start.12 = (bf16[32,1536]{1,0:T(8,128)(2,1)S(1)}, bf16[32,1536]{1,0:T(8,128)(2,1)S(1)}, u32[]{:S(2)}, u32[]{:S(2)}) collective-permute-start(bf16[32,1536]{1,0:T(8,128)(2,1)S(1)} %shard_map.58), channel_id=1, source_target_pairs={{0,4},{1,5},{2,6},{3,7},{4,0},{5,1},{6,2},{7,3},{8,12},{9,13},{10,... | collective-permute-start | bytes 294920 | tf_op jit(solution)/shard_map/ppermute | solution.py:23
  25.5 16.0 %collective-permute-start.4 = (bf16[512,512]{1,0:T(8,128)(2,1)S(1)}, bf16[512,512]{1,0:T(8,128)(2,1)S(1)}, u32[]{:S(2)}, u32[]{:S(2)}) collective-permute-start(bf16[512,512]{1,0:T(8,128)(2,1)S(1)} %shard_map.59), channel_id=1, source_target_pairs={{0,16},{8,24},{16,0},{24,8},{1,17},{9,25},{17,1},{25,9},{2,18},{10... | collective-permute-start | bytes 1572872 | tf_op jit(solution)/shard_map/ppermute | solution.py:23
  29.9 7.5 %collective-permute-start.8 = (bf16[4,32,1024]{2,1,0:T(8,128)(2,1)S(1)}, bf16[4,32,1024]{2,1,0:T(8,128)(2,1)S(1)}, u32[]{:S(2)}, u32[]{:S(2)}) collective-permute-start(bf16[4,32,1024]{2,1,0:T(8,128)(2,1)S(1)} %collective-permute-done.5.refs_4_), channel_id=1, source_target_pairs={{0,1},{1,0},{2,3},{3,2},{4,5},{5,4},{6,7},{7,6},{8,9},{9,8},{10,11... | collective-permute-start | bytes 786440 | tf_op jit(solution)/shard_map/ppermute | solution.py:23
  33.2 8.3 %collective-permute-start.6 = (bf16[4,32,1024]{2,1,0:T(8,128)(2,1)S(1)}, bf16[4,32,1024]{2,1,0:T(8,128)(2,1)S(1)}, u32[]{:S(2)}, u32[]{:S(2)}) collective-permute-start(bf16[4,32,1024]{2,1,0:T(8,128)(2,1)S(1)} %copy-done.2), channel_id=1, source_target_pairs={{0,6},{1,7},{2,4},{3,5},{4,2},{5,3},{6,0},{7,1},{8,14},{9,15},{10,... | collective-permute-start | bytes 786440 | tf_op jit(solution)/shard_map/ppermute | solution.py:23
  35.8 8.9 %collective-permute-start.13 = (bf16[128,1536]{1,0:T(8,128)(2,1)S(1)}, bf16[128,1536]{1,0:T(8,128)(2,1)S(1)}, u32[]{:S(2)}, u32[]{:S(2)}) collective-permute-start(bf16[128,1536]{1,0:T(8,128)(2,1)S(1)} %pad_maximum_fusion.refs_8_), channel_id=1, source_target_pairs={{0,1},{1,0},{2,3},{3,2},{4,5},{5,4},{6,7},{7,6},{8,9},{9,8},{10,11... | collective-permute-start | bytes 1179656 | tf_op jit(solution)/shard_map/ppermute | solution.py:23
  37.4 8.6 %collective-permute-start.14 = (bf16[128,1536]{1,0:T(8,128)(2,1)S(1)}, bf16[128,1536]{1,0:T(8,128)(2,1)S(1)}, u32[]{:S(2)}, u32[]{:S(2)}) collective-permute-start(bf16[128,1536]{1,0:T(8,128)(2,1)S(1)} %pad_maximum_fusion.refs_8_), channel_id=1, source_target_pairs={{0,8},{8,0},{16,24},{24,16},{1,9},{9,1},{17,25},{25,17},{2,10},{10... | collective-permute-start | bytes 1179656 | tf_op jit(solution)/shard_map/ppermute | solution.py:23
  41.5 7.7 %collective-permute-start.9 = (bf16[512,512]{1,0:T(8,128)(2,1)S(1)}, bf16[512,512]{1,0:T(8,128)(2,1)S(1)}, u32[]{:S(2)}, u32[]{:S(2)}) collective-permute-start(bf16[512,512]{1,0:T(8,128)(2,1)S(1)} %collective-permute-done.4.refs_3_), channel_id=1, source_target_pairs={{0,8},{8,0},{16,24},{24,16},{1,9},{9,1},{17,25},{25,17},{2,10},{10... | collective-permute-start | bytes 1572872 | tf_op jit(solution)/shard_map/ppermute | solution.py:23
  44.7 4.5 %collective-permute-start.15 = (bf16[128,1536]{1,0:T(8,128)(2,1)S(1)}, bf16[128,1536]{1,0:T(8,128)(2,1)S(1)}, u32[]{:S(2)}, u32[]{:S(2)}) collective-permute-start(bf16[128,1536]{1,0:T(8,128)(2,1)S(1)} %collective-permute-done.13.refs_9_), channel_id=1, source_target_pairs={{0,8},{8,0},{16,24},{24,16},{1,9},{9,1},{17,25},{25,17},{2,10},{10... | collective-permute-start | bytes 1179656 | tf_op jit(solution)/shard_map/ppermute | solution.py:23
  44.7 8.7 %collective-permute-start.17 = (bf16[4,32,1024]{2,1,0:T(8,128)(2,1)S(1)}, bf16[4,32,1024]{2,1,0:T(8,128)(2,1)S(1)}, u32[]{:S(2)}, u32[]{:S(2)}) collective-permute-start(bf16[4,32,1024]{2,1,0:T(8,128)(2,1)S(1)} %collective-permute-done.6.refs_6_), channel_id=1, source_target_pairs={{0,1},{1,0},{2,3},{3,2},{4,5},{5,4},{6,7},{7,6},{8,9},{9,8},{10,11... | collective-permute-start | bytes 786440 | tf_op jit(solution)/shard_map/ppermute | solution.py:23
  46.0 9.7 %collective-permute-start.16 = (bf16[4,32,1024]{2,1,0:T(8,128)(2,1)S(1)}, bf16[4,32,1024]{2,1,0:T(8,128)(2,1)S(1)}, u32[]{:S(2)}, u32[]{:S(2)}) collective-permute-start(bf16[4,32,1024]{2,1,0:T(8,128)(2,1)S(1)} %collective-permute-done.3.refs_1_), channel_id=1, source_target_pairs={{0,2},{1,3},{2,0},{3,1},{4,6},{5,7},{6,4},{7,5},{8,10},{9,11},{10,... | collective-permute-start | bytes 786440 | tf_op jit(solution)/shard_map/ppermute | solution.py:23

commit v5 on v4

--- a/solution.py
+++ b/solution.py
@@ -229,16 +229,9 @@
         base_ref[lo : lo + W, :] = jnp.where(taken > 0, 0.0, cur[lo : lo + W, :].astype(F32)).astype(BF)
 
 
-def chain_kernel(n_piece, split, n_side, scal, *refs):
-    piv, own, other, came, rest, put, start_rows, inv = refs[:8]
-    sides = refs[8 : 8 + n_side]
-    refs = refs[8 + n_side :]
-    mix_ref, base_ref, s_ref, u_ref = refs
+def assemble_kernel(scal, piv, own, other, came, rest, top_ref, pick_ref):
     row_of, col_of = pivot_views(piv)
-    row_dev, columns = start_rows.shape
-    part = W // n_piece
-    is_top = scal[ROW] == 0
-    top_block = scal[FIRST] == 0
+    is_top = scal[ROW] == 0
     low = scal[IS_LOW] == 1
     core0 = scal[CORE] == 0
     half = W // 2
@@ -254,7 +247,20 @@
         picks.append(jnp.where(here_column(scal, col_of(k)), chip, got))
     table = matches(STEPS, row_of, col_of)
     chosen = rows_resolved(scal, STEPS, table, col_of, tops, picks)
-
+    for k in STEPS:
+        top_ref[k * W : (k + 1) * W, :] = tops[k].astype(BF)
+        pick_ref[k * W : (k + 1) * W, :] = chosen[k].astype(BF)
+
+
+def chain_kernel(n_piece, split, n_side, scal, *refs):
+    _, tops, chosen, put, start_rows, inv = refs[:6]
+    sides = refs[6 : 6 + n_side]
+    refs = refs[6 + n_side :]
+    mix_ref, base_ref, s_ref, u_ref = refs
+    row_dev, columns = start_rows.shape
+    part = W // n_piece
+    top_block = scal[FIRST] == 0
+    core0 = scal[CORE] == 0
     def panel_rows(arrays, base):
         if len(arrays) == 1:
             return arrays[0][:, base : base + W]
@@ -274,7 +280,8 @@
         return jnp.where(mine_is, mine.astype(F32), theirs.astype(F32)).astype(BF)
 
     for k in STEPS:
-        acc, upper = chosen[k], tops[k]
+        rows = slice(k * W, (k + 1) * W)
+        acc, upper = chosen[rows, :].astype(F32), tops[rows, :].astype(F32)
         for e in STEPS[:k]:
             mixed = mix_ref[e * W : (e + 1) * W, :]
             acc = acc - dot_tn(side_rows((k, e), 1), mixed)
@@ -375,18 +382,25 @@
         else:
             sp, sp_other = psum_pair(sp, row)
             sp_came = sp
+        put, start_rows, weight = call(
+            functools.partial(pass_first, prepare_kernel, tile),
+            where,
+            [bf(row_dev, row_dev), bf(row_dev, columns), jax.ShapeDtypeStruct((8, row_dev), F32)],
+            1,
+            exponents, after(pivots, sp), matrix,
+        )
         if n_piece == 8:
             bz2 = swap(panels, "pcol", 8, 4)
             bx0 = swap(panels, "pcol", 8, 1)
             bz1 = swap(panels, "pcol", 8, 2)
-            sp_came = after(sp_came, bx0)
+            sp_came = after(sp_came, bx0, weight)
             own = call(final_slices, where2, bf(part, load), 0, pivots, sp, sp_other, sp_came)
         else:
             own = call(final_slices, where2, bf(part, load), 0, pivots, sp, sp_other, sp_came)
             bulk, special = gather(panels, 1), gather(own, 0)
         if split:
             other = swap(rows, "prow", 4, 1)
-            message = call(row_message_kernel, where, bf(row_dev // 2, columns), 0, after(pivots, own), rows, other)
+            message = call(row_message_kernel, where, bf(row_dev // 2, columns), 0, after(pivots, own, bz2), rows, other)
             came = swap(message, "prow", 4, 2)
             rest = None
         else:
@@ -394,37 +408,31 @@
             rows, other = psum_pair(rows, row)
             came = rest = rows[: row_dev // 2]
         held = pivots
-        put, start_rows, weight = call(
-            functools.partial(pass_first, prepare_kernel, tile),
-            where,
-            [bf(row_dev, row_dev), bf(row_dev, columns), jax.ShapeDtypeStruct((8, row_dev), F32)],
-            1,
-            exponents, after(pivots, message), matrix,
-        )
         if n_piece == 8:
             sz2 = swap(after(own, message, bz1), "pcol", 8, 4)
             sz3 = swap(own, "pcol", 8, 6)
             sz1 = swap(own, "pcol", 8, 2)
-            bz3 = swap(after(panels, bz2, weight), "pcol", 8, 6)
+            bz3 = swap(after(panels, bz2, sz2), "pcol", 8, 6)
             line = jnp.concatenate([own, sz1, sz2, sz3], axis=0)
             cross = swap(line, "pcol", 8, 1)
             bz2x = swap(after(bz2, sz3), "pcol", 8, 1)
             bz3x = swap(bz3, "pcol", 8, 1)
             line_other = swap(line, "prow", 4, 1)
-            bz1x = swap(after(bx0, line_other), "pcol", 8, 2)
-            rest = swap(after(came, bz3, bz2x), "prow", 4, 1)
+            bz1x = swap(after(bx0, sz1), "pcol", 8, 2)
+            rest = swap(after(came, bz2x, bz1x), "prow", 4, 1)
             bulk = [panels, bx0, bz1, bz1x, bz2, bz2x, bz3, bz3x]
-            cross_other = swap(cross, "prow", 4, 1)
+            cross_other = swap(after(cross, bz3), "prow", 4, 1)
             special = [line, cross, line_other, cross_other]
             held = pivots
         elif split:
             special = special + [swap(special[0], "prow", 4, 1)]
+        tops, chosen = call(assemble_kernel, where2, [bf(row_dev, columns)] * 2, 0, pivots, rows, other, came, rest)
         mix, base = call(
             functools.partial(chain_kernel, n_piece, split, len(special)),
             where2,
             [bf(row_dev, columns), bf(row_dev, columns)],
             0,
-            held, rows, other, came, rest, put, start_rows, inverses, *special,
+            held, tops, chosen, put, start_rows, inverses, *special,
             scratch=[pltpu.VMEM((row_dev, columns), BF)] * 2,
         )
         return pl.pallas_call(

time: 59.1 us -> 55.5 us (0.939)
  starting transfers between devices: 26.3 us -> 24.3 us
  waiting for transfers between devices: 15.7 us -> 14 us
    ppermute x18, starting transfers between devices: 26.3 us -> 24.3 us  [swap(): return lax.ppermute(value, axis, [(i, i ^ mask) for i in range(size)])]
    ppermute x18, waiting for transfers between devices: 15.7 us -> 14 us  [swap(): return lax.ppermute(value, axis, [(i, i ^ mask) for i in range(size)])]
    pallas_call x7 -> x8, Pallas kernels: 11.7 us -> 11.6 us  [call(): pl.pallas_call(body, out_shape=shapes, in_specs=[SMEM] * n_smem + [VMEM]...]
  transfers between devices with their start and end apart: 18 -> 18, of which waited for: 6 -> 9; matrix products, arithmetic and copies ran while one was open for 0% -> 0% of each run, Pallas kernels for 20% -> 21%
where the time goes in v5:
time: 55.5 us; the launch traced here: 55.2 us
  starting transfers between devices  24.3 us (44%)
  Pallas kernels  14.8 us (27%)
  waiting for transfers between devices  14 us (25%)
  local copies, waits for them, and re-layouts  1.93 us (3%)
    ppermute x18, starting transfers between devices, swap(): return lax.ppermute(value, axis, [(i, i ^ mask) for i in range(size)])  24.3 us
    ppermute x18, waiting for transfers between devices, swap(): return lax.ppermute(value, axis, [(i, i ^ mask) for i in range(size)])  14 us
    pallas_call x8, Pallas kernels, call(): pl.pallas_call(body, out_shape=shapes, in_specs=[SMEM] * n_smem + [VMEM]...  11.6 us
    pallas_call x1, Pallas kernels, on_device(): pl.pallas_call(functools.partial(update_kernel, n_piece), out_shape=bf(ro...  3.22 us
    unnamed x12, local copies, waits for them, and re-layouts  1.93 us
  transfers between devices with their start and end apart: 18, of which 9 were waited for; matrix products, arithmetic and copies ran while one was open for 0% of the time, Pallas kernels for 21%

profile of v5, /device:TPU:0, one launch (start us, length us, event | category | flops | bytes accessed | tf_op | source)
XLA Modules:
  0.0 55.2 jit_solution(11985373294741220702)
XLA Ops:
  0.0 1.2 %copy-done = bf16[1024,512]{1,0:T(8,128)(2,1)S(1)} copy-done((bf16[1024,512]{1,0:T(8,128)(2,1)S(1)}, bf16[1024,512]{1,0:T(8,128)(2,1)}, u32[]{:S(2)}) %copy-start) | copy-done | bytes 1048600
  1.2 0.7 %copy-done.4 = s32[4,256]{1,0:T(4,128)S(1)} copy-done((s32[4,256]{1,0:T(4,128)S(1)}, s32[4,256]{1,0:T(4,128)}, u32[]{:S(2)}) %copy-start.4) | copy-done | bytes 4120
  2.1 2.4 %collective-permute-start = (bf16[1024,512]{1,0:T(8,128)(2,1)S(1)}, bf16[1024,512]{1,0:T(8,128)(2,1)S(1)}, u32[]{:S(2)}, u32[]{:S(2)}) collective-permute-start(bf16[1024,512]{1,0:T(8,128)(2,1)S(1)} %shard_map.55.refs_1_), channel_id=1, source_target_pairs={{0,8},{8,0},{16,24},{24,16},{1,9},{9,1},{17,25},{25,17},{2,10},{10... | collective-permute-start | bytes 3145736 | tf_op jit(solution)/shard_map/ppermute | solution.py:23
  4.6 2.3 %collective-permute-start.3 = (bf16[4,32,1024]{2,1,0:T(8,128)(2,1)S(1)}, bf16[4,32,1024]{2,1,0:T(8,128)(2,1)S(1)}, u32[]{:S(2)}, u32[]{:S(2)}) collective-permute-start(bf16[4,32,1024]{2,1,0:T(8,128)(2,1)S(1)} %copy-done.2), channel_id=1, source_target_pairs={{0,1},{1,0},{2,3},{3,2},{4,5},{5,4},{6,7},{7,6},{8,9},{9,8},{10,11... | collective-permute-start | bytes 786440 | tf_op jit(solution)/shard_map/ppermute | solution.py:23
  6.9 2.6 %collective-permute-start.4 = (bf16[4,32,1024]{2,1,0:T(8,128)(2,1)S(1)}, bf16[4,32,1024]{2,1,0:T(8,128)(2,1)S(1)}, u32[]{:S(2)}, u32[]{:S(2)}) collective-permute-start(bf16[4,32,1024]{2,1,0:T(8,128)(2,1)S(1)} %copy-done.2), channel_id=1, source_target_pairs={{0,4},{1,5},{2,6},{3,7},{4,0},{5,1},{6,2},{7,3},{8,12},{9,13},{10,... | collective-permute-start | bytes 786440 | tf_op jit(solution)/shard_map/ppermute | solution.py:23
  9.5 1.6 %collective-permute-start.11 = (bf16[4,32,1024]{2,1,0:T(8,128)(2,1)S(1)}, bf16[4,32,1024]{2,1,0:T(8,128)(2,1)S(1)}, u32[]{:S(2)}, u32[]{:S(2)}) collective-permute-start(bf16[4,32,1024]{2,1,0:T(8,128)(2,1)S(1)} %copy-done.2), channel_id=1, source_target_pairs={{0,2},{1,3},{2,0},{3,1},{4,6},{5,7},{6,4},{7,5},{8,10},{9,11},{10,... | collective-permute-start | bytes 786440 | tf_op jit(solution)/shard_map/ppermute | solution.py:23
  11.1 1.4 %shard_map.56.refs_1_ = bf16[32,1536]{1,0:T(8,128)(2,1)S(1)} custom-call(s32[4,8]{1,0:T(4,128)S(1)} %copy-done.5, s32[4,256]{1,0:T(4,128)S(1)} %copy-done.4, bf16[4,32,1024]{2,1,0:T(8,128)(2,1)S(1)} %copy-done.2), custom_call_target="tpu_custom_call" | custom-call | flops 1000 | bytes 1000 | tf_op jit(solution)/shard_map/pallas_call | solution.py:334
  12.5 1.3 %collective-permute-done.1.refs_2_ = bf16[32,1536]{1,0:T(8,128)(2,1)S(1)} collective-permute-done((bf16[32,1536]{1,0:T(8,128)(2,1)S(1)}, bf16[32,1536]{1,0:T(8,128)(2,1)S(1)}, u32[]{:S(2)}, u32[]{:S(2)}) %collective-permute-start.1) | collective-permute-done | bytes 98336 | tf_op jit(solution)/shard_map/ppermute | solution.py:23
  13.8 0.7 %shard_map.57 = bf16[32,1536]{1,0:T(8,128)(2,1)S(1)} custom-call(s32[4,256]{1,0:T(4,128)S(1)} %copy-done.4, bf16[32,1536]{1,0:T(8,128)(2,1)S(1)} %shard_map.56.refs_1_, bf16[32,1536]{1,0:T(8,128)(2,1)S(1)} %collective-permute-done.1.refs_2_), custom_call_target="tpu_custom_call" | custom-call | flops 1000 | bytes 1000 | tf_op jit(solution)/shard_map/pallas_call | solution.py:334
  14.5 1.8 %collective-permute-start.2 = (bf16[32,1536]{1,0:T(8,128)(2,1)S(1)}, bf16[32,1536]{1,0:T(8,128)(2,1)S(1)}, u32[]{:S(2)}, u32[]{:S(2)}) collective-permute-start(bf16[32,1536]{1,0:T(8,128)(2,1)S(1)} %shard_map.57), channel_id=1, source_target_pairs={{0,16},{8,24},{16,0},{24,8},{1,17},{9,25},{17,1},{25,9},{2,18},{10... | collective-permute-start | bytes 294920 | tf_op jit(solution)/shard_map/ppermute | solution.py:23
  16.4 2.8 %shard_map.58 = (bf16[1024,1024]{1,0:T(8,128)(2,1)S(1)}, bf16[1024,512]{1,0:T(8,128)(2,1)S(1)}, f32[8,1024]{1,0:T(8,128)S(1)}) custom-call(s32[4,8]{1,0:T(4,128)S(1)} %copy-done.5, s32[4,256]{1,0:T(4,128)S(1)} %copy-done.4, bf16[1024,512]{1,0:T(8,128)(2,1)S(1)} %copy-done.1), custom_call_target="tpu_custom_call" | custom-call | flops 1000 | bytes 1000 | tf_op jit(solution)/shard_map/pallas_call | solution.py:334
  19.2 0.3 collective-permute-done.2.refs_3_
  19.5 0.7 %shard_map.59 = bf16[32,1536]{1,0:T(8,128)(2,1)S(1)} custom-call(s32[4,256]{1,0:T(4,128)S(1)} %copy-done.4, bf16[32,1536]{1,0:T(8,128)(2,1)S(1)} %shard_map.56.refs_1_, bf16[32,1536]{1,0:T(8,128)(2,1)S(1)} %collective-permute-done.1.refs_2_, bf16[32,1536]{1,0:T(8,128)(2,1)S(1)} %collective-permute-done.2.refs_3_), custom_call_target="tpu_custom_call" | custom-call | flops 1000 | bytes 1000 | tf_op jit(solution)/shard_map/pallas_call | solution.py:334
  20.5 0.7 %collective-permute-start.8 = (bf16[32,1536]{1,0:T(8,128)(2,1)S(1)}, bf16[32,1536]{1,0:T(8,128)(2,1)S(1)}, u32[]{:S(2)}, u32[]{:S(2)}) collective-permute-start(bf16[32,1536]{1,0:T(8,128)(2,1)S(1)} %shard_map.59), channel_id=1, source_target_pairs={{0,2},{1,3},{2,0},{3,1},{4,6},{5,7},{6,4},{7,5},{8,10},{9,11},{10,... | collective-permute-start | bytes 294920 | tf_op jit(solution)/shard_map/ppermute | solution.py:23
  21.2 0.3 collective-permute-done.4.refs_4_
  21.5 1.9 %shard_map.60 = bf16[512,512]{1,0:T(8,128)(2,1)S(1)} custom-call(s32[4,256]{1,0:T(4,128)S(1)} %copy-done.4, bf16[1024,512]{1,0:T(8,128)(2,1)S(1)} %shard_map.55.refs_1_, bf16[1024,512]{1,0:T(8,128)(2,1)S(1)} %collective-permute-done.refs_2_), custom_call_target="tpu_custom_call" | custom-call | flops 1000 | bytes 1000 | tf_op jit(solution)/shard_map/pallas_call | solution.py:334
  23.5 3.2 %collective-permute-start.12 = (bf16[32,1536]{1,0:T(8,128)(2,1)S(1)}, bf16[32,1536]{1,0:T(8,128)(2,1)S(1)}, u32[]{:S(2)}, u32[]{:S(2)}) collective-permute-start(bf16[32,1536]{1,0:T(8,128)(2,1)S(1)} %shard_map.59), channel_id=1, source_target_pairs={{0,4},{1,5},{2,6},{3,7},{4,0},{5,1},{6,2},{7,3},{8,12},{9,13},{10,... | collective-permute-start | bytes 294920 | tf_op jit(solution)/shard_map/ppermute | solution.py:23
  26.7 1.7 %collective-permute-start.5 = (bf16[512,512]{1,0:T(8,128)(2,1)S(1)}, bf16[512,512]{1,0:T(8,128)(2,1)S(1)}, u32[]{:S(2)}, u32[]{:S(2)}) collective-permute-start(bf16[512,512]{1,0:T(8,128)(2,1)S(1)} %shard_map.60), channel_id=1, source_target_pairs={{0,16},{8,24},{16,0},{24,8},{1,17},{9,25},{17,1},{25,9},{2,18},{10... | collective-permute-start | bytes 1572872 | tf_op jit(solution)/shard_map/ppermute | solution.py:23
  28.5 0.5 collective-permute-start.7
  29.0 2.0 %collective-permute-start.9 = (bf16[4,32,1024]{2,1,0:T(8,128)(2,1)S(1)}, bf16[4,32,1024]{2,1,0:T(8,128)(2,1)S(1)}, u32[]{:S(2)}, u32[]{:S(2)}) collective-permute-start(bf16[4,32,1024]{2,1,0:T(8,128)(2,1)S(1)} %collective-permute-done.3.refs_1_), channel_id=1, source_target_pairs={{0,2},{1,3},{2,0},{3,1},{4,6},{5,7},{6,4},{7,5},{8,10},{9,11},{10,... | collective-permute-start | bytes 786440 | tf_op jit(solution)/shard_map/ppermute | solution.py:23
  31.0 0.4 collective-permute-done.12
  31.5 1.1 %collective-permute-start.13 = (bf16[128,1536]{1,0:T(8,128)(2,1)S(1)}, bf16[128,1536]{1,0:T(8,128)(2,1)S(1)}, u32[]{:S(2)}, u32[]{:S(2)}) collective-permute-start(bf16[128,1536]{1,0:T(8,128)(2,1)S(1)} %pad_maximum_fusion.refs_6_), channel_id=1, source_target_pairs={{0,1},{1,0},{2,3},{3,2},{4,5},{5,4},{6,7},{7,6},{8,9},{9,8},{10,11... | collective-permute-start | bytes 1179656 | tf_op jit(solution)/shard_map/ppermute | solution.py:23
  32.6 2.4 %collective-permute-start.15 = (bf16[4,32,1024]{2,1,0:T(8,128)(2,1)S(1)}, bf16[4,32,1024]{2,1,0:T(8,128)(2,1)S(1)}, u32[]{:S(2)}, u32[]{:S(2)}) collective-permute-start(bf16[4,32,1024]{2,1,0:T(8,128)(2,1)S(1)} %copy-done.2), channel_id=1, source_target_pairs={{0,6},{1,7},{2,4},{3,5},{4,2},{5,3},{6,0},{7,1},{8,14},{9,15},{10,... | collective-permute-start | bytes 786440 | tf_op jit(solution)/shard_map/ppermute | solution.py:23
  35.1 2.3 %collective-permute-done.7.refs_5_ = bf16[4,32,1024]{2,1,0:T(8,128)(2,1)S(1)} collective-permute-done((bf16[4,32,1024]{2,1,0:T(8,128)(2,1)S(1)}, bf16[4,32,1024]{2,1,0:T(8,128)(2,1)S(1)}, u32[]{:S(2)}, u32[]{:S(2)}) %collective-permute-start.7) | collective-permute-done | bytes 262176 | tf_op jit(solution)/shard_map/ppermute | solution.py:23
  37.4 5.2 %collective-permute-done.9.refs_3_ = bf16[4,32,1024]{2,1,0:T(8,128)(2,1)S(1)} collective-permute-done((bf16[4,32,1024]{2,1,0:T(8,128)(2,1)S(1)}, bf16[4,32,1024]{2,1,0:T(8,128)(2,1)S(1)}, u32[]{:S(2)}, u32[]{:S(2)}) %collective-permute-start.9) | collective-permute-done | bytes 262176 | tf_op jit(solution)/shard_map/ppermute | solution.py:23
  42.6 0.5 collective-permute-start.14
  43.3 0.9 %collective-permute-start.17 = (bf16[4,32,1024]{2,1,0:T(8,128)(2,1)S(1)}, bf16[4,32,1024]{2,1,0:T(8,128)(2,1)S(1)}, u32[]{:S(2)}, u32[]{:S(2)}) collective-permute-start(bf16[4,32,1024]{2,1,0:T(8,128)(2,1)S(1)} %collective-permute-done.15.refs_6_), channel_id=1, source_target_pairs={{0,1},{1,0},{2,3},{3,2},{4,5},{5,4},{6,7},{7,6},{8,9},{9,8},{10,11... | collective-permute-start | bytes 786440 | tf_op jit(solution)/shard_map/ppermute | solution.py:23
  44.2 0.4 collective-permute-done.10.refs_4_
  44.6 1.9 %shard_map.61 = (bf16[1024,512]{1,0:T(8,128)(2,1)S(1)}, bf16[1024,512]{1,0:T(8,128)(2,1)S(1)}) custom-call(s32[4,256]{1,0:T(4,128)S(1)} %copy-done.4, bf16[1024,512]{1,0:T(8,128)(2,1)S(1)} %shard_map.55.refs_1_, bf16[1024,512]{1,0:T(8,128)(2,1)S(1)} %collective-permute-done.refs_2_, bf16[512,512]{1,0:T(8,128)(2,1)S(1)} %collective-permute-done.5.refs_3_, ...), custom_call_target="tpu_custom_call" | custom-call | flops 1000 | bytes 1000 | tf_op jit(solution)/shard_map/pallas_call | solution.py:334
  46.5 1.9 %shard_map.62 = (bf16[1024,512]{1,0:T(8,128)(2,1)S(1)}, bf16[1024,512]{1,0:T(8,128)(2,1)S(1)}) custom-call(s32[4,256]{1,0:T(4,128)S(1)} %copy-done.4, bf16[1024,512]{1,0:T(8,128)(2,1)S(1)} %get-tuple-element.28.refs_1_, bf16[1024,512]{1,0:T(8,128)(2,1)S(1)} %get-tuple-element.29.refs_2_, bf16[1024,1024]{1,0:T(8,128)(2,1)S(1)} %get-tuple-element.30.refs_3_, ...), custom_call_target="tpu_custom_call" | custom-call | flops 1000 | bytes 1000 | tf_op jit(solution)/shard_map/pallas_call | solution.py:334
  48.4 3.6 %collective-permute-done.17.refs_7_ = bf16[4,32,1024]{2,1,0:T(8,128)(2,1)S(1)} collective-permute-done((bf16[4,32,1024]{2,1,0:T(8,128)(2,1)S(1)}, bf16[4,32,1024]{2,1,0:T(8,128)(2,1)S(1)}, u32[]{:S(2)}, u32[]{:S(2)}) %collective-permute-start.17) | collective-permute-done | bytes 262176 | tf_op jit(solution)/shard_map/ppermute | solution.py:23
  52.0 3.2 %shard_map.63 = bf16[1024,512]{1,0:T(8,128)(2,1)} custom-call(bf16[1024,512]{1,0:T(8,128)(2,1)S(1)} %get-tuple-element.35.base, f32[8,1024]{1,0:T(8,128)S(1)} %get-tuple-element.22.weight, bf16[1024,512]{1,0:T(8,128)(2,1)S(1)} %get-tuple-element.36.mix, bf16[4,32,1024]{2,1,0:T(8,128)(2,1)S(1)} %copy-done.2, ...), custom_call_target="tpu_custom_call" | custom-call | flops 1000 | bytes 1000 | tf_op jit(solution)/shard_map/pallas_call | solution.py:438
  (26 shorter events, 0.8 us)
Async XLA Ops:
  0.0 1.2 %copy-start = (bf16[1024,512]{1,0:T(8,128)(2,1)S(1)}, bf16[1024,512]{1,0:T(8,128)(2,1)}, u32[]{:S(2)}) copy-start(bf16[1024,512]{1,0:T(8,128)(2,1)} %refs_2_.3) | copy-start | bytes 3145732
  1.2 0.7 %copy-start.4 = (s32[4,256]{1,0:T(4,128)S(1)}, s32[4,256]{1,0:T(4,128)}, u32[]{:S(2)}) copy-start(s32[4,256]{1,0:T(4,128)} %refs_0_.15) | copy-start | bytes 12292
  1.9 2.6 %copy-start.2 = (bf16[4,32,1024]{2,1,0:T(8,128)(2,1)S(1)}, bf16[4,32,1024]{2,1,0:T(8,128)(2,1)}, u32[]{:S(2)}) copy-start(bf16[4,32,1024]{2,1,0:T(8,128)(2,1)} %refs_0_.16) | copy-start | bytes 786436
  1.9 9.1 %copy-start.5 = (s32[4,8]{1,0:T(4,128)S(1)}, s32[4,8]{1,0:T(4,128)}, u32[]{:S(2)}) copy-start(s32[4,8]{1,0:T(4,128)} %refs_0_.11) | copy-start | bytes 388
  1.9 14.5 %copy-start.1 = (bf16[1024,512]{1,0:T(8,128)(2,1)S(1)}, bf16[1024,512]{1,0:T(8,128)(2,1)}, u32[]{:S(2)}) copy-start(bf16[1024,512]{1,0:T(8,128)(2,1)} %refs_2_.3) | copy-start | bytes 3145732
  2.1 19.4 %collective-permute-start = (bf16[1024,512]{1,0:T(8,128)(2,1)S(1)}, bf16[1024,512]{1,0:T(8,128)(2,1)S(1)}, u32[]{:S(2)}, u32[]{:S(2)}) collective-permute-start(bf16[1024,512]{1,0:T(8,128)(2,1)S(1)} %shard_map.55.refs_1_), channel_id=1, source_target_pairs={{0,8},{8,0},{16,24},{24,16},{1,9},{9,1},{17,25},{25,17},{2,10},{10... | collective-permute-start | bytes 3145736 | tf_op jit(solution)/shard_map/ppermute | solution.py:23
  4.6 14.9 %collective-permute-start.3 = (bf16[4,32,1024]{2,1,0:T(8,128)(2,1)S(1)}, bf16[4,32,1024]{2,1,0:T(8,128)(2,1)S(1)}, u32[]{:S(2)}, u32[]{:S(2)}) collective-permute-start(bf16[4,32,1024]{2,1,0:T(8,128)(2,1)S(1)} %copy-done.2), channel_id=1, source_target_pairs={{0,1},{1,0},{2,3},{3,2},{4,5},{5,4},{6,7},{7,6},{8,9},{9,8},{10,11... | collective-permute-start | bytes 786440 | tf_op jit(solution)/shard_map/ppermute | solution.py:23
  6.9 14.6 %collective-permute-start.4 = (bf16[4,32,1024]{2,1,0:T(8,128)(2,1)S(1)}, bf16[4,32,1024]{2,1,0:T(8,128)(2,1)S(1)}, u32[]{:S(2)}, u32[]{:S(2)}) collective-permute-start(bf16[4,32,1024]{2,1,0:T(8,128)(2,1)S(1)} %copy-done.2), channel_id=1, source_target_pairs={{0,4},{1,5},{2,6},{3,7},{4,0},{5,1},{6,2},{7,3},{8,12},{9,13},{10,... | collective-permute-start | bytes 786440 | tf_op jit(solution)/shard_map/ppermute | solution.py:23
  9.5 14.0 %collective-permute-start.11 = (bf16[4,32,1024]{2,1,0:T(8,128)(2,1)S(1)}, bf16[4,32,1024]{2,1,0:T(8,128)(2,1)S(1)}, u32[]{:S(2)}, u32[]{:S(2)}) collective-permute-start(bf16[4,32,1024]{2,1,0:T(8,128)(2,1)S(1)} %copy-done.2), channel_id=1, source_target_pairs={{0,2},{1,3},{2,0},{3,1},{4,6},{5,7},{6,4},{7,5},{8,10},{9,11},{10,... | collective-permute-start | bytes 786440 | tf_op jit(solution)/shard_map/ppermute | solution.py:23
  12.4 1.4 %collective-permute-start.1 = (bf16[32,1536]{1,0:T(8,128)(2,1)S(1)}, bf16[32,1536]{1,0:T(8,128)(2,1)S(1)}, u32[]{:S(2)}, u32[]{:S(2)}) collective-permute-start(bf16[32,1536]{1,0:T(8,128)(2,1)S(1)} %shard_map.56.refs_1_), channel_id=1, source_target_pairs={{0,8},{8,0},{16,24},{24,16},{1,9},{9,1},{17,25},{25,17},{2,10},{10... | collective-permute-start | bytes 294920 | tf_op jit(solution)/shard_map/ppermute | solution.py:23
  14.5 4.9 %collective-permute-start.2 = (bf16[32,1536]{1,0:T(8,128)(2,1)S(1)}, bf16[32,1536]{1,0:T(8,128)(2,1)S(1)}, u32[]{:S(2)}, u32[]{:S(2)}) collective-permute-start(bf16[32,1536]{1,0:T(8,128)(2,1)S(1)} %shard_map.57), channel_id=1, source_target_pairs={{0,16},{8,24},{16,0},{24,8},{1,17},{9,25},{17,1},{25,9},{2,18},{10... | collective-permute-start | bytes 294920 | tf_op jit(solution)/shard_map/ppermute | solution.py:23
  20.2 8.2 %collective-permute-start.6 = (bf16[32,1536]{1,0:T(8,128)(2,1)S(1)}, bf16[32,1536]{1,0:T(8,128)(2,1)S(1)}, u32[]{:S(2)}, u32[]{:S(2)}) collective-permute-start(bf16[32,1536]{1,0:T(8,128)(2,1)S(1)} %shard_map.59), channel_id=1, source_target_pairs={{0,6},{1,7},{2,4},{3,5},{4,2},{5,3},{6,0},{7,1},{8,14},{9,15},{10,... | collective-permute-start | bytes 294920 | tf_op jit(solution)/shard_map/ppermute | solution.py:23
  20.5 8.5 %collective-permute-start.8 = (bf16[32,1536]{1,0:T(8,128)(2,1)S(1)}, bf16[32,1536]{1,0:T(8,128)(2,1)S(1)}, u32[]{:S(2)}, u32[]{:S(2)}) collective-permute-start(bf16[32,1536]{1,0:T(8,128)(2,1)S(1)} %shard_map.59), channel_id=1, source_target_pairs={{0,2},{1,3},{2,0},{3,1},{4,6},{5,7},{6,4},{7,5},{8,10},{9,11},{10,... | collective-permute-start | bytes 294920 | tf_op jit(solution)/shard_map/ppermute | solution.py:23
  23.5 23.0 %copy-start.3 = (bf16[4,256,256]{2,1,0:T(8,128)(2,1)S(1)}, bf16[4,256,256]{2,1,0:T(8,128)(2,1)}, u32[]{:S(2)}) copy-start(bf16[4,256,256]{2,1,0:T(8,128)(2,1)} %refs_5_.1) | copy-start | bytes 1572868
  23.5 8.0 %collective-permute-start.12 = (bf16[32,1536]{1,0:T(8,128)(2,1)S(1)}, bf16[32,1536]{1,0:T(8,128)(2,1)S(1)}, u32[]{:S(2)}, u32[]{:S(2)}) collective-permute-start(bf16[32,1536]{1,0:T(8,128)(2,1)S(1)} %shard_map.59), channel_id=1, source_target_pairs={{0,4},{1,5},{2,6},{3,7},{4,0},{5,1},{6,2},{7,3},{8,12},{9,13},{10,... | collective-permute-start | bytes 294920 | tf_op jit(solution)/shard_map/ppermute | solution.py:23
  26.7 15.9 %collective-permute-start.5 = (bf16[512,512]{1,0:T(8,128)(2,1)S(1)}, bf16[512,512]{1,0:T(8,128)(2,1)S(1)}, u32[]{:S(2)}, u32[]{:S(2)}) collective-permute-start(bf16[512,512]{1,0:T(8,128)(2,1)S(1)} %shard_map.60), channel_id=1, source_target_pairs={{0,16},{8,24},{16,0},{24,8},{1,17},{9,25},{17,1},{25,9},{2,18},{10... | collective-permute-start | bytes 1572872 | tf_op jit(solution)/shard_map/ppermute | solution.py:23
  28.5 8.9 %collective-permute-start.7 = (bf16[4,32,1024]{2,1,0:T(8,128)(2,1)S(1)}, bf16[4,32,1024]{2,1,0:T(8,128)(2,1)S(1)}, u32[]{:S(2)}, u32[]{:S(2)}) collective-permute-start(bf16[4,32,1024]{2,1,0:T(8,128)(2,1)S(1)} %collective-permute-done.4.refs_4_), channel_id=1, source_target_pairs={{0,1},{1,0},{2,3},{3,2},{4,5},{5,4},{6,7},{7,6},{8,9},{9,8},{10,11... | collective-permute-start | bytes 786440 | tf_op jit(solution)/shard_map/ppermute | solution.py:23
  29.0 13.6 %collective-permute-start.9 = (bf16[4,32,1024]{2,1,0:T(8,128)(2,1)S(1)}, bf16[4,32,1024]{2,1,0:T(8,128)(2,1)S(1)}, u32[]{:S(2)}, u32[]{:S(2)}) collective-permute-start(bf16[4,32,1024]{2,1,0:T(8,128)(2,1)S(1)} %collective-permute-done.3.refs_1_), channel_id=1, source_target_pairs={{0,2},{1,3},{2,0},{3,1},{4,6},{5,7},{6,4},{7,5},{8,10},{9,11},{10,... | collective-permute-start | bytes 786440 | tf_op jit(solution)/shard_map/ppermute | solution.py:23
  31.5 11.8 %collective-permute-start.13 = (bf16[128,1536]{1,0:T(8,128)(2,1)S(1)}, bf16[128,1536]{1,0:T(8,128)(2,1)S(1)}, u32[]{:S(2)}, u32[]{:S(2)}) collective-permute-start(bf16[128,1536]{1,0:T(8,128)(2,1)S(1)} %pad_maximum_fusion.refs_6_), channel_id=1, source_target_pairs={{0,1},{1,0},{2,3},{3,2},{4,5},{5,4},{6,7},{7,6},{8,9},{9,8},{10,11... | collective-permute-start | bytes 1179656 | tf_op jit(solution)/shard_map/ppermute | solution.py:23
  32.6 10.5 %collective-permute-start.15 = (bf16[4,32,1024]{2,1,0:T(8,128)(2,1)S(1)}, bf16[4,32,1024]{2,1,0:T(8,128)(2,1)S(1)}, u32[]{:S(2)}, u32[]{:S(2)}) collective-permute-start(bf16[4,32,1024]{2,1,0:T(8,128)(2,1)S(1)} %copy-done.2), channel_id=1, source_target_pairs={{0,6},{1,7},{2,4},{3,5},{4,2},{5,3},{6,0},{7,1},{8,14},{9,15},{10,... | collective-permute-start | bytes 786440 | tf_op jit(solution)/shard_map/ppermute | solution.py:23
  42.6 1.9 %collective-permute-start.10 = (bf16[512,512]{1,0:T(8,128)(2,1)S(1)}, bf16[512,512]{1,0:T(8,128)(2,1)S(1)}, u32[]{:S(2)}, u32[]{:S(2)}) collective-permute-start(bf16[512,512]{1,0:T(8,128)(2,1)S(1)} %collective-permute-done.5.refs_3_), channel_id=1, source_target_pairs={{0,8},{8,0},{16,24},{24,16},{1,9},{9,1},{17,25},{25,17},{2,10},{10... | collective-permute-start | bytes 1572872 | tf_op jit(solution)/shard_map/ppermute | solution.py:23
  42.6 3.8 %collective-permute-start.14 = (bf16[128,1536]{1,0:T(8,128)(2,1)S(1)}, bf16[128,1536]{1,0:T(8,128)(2,1)S(1)}, u32[]{:S(2)}, u32[]{:S(2)}) collective-permute-start(bf16[128,1536]{1,0:T(8,128)(2,1)S(1)} %pad_maximum_fusion.refs_6_), channel_id=1, source_target_pairs={{0,8},{8,0},{16,24},{24,16},{1,9},{9,1},{17,25},{25,17},{2,10},{10... | collective-permute-start | bytes 1179656 | tf_op jit(solution)/shard_map/ppermute | solution.py:23
  43.3 3.2 %collective-permute-start.16 = (bf16[128,1536]{1,0:T(8,128)(2,1)S(1)}, bf16[128,1536]{1,0:T(8,128)(2,1)S(1)}, u32[]{:S(2)}, u32[]{:S(2)}) collective-permute-start(bf16[128,1536]{1,0:T(8,128)(2,1)S(1)} %collective-permute-done.13.refs_7_), channel_id=1, source_target_pairs={{0,8},{8,0},{16,24},{24,16},{1,9},{9,1},{17,25},{25,17},{2,10},{10... | collective-permute-start | bytes 1179656 | tf_op jit(solution)/shard_map/ppermute | solution.py:23
  43.3 8.7 %collective-permute-start.17 = (bf16[4,32,1024]{2,1,0:T(8,128)(2,1)S(1)}, bf16[4,32,1024]{2,1,0:T(8,128)(2,1)S(1)}, u32[]{:S(2)}, u32[]{:S(2)}) collective-permute-start(bf16[4,32,1024]{2,1,0:T(8,128)(2,1)S(1)} %collective-permute-done.15.refs_6_), channel_id=1, source_target_pairs={{0,1},{1,0},{2,3},{3,2},{4,5},{5,4},{6,7},{7,6},{8,9},{9,8},{10,11... | collective-permute-start | bytes 786440 | tf_op jit(solution)/shard_map/ppermute | solution.py:23

commit v6 on v5

--- a/solution.py
+++ b/solution.py
@@ -256,7 +256,8 @@
     _, tops, chosen, put, start_rows, inv = refs[:6]
     sides = refs[6 : 6 + n_side]
     refs = refs[6 + n_side :]
-    mix_ref, base_ref, s_ref, u_ref = refs
+    weight, pieces = refs[0], refs[1:n_piece]
+    mix_ref, base_ref, s_ref, u_ref = refs[n_piece:]
     row_dev, columns = start_rows.shape
     part = W // n_piece
     top_block = scal[FIRST] == 0
@@ -297,22 +298,27 @@
 
     @pl.when(top_block)
     def _():
-        base_ref[...] = s_ref[...]
+        base_ref[...] = s_ref[...].astype(F32)
 
     @pl.when(jnp.logical_not(top_block))
     def _():
+        early = (n_piece - 1) * part
         for lo in range(0, row_dev, W):
-            placed = dot(put[lo : lo + W, :], u_ref[...])
-            base_ref[lo : lo + W, :] = (start_rows[lo : lo + W, :].astype(F32) + placed).astype(BF)
-
-
-def update_kernel(n_piece, base, weight, mix, *refs):
-    pieces, out = refs[:n_piece], refs[n_piece]
-    acc = base[...].astype(F32)
-    for k in STEPS:
-        block = jnp.concatenate([p[k] for p in pieces], axis=0) * weight[k : k + 1, :].astype(BF)
-        acc = acc - dot_tn(block, mix[k * W : (k + 1) * W, :])
-    out[...] = acc.astype(BF)
+            rows = slice(lo, lo + W)
+            acc = start_rows[rows, :].astype(F32) + dot(put[rows, :], u_ref[...])
+            for k in STEPS:
+                if early:
+                    block = jnp.concatenate([p[k, :, rows] for p in pieces], axis=0) * weight[k : k + 1, rows].astype(BF)
+                    acc = acc - dot_tn(block, mix_ref[k * W : k * W + early, :])
+            base_ref[rows, :] = acc
+
+
+def update_kernel(base, weight, mix, last, out):
+    rows = pl.ds(pl.multiple_of(pl.program_id(0) * out.shape[0], out.shape[0]), out.shape[0])
+    part = last.shape[1]
+    block = jnp.concatenate([last[k, :, rows] * weight[k : k + 1, rows].astype(BF) for k in STEPS], axis=0)
+    mixed = jnp.concatenate([mix[(k + 1) * W - part : (k + 1) * W, :] for k in STEPS], axis=0)
+    out[...] = (base[...] - dot_tn(block, mixed)).astype(BF)
 
 
 def place(split, row_dev, n_row, summed):
@@ -430,25 +436,20 @@
         mix, base = call(
             functools.partial(chain_kernel, n_piece, split, len(special)),
             where2,
-            [bf(row_dev, columns), bf(row_dev, columns)],
+            [bf(row_dev, columns), jax.ShapeDtypeStruct((row_dev, columns), F32)],
             0,
-            held, tops, chosen, put, start_rows, inverses, *special,
+            held, tops, chosen, put, start_rows, inverses, *special, weight, *bulk[:-1],
             scratch=[pltpu.VMEM((row_dev, columns), BF)] * 2,
         )
         return pl.pallas_call(
-            functools.partial(update_kernel, n_piece),
+            update_kernel,
             out_shape=bf(row_dev, columns),
-            grid=(row_dev // W,),
-            in_specs=[
-                pl.BlockSpec((W, columns), lambda i: (i, 0)),
-                pl.BlockSpec((8, W), lambda i: (0, i)),
-                pl.BlockSpec((row_dev, columns), lambda i: (0, 0)),
-            ]
-            + [pl.BlockSpec((len(STEPS), W // n_piece, W), lambda i: (0, 0, i))] * n_piece,
-            out_specs=pl.BlockSpec((W, columns), lambda i: (i, 0)),
+            grid=(row_dev // 512,),
+            in_specs=[pl.BlockSpec((512, columns), lambda i: (i, 0))] + [VMEM] * 3,
+            out_specs=pl.BlockSpec((512, columns), lambda i: (i, 0)),
             cost_estimate=COST,
             compiler_params=pltpu.CompilerParams(vmem_limit_bytes=40 * 1024 * 1024),
-        )(base, weight, mix, *bulk)
+        )(base, weight, mix, bulk[-1])
 
     return on_device
 

time: 55.5 us -> 53.7 us (0.968)
  Pallas kernels: 14.8 us -> 13.3 us
    pallas_call x1, Pallas kernels: 3.22 us -> 1.46 us  [on_device(): pl.pallas_call(update_kernel, out_shape=bf(row_dev, columns), grid=(row_d...]
  transfers between devices with their start and end apart: 18 -> 18, of which waited for: 9 -> 9; matrix products, arithmetic and copies ran while one was open for 0% -> 0% of each run, Pallas kernels for 21% -> 22%
where the time goes in v6:
time: 53.7 us; the launch traced here: 53.5 us
  starting transfers between devices  24.3 us (45%)
  waiting for transfers between devices  13.8 us (26%)
  Pallas kernels  13.3 us (25%)
  local copies, waits for them, and re-layouts  1.93 us (4%)
    ppermute x18, starting transfers between devices, swap(): return lax.ppermute(value, axis, [(i, i ^ mask) for i in range(size)])  24.3 us
    ppermute x18, waiting for transfers between devices, swap(): return lax.ppermute(value, axis, [(i, i ^ mask) for i in range(size)])  13.8 us
    pallas_call x8, Pallas kernels, call(): pl.pallas_call(body, out_shape=shapes, in_specs=[SMEM] * n_smem + [VMEM]...  11.8 us
    unnamed x12, local copies, waits for them, and re-layouts  1.93 us
    pallas_call x1, Pallas kernels, on_device(): pl.pallas_call(update_kernel, out_shape=bf(row_dev, columns), grid=(row_d...  1.46 us
  transfers between devices with their start and end apart: 18, of which 9 were waited for; matrix products, arithmetic and copies ran while one was open for 0% of the time, Pallas kernels for 22%

profile of v6, /device:TPU:0, one launch (start us, length us, event | category | flops | bytes accessed | tf_op | source)
XLA Modules:
  0.0 53.5 jit_solution(5591087932490130489)
XLA Ops:
  0.0 1.2 %copy-done = bf16[1024,512]{1,0:T(8,128)(2,1)S(1)} copy-done((bf16[1024,512]{1,0:T(8,128)(2,1)S(1)}, bf16[1024,512]{1,0:T(8,128)(2,1)}, u32[]{:S(2)}) %copy-start) | copy-done | bytes 1048600
  1.2 0.7 %copy-done.4 = s32[4,256]{1,0:T(4,128)S(1)} copy-done((s32[4,256]{1,0:T(4,128)S(1)}, s32[4,256]{1,0:T(4,128)}, u32[]{:S(2)}) %copy-start.4) | copy-done | bytes 4120
  2.1 2.4 %collective-permute-start = (bf16[1024,512]{1,0:T(8,128)(2,1)S(1)}, bf16[1024,512]{1,0:T(8,128)(2,1)S(1)}, u32[]{:S(2)}, u32[]{:S(2)}) collective-permute-start(bf16[1024,512]{1,0:T(8,128)(2,1)S(1)} %shard_map.55.refs_1_), channel_id=1, source_target_pairs={{0,8},{8,0},{16,24},{24,16},{1,9},{9,1},{17,25},{25,17},{2,10},{10... | collective-permute-start | bytes 3145736 | tf_op jit(solution)/shard_map/ppermute | solution.py:23
  4.6 2.3 %collective-permute-start.3 = (bf16[4,32,1024]{2,1,0:T(8,128)(2,1)S(1)}, bf16[4,32,1024]{2,1,0:T(8,128)(2,1)S(1)}, u32[]{:S(2)}, u32[]{:S(2)}) collective-permute-start(bf16[4,32,1024]{2,1,0:T(8,128)(2,1)S(1)} %copy-done.2), channel_id=1, source_target_pairs={{0,1},{1,0},{2,3},{3,2},{4,5},{5,4},{6,7},{7,6},{8,9},{9,8},{10,11... | collective-permute-start | bytes 786440 | tf_op jit(solution)/shard_map/ppermute | solution.py:23
  6.9 2.6 %collective-permute-start.4 = (bf16[4,32,1024]{2,1,0:T(8,128)(2,1)S(1)}, bf16[4,32,1024]{2,1,0:T(8,128)(2,1)S(1)}, u32[]{:S(2)}, u32[]{:S(2)}) collective-permute-start(bf16[4,32,1024]{2,1,0:T(8,128)(2,1)S(1)} %copy-done.2), channel_id=1, source_target_pairs={{0,4},{1,5},{2,6},{3,7},{4,0},{5,1},{6,2},{7,3},{8,12},{9,13},{10,... | collective-permute-start | bytes 786440 | tf_op jit(solution)/shard_map/ppermute | solution.py:23
  9.5 1.6 %collective-permute-start.11 = (bf16[4,32,1024]{2,1,0:T(8,128)(2,1)S(1)}, bf16[4,32,1024]{2,1,0:T(8,128)(2,1)S(1)}, u32[]{:S(2)}, u32[]{:S(2)}) collective-permute-start(bf16[4,32,1024]{2,1,0:T(8,128)(2,1)S(1)} %copy-done.2), channel_id=1, source_target_pairs={{0,2},{1,3},{2,0},{3,1},{4,6},{5,7},{6,4},{7,5},{8,10},{9,11},{10,... | collective-permute-start | bytes 786440 | tf_op jit(solution)/shard_map/ppermute | solution.py:23
  11.0 1.4 %shard_map.56.refs_1_ = bf16[32,1536]{1,0:T(8,128)(2,1)S(1)} custom-call(s32[4,8]{1,0:T(4,128)S(1)} %copy-done.5, s32[4,256]{1,0:T(4,128)S(1)} %copy-done.4, bf16[4,32,1024]{2,1,0:T(8,128)(2,1)S(1)} %copy-done.2), custom_call_target="tpu_custom_call" | custom-call | flops 1000 | bytes 1000 | tf_op jit(solution)/shard_map/pallas_call | solution.py:340
  12.5 1.3 %collective-permute-done.1.refs_2_ = bf16[32,1536]{1,0:T(8,128)(2,1)S(1)} collective-permute-done((bf16[32,1536]{1,0:T(8,128)(2,1)S(1)}, bf16[32,1536]{1,0:T(8,128)(2,1)S(1)}, u32[]{:S(2)}, u32[]{:S(2)}) %collective-permute-start.1) | collective-permute-done | bytes 98336 | tf_op jit(solution)/shard_map/ppermute | solution.py:23
  13.8 0.7 %shard_map.57 = bf16[32,1536]{1,0:T(8,128)(2,1)S(1)} custom-call(s32[4,256]{1,0:T(4,128)S(1)} %copy-done.4, bf16[32,1536]{1,0:T(8,128)(2,1)S(1)} %shard_map.56.refs_1_, bf16[32,1536]{1,0:T(8,128)(2,1)S(1)} %collective-permute-done.1.refs_2_), custom_call_target="tpu_custom_call" | custom-call | flops 1000 | bytes 1000 | tf_op jit(solution)/shard_map/pallas_call | solution.py:340
  14.5 1.8 %collective-permute-start.2 = (bf16[32,1536]{1,0:T(8,128)(2,1)S(1)}, bf16[32,1536]{1,0:T(8,128)(2,1)S(1)}, u32[]{:S(2)}, u32[]{:S(2)}) collective-permute-start(bf16[32,1536]{1,0:T(8,128)(2,1)S(1)} %shard_map.57), channel_id=1, source_target_pairs={{0,16},{8,24},{16,0},{24,8},{1,17},{9,25},{17,1},{25,9},{2,18},{10... | collective-permute-start | bytes 294920 | tf_op jit(solution)/shard_map/ppermute | solution.py:23
  16.4 2.8 %shard_map.58 = (bf16[1024,1024]{1,0:T(8,128)(2,1)S(1)}, bf16[1024,512]{1,0:T(8,128)(2,1)S(1)}, f32[8,1024]{1,0:T(8,128)S(1)}) custom-call(s32[4,8]{1,0:T(4,128)S(1)} %copy-done.5, s32[4,256]{1,0:T(4,128)S(1)} %copy-done.4, bf16[1024,512]{1,0:T(8,128)(2,1)S(1)} %copy-done.1), custom_call_target="tpu_custom_call" | custom-call | flops 1000 | bytes 1000 | tf_op jit(solution)/shard_map/pallas_call | solution.py:340
  19.2 0.3 collective-permute-done.2.refs_3_
  19.5 0.7 %shard_map.59 = bf16[32,1536]{1,0:T(8,128)(2,1)S(1)} custom-call(s32[4,256]{1,0:T(4,128)S(1)} %copy-done.4, bf16[32,1536]{1,0:T(8,128)(2,1)S(1)} %shard_map.56.refs_1_, bf16[32,1536]{1,0:T(8,128)(2,1)S(1)} %collective-permute-done.1.refs_2_, bf16[32,1536]{1,0:T(8,128)(2,1)S(1)} %collective-permute-done.2.refs_3_), custom_call_target="tpu_custom_call" | custom-call | flops 1000 | bytes 1000 | tf_op jit(solution)/shard_map/pallas_call | solution.py:340
  20.5 0.7 %collective-permute-start.8 = (bf16[32,1536]{1,0:T(8,128)(2,1)S(1)}, bf16[32,1536]{1,0:T(8,128)(2,1)S(1)}, u32[]{:S(2)}, u32[]{:S(2)}) collective-permute-start(bf16[32,1536]{1,0:T(8,128)(2,1)S(1)} %shard_map.59), channel_id=1, source_target_pairs={{0,2},{1,3},{2,0},{3,1},{4,6},{5,7},{6,4},{7,5},{8,10},{9,11},{10,... | collective-permute-start | bytes 294920 | tf_op jit(solution)/shard_map/ppermute | solution.py:23
  21.2 0.3 collective-permute-done.4.refs_15_
  21.5 1.9 %shard_map.60 = bf16[512,512]{1,0:T(8,128)(2,1)S(1)} custom-call(s32[4,256]{1,0:T(4,128)S(1)} %copy-done.4, bf16[1024,512]{1,0:T(8,128)(2,1)S(1)} %shard_map.55.refs_1_, bf16[1024,512]{1,0:T(8,128)(2,1)S(1)} %collective-permute-done.refs_2_), custom_call_target="tpu_custom_call" | custom-call | flops 1000 | bytes 1000 | tf_op jit(solution)/shard_map/pallas_call | solution.py:340
  23.5 3.2 %collective-permute-start.12 = (bf16[32,1536]{1,0:T(8,128)(2,1)S(1)}, bf16[32,1536]{1,0:T(8,128)(2,1)S(1)}, u32[]{:S(2)}, u32[]{:S(2)}) collective-permute-start(bf16[32,1536]{1,0:T(8,128)(2,1)S(1)} %shard_map.59), channel_id=1, source_target_pairs={{0,4},{1,5},{2,6},{3,7},{4,0},{5,1},{6,2},{7,3},{8,12},{9,13},{10,... | collective-permute-start | bytes 294920 | tf_op jit(solution)/shard_map/ppermute | solution.py:23
  26.7 1.7 %collective-permute-start.5 = (bf16[512,512]{1,0:T(8,128)(2,1)S(1)}, bf16[512,512]{1,0:T(8,128)(2,1)S(1)}, u32[]{:S(2)}, u32[]{:S(2)}) collective-permute-start(bf16[512,512]{1,0:T(8,128)(2,1)S(1)} %shard_map.60), channel_id=1, source_target_pairs={{0,16},{8,24},{16,0},{24,8},{1,17},{9,25},{17,1},{25,9},{2,18},{10... | collective-permute-start | bytes 1572872 | tf_op jit(solution)/shard_map/ppermute | solution.py:23
  28.5 0.5 collective-permute-start.7
  29.0 2.0 %collective-permute-start.9 = (bf16[4,32,1024]{2,1,0:T(8,128)(2,1)S(1)}, bf16[4,32,1024]{2,1,0:T(8,128)(2,1)S(1)}, u32[]{:S(2)}, u32[]{:S(2)}) collective-permute-start(bf16[4,32,1024]{2,1,0:T(8,128)(2,1)S(1)} %collective-permute-done.3.refs_12_), channel_id=1, source_target_pairs={{0,2},{1,3},{2,0},{3,1},{4,6},{5,7},{6,4},{7,5},{8,10},{9,11},{10,... | collective-permute-start | bytes 786440 | tf_op jit(solution)/shard_map/ppermute | solution.py:23
  31.0 0.4 collective-permute-done.12
  31.5 1.1 %collective-permute-start.13 = (bf16[128,1536]{1,0:T(8,128)(2,1)S(1)}, bf16[128,1536]{1,0:T(8,128)(2,1)S(1)}, u32[]{:S(2)}, u32[]{:S(2)}) collective-permute-start(bf16[128,1536]{1,0:T(8,128)(2,1)S(1)} %pad_maximum_fusion.refs_6_), channel_id=1, source_target_pairs={{0,1},{1,0},{2,3},{3,2},{4,5},{5,4},{6,7},{7,6},{8,9},{9,8},{10,11... | collective-permute-start | bytes 1179656 | tf_op jit(solution)/shard_map/ppermute | solution.py:23
  32.6 2.4 %collective-permute-start.15 = (bf16[4,32,1024]{2,1,0:T(8,128)(2,1)S(1)}, bf16[4,32,1024]{2,1,0:T(8,128)(2,1)S(1)}, u32[]{:S(2)}, u32[]{:S(2)}) collective-permute-start(bf16[4,32,1024]{2,1,0:T(8,128)(2,1)S(1)} %copy-done.2), channel_id=1, source_target_pairs={{0,6},{1,7},{2,4},{3,5},{4,2},{5,3},{6,0},{7,1},{8,14},{9,15},{10,... | collective-permute-start | bytes 786440 | tf_op jit(solution)/shard_map/ppermute | solution.py:23
  35.0 2.3 %collective-permute-done.7.refs_16_ = bf16[4,32,1024]{2,1,0:T(8,128)(2,1)S(1)} collective-permute-done((bf16[4,32,1024]{2,1,0:T(8,128)(2,1)S(1)}, bf16[4,32,1024]{2,1,0:T(8,128)(2,1)S(1)}, u32[]{:S(2)}, u32[]{:S(2)}) %collective-permute-start.7) | collective-permute-done | bytes 262176 | tf_op jit(solution)/shard_map/ppermute | solution.py:23
  37.4 5.3 %collective-permute-done.9.refs_14_ = bf16[4,32,1024]{2,1,0:T(8,128)(2,1)S(1)} collective-permute-done((bf16[4,32,1024]{2,1,0:T(8,128)(2,1)S(1)}, bf16[4,32,1024]{2,1,0:T(8,128)(2,1)S(1)}, u32[]{:S(2)}, u32[]{:S(2)}) %collective-permute-start.9) | collective-permute-done | bytes 262176 | tf_op jit(solution)/shard_map/ppermute | solution.py:23
  42.6 0.5 collective-permute-start.14
  43.3 0.9 %collective-permute-start.17 = (bf16[4,32,1024]{2,1,0:T(8,128)(2,1)S(1)}, bf16[4,32,1024]{2,1,0:T(8,128)(2,1)S(1)}, u32[]{:S(2)}, u32[]{:S(2)}) collective-permute-start(bf16[4,32,1024]{2,1,0:T(8,128)(2,1)S(1)} %collective-permute-done.15.refs_17_), channel_id=1, source_target_pairs={{0,1},{1,0},{2,3},{3,2},{4,5},{5,4},{6,7},{7,6},{8,9},{9,8},{10,11... | collective-permute-start | bytes 786440 | tf_op jit(solution)/shard_map/ppermute | solution.py:23
  44.2 0.4 collective-permute-done.10.refs_4_
  44.5 1.9 %shard_map.61 = (bf16[1024,512]{1,0:T(8,128)(2,1)S(1)}, bf16[1024,512]{1,0:T(8,128)(2,1)S(1)}) custom-call(s32[4,256]{1,0:T(4,128)S(1)} %copy-done.4, bf16[1024,512]{1,0:T(8,128)(2,1)S(1)} %shard_map.55.refs_1_, bf16[1024,512]{1,0:T(8,128)(2,1)S(1)} %collective-permute-done.refs_2_, bf16[512,512]{1,0:T(8,128)(2,1)S(1)} %collective-permute-done.5.refs_3_, ...), custom_call_target="tpu_custom_call" | custom-call | flops 1000 | bytes 1000 | tf_op jit(solution)/shard_map/pallas_call | solution.py:340
  46.5 2.2 %shard_map.62 = (bf16[1024,512]{1,0:T(8,128)(2,1)S(1)}, f32[1024,512]{1,0:T(8,128)S(1)}) custom-call(s32[4,256]{1,0:T(4,128)S(1)} %copy-done.4, bf16[1024,512]{1,0:T(8,128)(2,1)S(1)} %get-tuple-element.28.refs_1_, bf16[1024,512]{1,0:T(8,128)(2,1)S(1)} %get-tuple-element.29.refs_2_, bf16[1024,1024]{1,0:T(8,128)(2,1)S(1)} %get-tuple-element.30.refs_3_, ...), custom_call_target="tpu_custom_call" | custom-call | flops 1000 | bytes 1000 | tf_op jit(solution)/shard_map/pallas_call | solution.py:340
  48.7 3.3 %collective-permute-done.17.last = bf16[4,32,1024]{2,1,0:T(8,128)(2,1)S(1)} collective-permute-done((bf16[4,32,1024]{2,1,0:T(8,128)(2,1)S(1)}, bf16[4,32,1024]{2,1,0:T(8,128)(2,1)S(1)}, u32[]{:S(2)}, u32[]{:S(2)}) %collective-permute-start.17) | collective-permute-done | bytes 262176 | tf_op jit(solution)/shard_map/ppermute | solution.py:23
  52.0 1.5 %shard_map.63 = bf16[1024,512]{1,0:T(8,128)(2,1)} custom-call(f32[1024,512]{1,0:T(8,128)S(1)} %get-tuple-element.35.base, f32[8,1024]{1,0:T(8,128)S(1)} %get-tuple-element.22.refs_10_.weight, bf16[1024,512]{1,0:T(8,128)(2,1)S(1)} %get-tuple-element.36.mix, bf16[4,32,1024]{2,1,0:T(8,128)(2,1)S(1)} %collective-permute-done.17.last), custom_call_target="tpu_custom_call" | custom-call | flops 1000 | bytes 1000 | tf_op jit(solution)/shard_map/pallas_call | solution.py:444
  (26 shorter events, 0.8 us)
Async XLA Ops:
  0.0 1.2 %copy-start = (bf16[1024,512]{1,0:T(8,128)(2,1)S(1)}, bf16[1024,512]{1,0:T(8,128)(2,1)}, u32[]{:S(2)}) copy-start(bf16[1024,512]{1,0:T(8,128)(2,1)} %refs_2_.3) | copy-start | bytes 3145732
  1.2 0.7 %copy-start.4 = (s32[4,256]{1,0:T(4,128)S(1)}, s32[4,256]{1,0:T(4,128)}, u32[]{:S(2)}) copy-start(s32[4,256]{1,0:T(4,128)} %refs_0_.14) | copy-start | bytes 12292
  1.9 2.6 %copy-start.2 = (bf16[4,32,1024]{2,1,0:T(8,128)(2,1)S(1)}, bf16[4,32,1024]{2,1,0:T(8,128)(2,1)}, u32[]{:S(2)}) copy-start(bf16[4,32,1024]{2,1,0:T(8,128)(2,1)} %refs_11_.1) | copy-start | bytes 786436
  1.9 9.1 %copy-start.5 = (s32[4,8]{1,0:T(4,128)S(1)}, s32[4,8]{1,0:T(4,128)}, u32[]{:S(2)}) copy-start(s32[4,8]{1,0:T(4,128)} %refs_0_.10) | copy-start | bytes 388
  1.9 14.5 %copy-start.1 = (bf16[1024,512]{1,0:T(8,128)(2,1)S(1)}, bf16[1024,512]{1,0:T(8,128)(2,1)}, u32[]{:S(2)}) copy-start(bf16[1024,512]{1,0:T(8,128)(2,1)} %refs_2_.3) | copy-start | bytes 3145732
  2.1 19.4 %collective-permute-start = (bf16[1024,512]{1,0:T(8,128)(2,1)S(1)}, bf16[1024,512]{1,0:T(8,128)(2,1)S(1)}, u32[]{:S(2)}, u32[]{:S(2)}) collective-permute-start(bf16[1024,512]{1,0:T(8,128)(2,1)S(1)} %shard_map.55.refs_1_), channel_id=1, source_target_pairs={{0,8},{8,0},{16,24},{24,16},{1,9},{9,1},{17,25},{25,17},{2,10},{10... | collective-permute-start | bytes 3145736 | tf_op jit(solution)/shard_map/ppermute | solution.py:23
  4.6 14.9 %collective-permute-start.3 = (bf16[4,32,1024]{2,1,0:T(8,128)(2,1)S(1)}, bf16[4,32,1024]{2,1,0:T(8,128)(2,1)S(1)}, u32[]{:S(2)}, u32[]{:S(2)}) collective-permute-start(bf16[4,32,1024]{2,1,0:T(8,128)(2,1)S(1)} %copy-done.2), channel_id=1, source_target_pairs={{0,1},{1,0},{2,3},{3,2},{4,5},{5,4},{6,7},{7,6},{8,9},{9,8},{10,11... | collective-permute-start | bytes 786440 | tf_op jit(solution)/shard_map/ppermute | solution.py:23
  6.9 14.6 %collective-permute-start.4 = (bf16[4,32,1024]{2,1,0:T(8,128)(2,1)S(1)}, bf16[4,32,1024]{2,1,0:T(8,128)(2,1)S(1)}, u32[]{:S(2)}, u32[]{:S(2)}) collective-permute-start(bf16[4,32,1024]{2,1,0:T(8,128)(2,1)S(1)} %copy-done.2), channel_id=1, source_target_pairs={{0,4},{1,5},{2,6},{3,7},{4,0},{5,1},{6,2},{7,3},{8,12},{9,13},{10,... | collective-permute-start | bytes 786440 | tf_op jit(solution)/shard_map/ppermute | solution.py:23
  9.5 14.0 %collective-permute-start.11 = (bf16[4,32,1024]{2,1,0:T(8,128)(2,1)S(1)}, bf16[4,32,1024]{2,1,0:T(8,128)(2,1)S(1)}, u32[]{:S(2)}, u32[]{:S(2)}) collective-permute-start(bf16[4,32,1024]{2,1,0:T(8,128)(2,1)S(1)} %copy-done.2), channel_id=1, source_target_pairs={{0,2},{1,3},{2,0},{3,1},{4,6},{5,7},{6,4},{7,5},{8,10},{9,11},{10,... | collective-permute-start | bytes 786440 | tf_op jit(solution)/shard_map/ppermute | solution.py:23
  12.4 1.4 %collective-permute-start.1 = (bf16[32,1536]{1,0:T(8,128)(2,1)S(1)}, bf16[32,1536]{1,0:T(8,128)(2,1)S(1)}, u32[]{:S(2)}, u32[]{:S(2)}) collective-permute-start(bf16[32,1536]{1,0:T(8,128)(2,1)S(1)} %shard_map.56.refs_1_), channel_id=1, source_target_pairs={{0,8},{8,0},{16,24},{24,16},{1,9},{9,1},{17,25},{25,17},{2,10},{10... | collective-permute-start | bytes 294920 | tf_op jit(solution)/shard_map/ppermute | solution.py:23
  14.5 4.9 %collective-permute-start.2 = (bf16[32,1536]{1,0:T(8,128)(2,1)S(1)}, bf16[32,1536]{1,0:T(8,128)(2,1)S(1)}, u32[]{:S(2)}, u32[]{:S(2)}) collective-permute-start(bf16[32,1536]{1,0:T(8,128)(2,1)S(1)} %shard_map.57), channel_id=1, source_target_pairs={{0,16},{8,24},{16,0},{24,8},{1,17},{9,25},{17,1},{25,9},{2,18},{10... | collective-permute-start | bytes 294920 | tf_op jit(solution)/shard_map/ppermute | solution.py:23
  20.2 8.2 %collective-permute-start.6 = (bf16[32,1536]{1,0:T(8,128)(2,1)S(1)}, bf16[32,1536]{1,0:T(8,128)(2,1)S(1)}, u32[]{:S(2)}, u32[]{:S(2)}) collective-permute-start(bf16[32,1536]{1,0:T(8,128)(2,1)S(1)} %shard_map.59), channel_id=1, source_target_pairs={{0,6},{1,7},{2,4},{3,5},{4,2},{5,3},{6,0},{7,1},{8,14},{9,15},{10,... | collective-permute-start | bytes 294920 | tf_op jit(solution)/shard_map/ppermute | solution.py:23
  20.5 8.5 %collective-permute-start.8 = (bf16[32,1536]{1,0:T(8,128)(2,1)S(1)}, bf16[32,1536]{1,0:T(8,128)(2,1)S(1)}, u32[]{:S(2)}, u32[]{:S(2)}) collective-permute-start(bf16[32,1536]{1,0:T(8,128)(2,1)S(1)} %shard_map.59), channel_id=1, source_target_pairs={{0,2},{1,3},{2,0},{3,1},{4,6},{5,7},{6,4},{7,5},{8,10},{9,11},{10,... | collective-permute-start | bytes 294920 | tf_op jit(solution)/shard_map/ppermute | solution.py:23
  23.5 23.0 %copy-start.3 = (bf16[4,256,256]{2,1,0:T(8,128)(2,1)S(1)}, bf16[4,256,256]{2,1,0:T(8,128)(2,1)}, u32[]{:S(2)}) copy-start(bf16[4,256,256]{2,1,0:T(8,128)(2,1)} %refs_5_.1) | copy-start | bytes 1572868
  23.5 8.0 %collective-permute-start.12 = (bf16[32,1536]{1,0:T(8,128)(2,1)S(1)}, bf16[32,1536]{1,0:T(8,128)(2,1)S(1)}, u32[]{:S(2)}, u32[]{:S(2)}) collective-permute-start(bf16[32,1536]{1,0:T(8,128)(2,1)S(1)} %shard_map.59), channel_id=1, source_target_pairs={{0,4},{1,5},{2,6},{3,7},{4,0},{5,1},{6,2},{7,3},{8,12},{9,13},{10,... | collective-permute-start | bytes 294920 | tf_op jit(solution)/shard_map/ppermute | solution.py:23
  26.7 15.9 %collective-permute-start.5 = (bf16[512,512]{1,0:T(8,128)(2,1)S(1)}, bf16[512,512]{1,0:T(8,128)(2,1)S(1)}, u32[]{:S(2)}, u32[]{:S(2)}) collective-permute-start(bf16[512,512]{1,0:T(8,128)(2,1)S(1)} %shard_map.60), channel_id=1, source_target_pairs={{0,16},{8,24},{16,0},{24,8},{1,17},{9,25},{17,1},{25,9},{2,18},{10... | collective-permute-start | bytes 1572872 | tf_op jit(solution)/shard_map/ppermute | solution.py:23
  28.5 8.9 %collective-permute-start.7 = (bf16[4,32,1024]{2,1,0:T(8,128)(2,1)S(1)}, bf16[4,32,1024]{2,1,0:T(8,128)(2,1)S(1)}, u32[]{:S(2)}, u32[]{:S(2)}) collective-permute-start(bf16[4,32,1024]{2,1,0:T(8,128)(2,1)S(1)} %collective-permute-done.4.refs_15_), channel_id=1, source_target_pairs={{0,1},{1,0},{2,3},{3,2},{4,5},{5,4},{6,7},{7,6},{8,9},{9,8},{10,11... | collective-permute-start | bytes 786440 | tf_op jit(solution)/shard_map/ppermute | solution.py:23
  29.0 13.6 %collective-permute-start.9 = (bf16[4,32,1024]{2,1,0:T(8,128)(2,1)S(1)}, bf16[4,32,1024]{2,1,0:T(8,128)(2,1)S(1)}, u32[]{:S(2)}, u32[]{:S(2)}) collective-permute-start(bf16[4,32,1024]{2,1,0:T(8,128)(2,1)S(1)} %collective-permute-done.3.refs_12_), channel_id=1, source_target_pairs={{0,2},{1,3},{2,0},{3,1},{4,6},{5,7},{6,4},{7,5},{8,10},{9,11},{10,... | collective-permute-start | bytes 786440 | tf_op jit(solution)/shard_map/ppermute | solution.py:23
  31.5 11.8 %collective-permute-start.13 = (bf16[128,1536]{1,0:T(8,128)(2,1)S(1)}, bf16[128,1536]{1,0:T(8,128)(2,1)S(1)}, u32[]{:S(2)}, u32[]{:S(2)}) collective-permute-start(bf16[128,1536]{1,0:T(8,128)(2,1)S(1)} %pad_maximum_fusion.refs_6_), channel_id=1, source_target_pairs={{0,1},{1,0},{2,3},{3,2},{4,5},{5,4},{6,7},{7,6},{8,9},{9,8},{10,11... | collective-permute-start | bytes 1179656 | tf_op jit(solution)/shard_map/ppermute | solution.py:23
  32.6 10.6 %collective-permute-start.15 = (bf16[4,32,1024]{2,1,0:T(8,128)(2,1)S(1)}, bf16[4,32,1024]{2,1,0:T(8,128)(2,1)S(1)}, u32[]{:S(2)}, u32[]{:S(2)}) collective-permute-start(bf16[4,32,1024]{2,1,0:T(8,128)(2,1)S(1)} %copy-done.2), channel_id=1, source_target_pairs={{0,6},{1,7},{2,4},{3,5},{4,2},{5,3},{6,0},{7,1},{8,14},{9,15},{10,... | collective-permute-start | bytes 786440 | tf_op jit(solution)/shard_map/ppermute | solution.py:23
  42.6 1.9 %collective-permute-start.10 = (bf16[512,512]{1,0:T(8,128)(2,1)S(1)}, bf16[512,512]{1,0:T(8,128)(2,1)S(1)}, u32[]{:S(2)}, u32[]{:S(2)}) collective-permute-start(bf16[512,512]{1,0:T(8,128)(2,1)S(1)} %collective-permute-done.5.refs_3_), channel_id=1, source_target_pairs={{0,8},{8,0},{16,24},{24,16},{1,9},{9,1},{17,25},{25,17},{2,10},{10... | collective-permute-start | bytes 1572872 | tf_op jit(solution)/shard_map/ppermute | solution.py:23
  42.6 3.8 %collective-permute-start.14 = (bf16[128,1536]{1,0:T(8,128)(2,1)S(1)}, bf16[128,1536]{1,0:T(8,128)(2,1)S(1)}, u32[]{:S(2)}, u32[]{:S(2)}) collective-permute-start(bf16[128,1536]{1,0:T(8,128)(2,1)S(1)} %pad_maximum_fusion.refs_6_), channel_id=1, source_target_pairs={{0,8},{8,0},{16,24},{24,16},{1,9},{9,1},{17,25},{25,17},{2,10},{10... | collective-permute-start | bytes 1179656 | tf_op jit(solution)/shard_map/ppermute | solution.py:23
  43.3 3.2 %collective-permute-start.16 = (bf16[128,1536]{1,0:T(8,128)(2,1)S(1)}, bf16[128,1536]{1,0:T(8,128)(2,1)S(1)}, u32[]{:S(2)}, u32[]{:S(2)}) collective-permute-start(bf16[128,1536]{1,0:T(8,128)(2,1)S(1)} %collective-permute-done.13.refs_7_), channel_id=1, source_target_pairs={{0,8},{8,0},{16,24},{24,16},{1,9},{9,1},{17,25},{25,17},{2,10},{10... | collective-permute-start | bytes 1179656 | tf_op jit(solution)/shard_map/ppermute | solution.py:23
  43.3 8.7 %collective-permute-start.17 = (bf16[4,32,1024]{2,1,0:T(8,128)(2,1)S(1)}, bf16[4,32,1024]{2,1,0:T(8,128)(2,1)S(1)}, u32[]{:S(2)}, u32[]{:S(2)}) collective-permute-start(bf16[4,32,1024]{2,1,0:T(8,128)(2,1)S(1)} %collective-permute-done.15.refs_17_), channel_id=1, source_target_pairs={{0,1},{1,0},{2,3},{3,2},{4,5},{5,4},{6,7},{7,6},{8,9},{9,8},{10,11... | collective-permute-start | bytes 786440 | tf_op jit(solution)/shard_map/ppermute | solution.py:23

commit v7 on v6

--- a/solution.py
+++ b/solution.py
@@ -418,13 +418,13 @@
             sz2 = swap(after(own, message, bz1), "pcol", 8, 4)
             sz3 = swap(own, "pcol", 8, 6)
             sz1 = swap(own, "pcol", 8, 2)
-            bz3 = swap(after(panels, bz2, sz2), "pcol", 8, 6)
+            bz3 = swap(after(panels, bz2, sz1), "pcol", 8, 6)
             line = jnp.concatenate([own, sz1, sz2, sz3], axis=0)
             cross = swap(line, "pcol", 8, 1)
             bz2x = swap(after(bz2, sz3), "pcol", 8, 1)
             bz3x = swap(bz3, "pcol", 8, 1)
             line_other = swap(line, "prow", 4, 1)
-            bz1x = swap(after(bx0, sz1), "pcol", 8, 2)
+            bz1x = swap(after(bx0, sz3), "pcol", 8, 2)
             rest = swap(after(came, bz2x, bz1x), "prow", 4, 1)
             bulk = [panels, bx0, bz1, bz1x, bz2, bz2x, bz3, bz3x]
             cross_other = swap(after(cross, bz3), "prow", 4, 1)

time: 53.7 us -> 53.7 us (level)
  no operation moved by 1% of the time
where the time goes in v7:
time: 53.7 us; the launch traced here: 53.5 us
  starting transfers between devices  24.3 us (45%)
  waiting for transfers between devices  13.8 us (26%)
  Pallas kernels  13.3 us (25%)
  local copies, waits for them, and re-layouts  1.93 us (4%)
    ppermute x18, starting transfers between devices, swap(): return lax.ppermute(value, axis, [(i, i ^ mask) for i in range(size)])  24.3 us
    ppermute x18, waiting for transfers between devices, swap(): return lax.ppermute(value, axis, [(i, i ^ mask) for i in range(size)])  13.8 us
    pallas_call x8, Pallas kernels, call(): pl.pallas_call(body, out_shape=shapes, in_specs=[SMEM] * n_smem + [VMEM]...  11.8 us
    unnamed x12, local copies, waits for them, and re-layouts  1.93 us
    pallas_call x1, Pallas kernels, on_device(): pl.pallas_call(update_kernel, out_shape=bf(row_dev, columns), grid=(row_d...  1.46 us
  transfers between devices with their start and end apart: 18, of which 9 were waited for; matrix products, arithmetic and copies ran while one was open for 0% of the time, Pallas kernels for 22%

profile of v7, /device:TPU:0, one launch (start us, length us, event | category | flops | bytes accessed | tf_op | source)
XLA Modules:
  0.0 53.5 jit_solution(10841873263326207464)
XLA Ops:
  0.0 1.2 %copy-done = bf16[1024,512]{1,0:T(8,128)(2,1)S(1)} copy-done((bf16[1024,512]{1,0:T(8,128)(2,1)S(1)}, bf16[1024,512]{1,0:T(8,128)(2,1)}, u32[]{:S(2)}) %copy-start) | copy-done | bytes 1048600
  1.2 0.7 %copy-done.4 = s32[4,256]{1,0:T(4,128)S(1)} copy-done((s32[4,256]{1,0:T(4,128)S(1)}, s32[4,256]{1,0:T(4,128)}, u32[]{:S(2)}) %copy-start.4) | copy-done | bytes 4120
  2.1 2.4 %collective-permute-start = (bf16[1024,512]{1,0:T(8,128)(2,1)S(1)}, bf16[1024,512]{1,0:T(8,128)(2,1)S(1)}, u32[]{:S(2)}, u32[]{:S(2)}) collective-permute-start(bf16[1024,512]{1,0:T(8,128)(2,1)S(1)} %shard_map.55.refs_1_), channel_id=1, source_target_pairs={{0,8},{8,0},{16,24},{24,16},{1,9},{9,1},{17,25},{25,17},{2,10},{10... | collective-permute-start | bytes 3145736 | tf_op jit(solution)/shard_map/ppermute | solution.py:23
  4.6 2.3 %collective-permute-start.3 = (bf16[4,32,1024]{2,1,0:T(8,128)(2,1)S(1)}, bf16[4,32,1024]{2,1,0:T(8,128)(2,1)S(1)}, u32[]{:S(2)}, u32[]{:S(2)}) collective-permute-start(bf16[4,32,1024]{2,1,0:T(8,128)(2,1)S(1)} %copy-done.2), channel_id=1, source_target_pairs={{0,1},{1,0},{2,3},{3,2},{4,5},{5,4},{6,7},{7,6},{8,9},{9,8},{10,11... | collective-permute-start | bytes 786440 | tf_op jit(solution)/shard_map/ppermute | solution.py:23
  6.9 2.6 %collective-permute-start.4 = (bf16[4,32,1024]{2,1,0:T(8,128)(2,1)S(1)}, bf16[4,32,1024]{2,1,0:T(8,128)(2,1)S(1)}, u32[]{:S(2)}, u32[]{:S(2)}) collective-permute-start(bf16[4,32,1024]{2,1,0:T(8,128)(2,1)S(1)} %copy-done.2), channel_id=1, source_target_pairs={{0,4},{1,5},{2,6},{3,7},{4,0},{5,1},{6,2},{7,3},{8,12},{9,13},{10,... | collective-permute-start | bytes 786440 | tf_op jit(solution)/shard_map/ppermute | solution.py:23
  9.5 1.6 %collective-permute-start.11 = (bf16[4,32,1024]{2,1,0:T(8,128)(2,1)S(1)}, bf16[4,32,1024]{2,1,0:T(8,128)(2,1)S(1)}, u32[]{:S(2)}, u32[]{:S(2)}) collective-permute-start(bf16[4,32,1024]{2,1,0:T(8,128)(2,1)S(1)} %copy-done.2), channel_id=1, source_target_pairs={{0,2},{1,3},{2,0},{3,1},{4,6},{5,7},{6,4},{7,5},{8,10},{9,11},{10,... | collective-permute-start | bytes 786440 | tf_op jit(solution)/shard_map/ppermute | solution.py:23
  11.0 1.4 %shard_map.56.refs_1_ = bf16[32,1536]{1,0:T(8,128)(2,1)S(1)} custom-call(s32[4,8]{1,0:T(4,128)S(1)} %copy-done.5, s32[4,256]{1,0:T(4,128)S(1)} %copy-done.4, bf16[4,32,1024]{2,1,0:T(8,128)(2,1)S(1)} %copy-done.2), custom_call_target="tpu_custom_call" | custom-call | flops 1000 | bytes 1000 | tf_op jit(solution)/shard_map/pallas_call | solution.py:340
  12.5 1.3 %collective-permute-done.1.refs_2_ = bf16[32,1536]{1,0:T(8,128)(2,1)S(1)} collective-permute-done((bf16[32,1536]{1,0:T(8,128)(2,1)S(1)}, bf16[32,1536]{1,0:T(8,128)(2,1)S(1)}, u32[]{:S(2)}, u32[]{:S(2)}) %collective-permute-start.1) | collective-permute-done | bytes 98336 | tf_op jit(solution)/shard_map/ppermute | solution.py:23
  13.8 0.7 %shard_map.57 = bf16[32,1536]{1,0:T(8,128)(2,1)S(1)} custom-call(s32[4,256]{1,0:T(4,128)S(1)} %copy-done.4, bf16[32,1536]{1,0:T(8,128)(2,1)S(1)} %shard_map.56.refs_1_, bf16[32,1536]{1,0:T(8,128)(2,1)S(1)} %collective-permute-done.1.refs_2_), custom_call_target="tpu_custom_call" | custom-call | flops 1000 | bytes 1000 | tf_op jit(solution)/shard_map/pallas_call | solution.py:340
  14.5 1.8 %collective-permute-start.2 = (bf16[32,1536]{1,0:T(8,128)(2,1)S(1)}, bf16[32,1536]{1,0:T(8,128)(2,1)S(1)}, u32[]{:S(2)}, u32[]{:S(2)}) collective-permute-start(bf16[32,1536]{1,0:T(8,128)(2,1)S(1)} %shard_map.57), channel_id=1, source_target_pairs={{0,16},{8,24},{16,0},{24,8},{1,17},{9,25},{17,1},{25,9},{2,18},{10... | collective-permute-start | bytes 294920 | tf_op jit(solution)/shard_map/ppermute | solution.py:23
  16.4 2.8 %shard_map.58 = (bf16[1024,1024]{1,0:T(8,128)(2,1)S(1)}, bf16[1024,512]{1,0:T(8,128)(2,1)S(1)}, f32[8,1024]{1,0:T(8,128)S(1)}) custom-call(s32[4,8]{1,0:T(4,128)S(1)} %copy-done.5, s32[4,256]{1,0:T(4,128)S(1)} %copy-done.4, bf16[1024,512]{1,0:T(8,128)(2,1)S(1)} %copy-done.1), custom_call_target="tpu_custom_call" | custom-call | flops 1000 | bytes 1000 | tf_op jit(solution)/shard_map/pallas_call | solution.py:340
  19.2 0.3 collective-permute-done.2.refs_3_
  19.5 0.7 %shard_map.59 = bf16[32,1536]{1,0:T(8,128)(2,1)S(1)} custom-call(s32[4,256]{1,0:T(4,128)S(1)} %copy-done.4, bf16[32,1536]{1,0:T(8,128)(2,1)S(1)} %shard_map.56.refs_1_, bf16[32,1536]{1,0:T(8,128)(2,1)S(1)} %collective-permute-done.1.refs_2_, bf16[32,1536]{1,0:T(8,128)(2,1)S(1)} %collective-permute-done.2.refs_3_), custom_call_target="tpu_custom_call" | custom-call | flops 1000 | bytes 1000 | tf_op jit(solution)/shard_map/pallas_call | solution.py:340
  20.5 0.7 %collective-permute-start.10 = (bf16[32,1536]{1,0:T(8,128)(2,1)S(1)}, bf16[32,1536]{1,0:T(8,128)(2,1)S(1)}, u32[]{:S(2)}, u32[]{:S(2)}) collective-permute-start(bf16[32,1536]{1,0:T(8,128)(2,1)S(1)} %shard_map.59), channel_id=1, source_target_pairs={{0,2},{1,3},{2,0},{3,1},{4,6},{5,7},{6,4},{7,5},{8,10},{9,11},{10,... | collective-permute-start | bytes 294920 | tf_op jit(solution)/shard_map/ppermute | solution.py:23
  21.2 0.3 collective-permute-done.4.refs_15_
  21.5 1.9 %shard_map.60 = bf16[512,512]{1,0:T(8,128)(2,1)S(1)} custom-call(s32[4,256]{1,0:T(4,128)S(1)} %copy-done.4, bf16[1024,512]{1,0:T(8,128)(2,1)S(1)} %shard_map.55.refs_1_, bf16[1024,512]{1,0:T(8,128)(2,1)S(1)} %collective-permute-done.refs_2_), custom_call_target="tpu_custom_call" | custom-call | flops 1000 | bytes 1000 | tf_op jit(solution)/shard_map/pallas_call | solution.py:340
  23.5 3.2 %collective-permute-start.12 = (bf16[32,1536]{1,0:T(8,128)(2,1)S(1)}, bf16[32,1536]{1,0:T(8,128)(2,1)S(1)}, u32[]{:S(2)}, u32[]{:S(2)}) collective-permute-start(bf16[32,1536]{1,0:T(8,128)(2,1)S(1)} %shard_map.59), channel_id=1, source_target_pairs={{0,4},{1,5},{2,6},{3,7},{4,0},{5,1},{6,2},{7,3},{8,12},{9,13},{10,... | collective-permute-start | bytes 294920 | tf_op jit(solution)/shard_map/ppermute | solution.py:23
  26.7 1.7 %collective-permute-start.5 = (bf16[512,512]{1,0:T(8,128)(2,1)S(1)}, bf16[512,512]{1,0:T(8,128)(2,1)S(1)}, u32[]{:S(2)}, u32[]{:S(2)}) collective-permute-start(bf16[512,512]{1,0:T(8,128)(2,1)S(1)} %shard_map.60), channel_id=1, source_target_pairs={{0,16},{8,24},{16,0},{24,8},{1,17},{9,25},{17,1},{25,9},{2,18},{10... | collective-permute-start | bytes 1572872 | tf_op jit(solution)/shard_map/ppermute | solution.py:23
  28.5 0.5 collective-permute-start.7
  29.0 2.0 %collective-permute-start.8 = (bf16[4,32,1024]{2,1,0:T(8,128)(2,1)S(1)}, bf16[4,32,1024]{2,1,0:T(8,128)(2,1)S(1)}, u32[]{:S(2)}, u32[]{:S(2)}) collective-permute-start(bf16[4,32,1024]{2,1,0:T(8,128)(2,1)S(1)} %collective-permute-done.3.refs_12_), channel_id=1, source_target_pairs={{0,2},{1,3},{2,0},{3,1},{4,6},{5,7},{6,4},{7,5},{8,10},{9,11},{10,... | collective-permute-start | bytes 786440 | tf_op jit(solution)/shard_map/ppermute | solution.py:23
  31.0 0.4 collective-permute-done.12
  31.5 1.1 %collective-permute-start.13 = (bf16[128,1536]{1,0:T(8,128)(2,1)S(1)}, bf16[128,1536]{1,0:T(8,128)(2,1)S(1)}, u32[]{:S(2)}, u32[]{:S(2)}) collective-permute-start(bf16[128,1536]{1,0:T(8,128)(2,1)S(1)} %pad_maximum_fusion.refs_6_), channel_id=1, source_target_pairs={{0,1},{1,0},{2,3},{3,2},{4,5},{5,4},{6,7},{7,6},{8,9},{9,8},{10,11... | collective-permute-start | bytes 1179656 | tf_op jit(solution)/shard_map/ppermute | solution.py:23
  32.6 2.4 %collective-permute-start.15 = (bf16[4,32,1024]{2,1,0:T(8,128)(2,1)S(1)}, bf16[4,32,1024]{2,1,0:T(8,128)(2,1)S(1)}, u32[]{:S(2)}, u32[]{:S(2)}) collective-permute-start(bf16[4,32,1024]{2,1,0:T(8,128)(2,1)S(1)} %copy-done.2), channel_id=1, source_target_pairs={{0,6},{1,7},{2,4},{3,5},{4,2},{5,3},{6,0},{7,1},{8,14},{9,15},{10,... | collective-permute-start | bytes 786440 | tf_op jit(solution)/shard_map/ppermute | solution.py:23
  35.0 2.3 %collective-permute-done.7.refs_16_ = bf16[4,32,1024]{2,1,0:T(8,128)(2,1)S(1)} collective-permute-done((bf16[4,32,1024]{2,1,0:T(8,128)(2,1)S(1)}, bf16[4,32,1024]{2,1,0:T(8,128)(2,1)S(1)}, u32[]{:S(2)}, u32[]{:S(2)}) %collective-permute-start.7) | collective-permute-done | bytes 262176 | tf_op jit(solution)/shard_map/ppermute | solution.py:23
  37.4 5.3 %collective-permute-done.8.refs_14_ = bf16[4,32,1024]{2,1,0:T(8,128)(2,1)S(1)} collective-permute-done((bf16[4,32,1024]{2,1,0:T(8,128)(2,1)S(1)}, bf16[4,32,1024]{2,1,0:T(8,128)(2,1)S(1)}, u32[]{:S(2)}, u32[]{:S(2)}) %collective-permute-start.8) | collective-permute-done | bytes 262176 | tf_op jit(solution)/shard_map/ppermute | solution.py:23
  42.6 0.5 collective-permute-start.14
  43.3 0.9 %collective-permute-start.17 = (bf16[4,32,1024]{2,1,0:T(8,128)(2,1)S(1)}, bf16[4,32,1024]{2,1,0:T(8,128)(2,1)S(1)}, u32[]{:S(2)}, u32[]{:S(2)}) collective-permute-start(bf16[4,32,1024]{2,1,0:T(8,128)(2,1)S(1)} %collective-permute-done.15.refs_17_), channel_id=1, source_target_pairs={{0,1},{1,0},{2,3},{3,2},{4,5},{5,4},{6,7},{7,6},{8,9},{9,8},{10,11... | collective-permute-start | bytes 786440 | tf_op jit(solution)/shard_map/ppermute | solution.py:23
  44.2 0.4 collective-permute-done.9.refs_4_
  44.5 1.9 %shard_map.61 = (bf16[1024,512]{1,0:T(8,128)(2,1)S(1)}, bf16[1024,512]{1,0:T(8,128)(2,1)S(1)}) custom-call(s32[4,256]{1,0:T(4,128)S(1)} %copy-done.4, bf16[1024,512]{1,0:T(8,128)(2,1)S(1)} %shard_map.55.refs_1_, bf16[1024,512]{1,0:T(8,128)(2,1)S(1)} %collective-permute-done.refs_2_, bf16[512,512]{1,0:T(8,128)(2,1)S(1)} %collective-permute-done.5.refs_3_, ...), custom_call_target="tpu_custom_call" | custom-call | flops 1000 | bytes 1000 | tf_op jit(solution)/shard_map/pallas_call | solution.py:340
  46.5 2.2 %shard_map.62 = (bf16[1024,512]{1,0:T(8,128)(2,1)S(1)}, f32[1024,512]{1,0:T(8,128)S(1)}) custom-call(s32[4,256]{1,0:T(4,128)S(1)} %copy-done.4, bf16[1024,512]{1,0:T(8,128)(2,1)S(1)} %get-tuple-element.28.refs_1_, bf16[1024,512]{1,0:T(8,128)(2,1)S(1)} %get-tuple-element.29.refs_2_, bf16[1024,1024]{1,0:T(8,128)(2,1)S(1)} %get-tuple-element.30.refs_3_, ...), custom_call_target="tpu_custom_call" | custom-call | flops 1000 | bytes 1000 | tf_op jit(solution)/shard_map/pallas_call | solution.py:340
  48.7 3.3 %collective-permute-done.17.last = bf16[4,32,1024]{2,1,0:T(8,128)(2,1)S(1)} collective-permute-done((bf16[4,32,1024]{2,1,0:T(8,128)(2,1)S(1)}, bf16[4,32,1024]{2,1,0:T(8,128)(2,1)S(1)}, u32[]{:S(2)}, u32[]{:S(2)}) %collective-permute-start.17) | collective-permute-done | bytes 262176 | tf_op jit(solution)/shard_map/ppermute | solution.py:23
  52.0 1.5 %shard_map.63 = bf16[1024,512]{1,0:T(8,128)(2,1)} custom-call(f32[1024,512]{1,0:T(8,128)S(1)} %get-tuple-element.35.base, f32[8,1024]{1,0:T(8,128)S(1)} %get-tuple-element.22.refs_10_.weight, bf16[1024,512]{1,0:T(8,128)(2,1)S(1)} %get-tuple-element.36.mix, bf16[4,32,1024]{2,1,0:T(8,128)(2,1)S(1)} %collective-permute-done.17.last), custom_call_target="tpu_custom_call" | custom-call | flops 1000 | bytes 1000 | tf_op jit(solution)/shard_map/pallas_call | solution.py:444
  (26 shorter events, 0.8 us)
Async XLA Ops:
  0.0 1.2 %copy-start = (bf16[1024,512]{1,0:T(8,128)(2,1)S(1)}, bf16[1024,512]{1,0:T(8,128)(2,1)}, u32[]{:S(2)}) copy-start(bf16[1024,512]{1,0:T(8,128)(2,1)} %refs_2_.3) | copy-start | bytes 3145732
  1.2 0.7 %copy-start.4 = (s32[4,256]{1,0:T(4,128)S(1)}, s32[4,256]{1,0:T(4,128)}, u32[]{:S(2)}) copy-start(s32[4,256]{1,0:T(4,128)} %refs_0_.14) | copy-start | bytes 12292
  1.9 2.6 %copy-start.2 = (bf16[4,32,1024]{2,1,0:T(8,128)(2,1)S(1)}, bf16[4,32,1024]{2,1,0:T(8,128)(2,1)}, u32[]{:S(2)}) copy-start(bf16[4,32,1024]{2,1,0:T(8,128)(2,1)} %refs_11_.1) | copy-start | bytes 786436
  1.9 9.1 %copy-start.5 = (s32[4,8]{1,0:T(4,128)S(1)}, s32[4,8]{1,0:T(4,128)}, u32[]{:S(2)}) copy-start(s32[4,8]{1,0:T(4,128)} %refs_0_.10) | copy-start | bytes 388
  1.9 14.5 %copy-start.1 = (bf16[1024,512]{1,0:T(8,128)(2,1)S(1)}, bf16[1024,512]{1,0:T(8,128)(2,1)}, u32[]{:S(2)}) copy-start(bf16[1024,512]{1,0:T(8,128)(2,1)} %refs_2_.3) | copy-start | bytes 3145732
  2.1 19.4 %collective-permute-start = (bf16[1024,512]{1,0:T(8,128)(2,1)S(1)}, bf16[1024,512]{1,0:T(8,128)(2,1)S(1)}, u32[]{:S(2)}, u32[]{:S(2)}) collective-permute-start(bf16[1024,512]{1,0:T(8,128)(2,1)S(1)} %shard_map.55.refs_1_), channel_id=1, source_target_pairs={{0,8},{8,0},{16,24},{24,16},{1,9},{9,1},{17,25},{25,17},{2,10},{10... | collective-permute-start | bytes 3145736 | tf_op jit(solution)/shard_map/ppermute | solution.py:23
  4.6 14.9 %collective-permute-start.3 = (bf16[4,32,1024]{2,1,0:T(8,128)(2,1)S(1)}, bf16[4,32,1024]{2,1,0:T(8,128)(2,1)S(1)}, u32[]{:S(2)}, u32[]{:S(2)}) collective-permute-start(bf16[4,32,1024]{2,1,0:T(8,128)(2,1)S(1)} %copy-done.2), channel_id=1, source_target_pairs={{0,1},{1,0},{2,3},{3,2},{4,5},{5,4},{6,7},{7,6},{8,9},{9,8},{10,11... | collective-permute-start | bytes 786440 | tf_op jit(solution)/shard_map/ppermute | solution.py:23
  6.9 14.6 %collective-permute-start.4 = (bf16[4,32,1024]{2,1,0:T(8,128)(2,1)S(1)}, bf16[4,32,1024]{2,1,0:T(8,128)(2,1)S(1)}, u32[]{:S(2)}, u32[]{:S(2)}) collective-permute-start(bf16[4,32,1024]{2,1,0:T(8,128)(2,1)S(1)} %copy-done.2), channel_id=1, source_target_pairs={{0,4},{1,5},{2,6},{3,7},{4,0},{5,1},{6,2},{7,3},{8,12},{9,13},{10,... | collective-permute-start | bytes 786440 | tf_op jit(solution)/shard_map/ppermute | solution.py:23
  9.5 14.0 %collective-permute-start.11 = (bf16[4,32,1024]{2,1,0:T(8,128)(2,1)S(1)}, bf16[4,32,1024]{2,1,0:T(8,128)(2,1)S(1)}, u32[]{:S(2)}, u32[]{:S(2)}) collective-permute-start(bf16[4,32,1024]{2,1,0:T(8,128)(2,1)S(1)} %copy-done.2), channel_id=1, source_target_pairs={{0,2},{1,3},{2,0},{3,1},{4,6},{5,7},{6,4},{7,5},{8,10},{9,11},{10,... | collective-permute-start | bytes 786440 | tf_op jit(solution)/shard_map/ppermute | solution.py:23
  12.4 1.4 %collective-permute-start.1 = (bf16[32,1536]{1,0:T(8,128)(2,1)S(1)}, bf16[32,1536]{1,0:T(8,128)(2,1)S(1)}, u32[]{:S(2)}, u32[]{:S(2)}) collective-permute-start(bf16[32,1536]{1,0:T(8,128)(2,1)S(1)} %shard_map.56.refs_1_), channel_id=1, source_target_pairs={{0,8},{8,0},{16,24},{24,16},{1,9},{9,1},{17,25},{25,17},{2,10},{10... | collective-permute-start | bytes 294920 | tf_op jit(solution)/shard_map/ppermute | solution.py:23
  14.5 4.9 %collective-permute-start.2 = (bf16[32,1536]{1,0:T(8,128)(2,1)S(1)}, bf16[32,1536]{1,0:T(8,128)(2,1)S(1)}, u32[]{:S(2)}, u32[]{:S(2)}) collective-permute-start(bf16[32,1536]{1,0:T(8,128)(2,1)S(1)} %shard_map.57), channel_id=1, source_target_pairs={{0,16},{8,24},{16,0},{24,8},{1,17},{9,25},{17,1},{25,9},{2,18},{10... | collective-permute-start | bytes 294920 | tf_op jit(solution)/shard_map/ppermute | solution.py:23
  20.2 8.2 %collective-permute-start.6 = (bf16[32,1536]{1,0:T(8,128)(2,1)S(1)}, bf16[32,1536]{1,0:T(8,128)(2,1)S(1)}, u32[]{:S(2)}, u32[]{:S(2)}) collective-permute-start(bf16[32,1536]{1,0:T(8,128)(2,1)S(1)} %shard_map.59), channel_id=1, source_target_pairs={{0,6},{1,7},{2,4},{3,5},{4,2},{5,3},{6,0},{7,1},{8,14},{9,15},{10,... | collective-permute-start | bytes 294920 | tf_op jit(solution)/shard_map/ppermute | solution.py:23
  20.5 10.5 %collective-permute-start.10 = (bf16[32,1536]{1,0:T(8,128)(2,1)S(1)}, bf16[32,1536]{1,0:T(8,128)(2,1)S(1)}, u32[]{:S(2)}, u32[]{:S(2)}) collective-permute-start(bf16[32,1536]{1,0:T(8,128)(2,1)S(1)} %shard_map.59), channel_id=1, source_target_pairs={{0,2},{1,3},{2,0},{3,1},{4,6},{5,7},{6,4},{7,5},{8,10},{9,11},{10,... | collective-permute-start | bytes 294920 | tf_op jit(solution)/shard_map/ppermute | solution.py:23
  23.5 23.0 %copy-start.3 = (bf16[4,256,256]{2,1,0:T(8,128)(2,1)S(1)}, bf16[4,256,256]{2,1,0:T(8,128)(2,1)}, u32[]{:S(2)}) copy-start(bf16[4,256,256]{2,1,0:T(8,128)(2,1)} %refs_5_.1) | copy-start | bytes 1572868
  23.5 8.0 %collective-permute-start.12 = (bf16[32,1536]{1,0:T(8,128)(2,1)S(1)}, bf16[32,1536]{1,0:T(8,128)(2,1)S(1)}, u32[]{:S(2)}, u32[]{:S(2)}) collective-permute-start(bf16[32,1536]{1,0:T(8,128)(2,1)S(1)} %shard_map.59), channel_id=1, source_target_pairs={{0,4},{1,5},{2,6},{3,7},{4,0},{5,1},{6,2},{7,3},{8,12},{9,13},{10,... | collective-permute-start | bytes 294920 | tf_op jit(solution)/shard_map/ppermute | solution.py:23
  26.7 15.9 %collective-permute-start.5 = (bf16[512,512]{1,0:T(8,128)(2,1)S(1)}, bf16[512,512]{1,0:T(8,128)(2,1)S(1)}, u32[]{:S(2)}, u32[]{:S(2)}) collective-permute-start(bf16[512,512]{1,0:T(8,128)(2,1)S(1)} %shard_map.60), channel_id=1, source_target_pairs={{0,16},{8,24},{16,0},{24,8},{1,17},{9,25},{17,1},{25,9},{2,18},{10... | collective-permute-start | bytes 1572872 | tf_op jit(solution)/shard_map/ppermute | solution.py:23
  28.5 8.9 %collective-permute-start.7 = (bf16[4,32,1024]{2,1,0:T(8,128)(2,1)S(1)}, bf16[4,32,1024]{2,1,0:T(8,128)(2,1)S(1)}, u32[]{:S(2)}, u32[]{:S(2)}) collective-permute-start(bf16[4,32,1024]{2,1,0:T(8,128)(2,1)S(1)} %collective-permute-done.4.refs_15_), channel_id=1, source_target_pairs={{0,1},{1,0},{2,3},{3,2},{4,5},{5,4},{6,7},{7,6},{8,9},{9,8},{10,11... | collective-permute-start | bytes 786440 | tf_op jit(solution)/shard_map/ppermute | solution.py:23
  29.0 13.6 %collective-permute-start.8 = (bf16[4,32,1024]{2,1,0:T(8,128)(2,1)S(1)}, bf16[4,32,1024]{2,1,0:T(8,128)(2,1)S(1)}, u32[]{:S(2)}, u32[]{:S(2)}) collective-permute-start(bf16[4,32,1024]{2,1,0:T(8,128)(2,1)S(1)} %collective-permute-done.3.refs_12_), channel_id=1, source_target_pairs={{0,2},{1,3},{2,0},{3,1},{4,6},{5,7},{6,4},{7,5},{8,10},{9,11},{10,... | collective-permute-start | bytes 786440 | tf_op jit(solution)/shard_map/ppermute | solution.py:23
  31.5 11.8 %collective-permute-start.13 = (bf16[128,1536]{1,0:T(8,128)(2,1)S(1)}, bf16[128,1536]{1,0:T(8,128)(2,1)S(1)}, u32[]{:S(2)}, u32[]{:S(2)}) collective-permute-start(bf16[128,1536]{1,0:T(8,128)(2,1)S(1)} %pad_maximum_fusion.refs_6_), channel_id=1, source_target_pairs={{0,1},{1,0},{2,3},{3,2},{4,5},{5,4},{6,7},{7,6},{8,9},{9,8},{10,11... | collective-permute-start | bytes 1179656 | tf_op jit(solution)/shard_map/ppermute | solution.py:23
  32.6 10.5 %collective-permute-start.15 = (bf16[4,32,1024]{2,1,0:T(8,128)(2,1)S(1)}, bf16[4,32,1024]{2,1,0:T(8,128)(2,1)S(1)}, u32[]{:S(2)}, u32[]{:S(2)}) collective-permute-start(bf16[4,32,1024]{2,1,0:T(8,128)(2,1)S(1)} %copy-done.2), channel_id=1, source_target_pairs={{0,6},{1,7},{2,4},{3,5},{4,2},{5,3},{6,0},{7,1},{8,14},{9,15},{10,... | collective-permute-start | bytes 786440 | tf_op jit(solution)/shard_map/ppermute | solution.py:23
  42.6 1.9 %collective-permute-start.9 = (bf16[512,512]{1,0:T(8,128)(2,1)S(1)}, bf16[512,512]{1,0:T(8,128)(2,1)S(1)}, u32[]{:S(2)}, u32[]{:S(2)}) collective-permute-start(bf16[512,512]{1,0:T(8,128)(2,1)S(1)} %collective-permute-done.5.refs_3_), channel_id=1, source_target_pairs={{0,8},{8,0},{16,24},{24,16},{1,9},{9,1},{17,25},{25,17},{2,10},{10... | collective-permute-start | bytes 1572872 | tf_op jit(solution)/shard_map/ppermute | solution.py:23
  42.6 3.8 %collective-permute-start.14 = (bf16[128,1536]{1,0:T(8,128)(2,1)S(1)}, bf16[128,1536]{1,0:T(8,128)(2,1)S(1)}, u32[]{:S(2)}, u32[]{:S(2)}) collective-permute-start(bf16[128,1536]{1,0:T(8,128)(2,1)S(1)} %pad_maximum_fusion.refs_6_), channel_id=1, source_target_pairs={{0,8},{8,0},{16,24},{24,16},{1,9},{9,1},{17,25},{25,17},{2,10},{10... | collective-permute-start | bytes 1179656 | tf_op jit(solution)/shard_map/ppermute | solution.py:23
  43.3 3.2 %collective-permute-start.16 = (bf16[128,1536]{1,0:T(8,128)(2,1)S(1)}, bf16[128,1536]{1,0:T(8,128)(2,1)S(1)}, u32[]{:S(2)}, u32[]{:S(2)}) collective-permute-start(bf16[128,1536]{1,0:T(8,128)(2,1)S(1)} %collective-permute-done.13.refs_7_), channel_id=1, source_target_pairs={{0,8},{8,0},{16,24},{24,16},{1,9},{9,1},{17,25},{25,17},{2,10},{10... | collective-permute-start | bytes 1179656 | tf_op jit(solution)/shard_map/ppermute | solution.py:23
  43.3 8.7 %collective-permute-start.17 = (bf16[4,32,1024]{2,1,0:T(8,128)(2,1)S(1)}, bf16[4,32,1024]{2,1,0:T(8,128)(2,1)S(1)}, u32[]{:S(2)}, u32[]{:S(2)}) collective-permute-start(bf16[4,32,1024]{2,1,0:T(8,128)(2,1)S(1)} %collective-permute-done.15.refs_17_), channel_id=1, source_target_pairs={{0,1},{1,0},{2,3},{3,2},{4,5},{5,4},{6,7},{7,6},{8,9},{9,8},{10,11... | collective-permute-start | bytes 786440 | tf_op jit(solution)/shard_map/ppermute | solution.py:23

commit v8 on v6

--- a/solution.py
+++ b/solution.py
@@ -444,9 +444,9 @@
         return pl.pallas_call(
             update_kernel,
             out_shape=bf(row_dev, columns),
-            grid=(row_dev // 512,),
-            in_specs=[pl.BlockSpec((512, columns), lambda i: (i, 0))] + [VMEM] * 3,
-            out_specs=pl.BlockSpec((512, columns), lambda i: (i, 0)),
+            grid=(row_dev // W,),
+            in_specs=[pl.BlockSpec((W, columns), lambda i: (i, 0))] + [VMEM] * 3,
+            out_specs=pl.BlockSpec((W, columns), lambda i: (i, 0)),
             cost_estimate=COST,
             compiler_params=pltpu.CompilerParams(vmem_limit_bytes=40 * 1024 * 1024),
         )(base, weight, mix, bulk[-1])

time: 53.7 us -> 54.5 us (1.015)
  Pallas kernels: 13.3 us -> 13.9 us
    pallas_call x1, Pallas kernels: 1.46 us -> 2.21 us  [on_device(): pl.pallas_call(update_kernel, out_shape=bf(row_dev, columns), grid=(row_d...]
  transfers between devices with their start and end apart: 18 -> 18, of which waited for: 9 -> 9; matrix products, arithmetic and copies ran while one was open for 0% -> 0% of each run, Pallas kernels for 22% -> 21%
where the time goes in v8:
time: 54.5 us; the launch traced here: 54.2 us
  starting transfers between devices  24.3 us (45%)
  waiting for transfers between devices  14 us (26%)
  Pallas kernels  13.9 us (26%)
  local copies, waits for them, and re-layouts  1.93 us (4%)
    ppermute x18, starting transfers between devices, swap(): return lax.ppermute(value, axis, [(i, i ^ mask) for i in range(size)])  24.3 us
    ppermute x18, waiting for transfers between devices, swap(): return lax.ppermute(value, axis, [(i, i ^ mask) for i in range(size)])  14 us
    pallas_call x8, Pallas kernels, call(): pl.pallas_call(body, out_shape=shapes, in_specs=[SMEM] * n_smem + [VMEM]...  11.7 us
    pallas_call x1, Pallas kernels, on_device(): pl.pallas_call(update_kernel, out_shape=bf(row_dev, columns), grid=(row_d...  2.21 us
    unnamed x12, local copies, waits for them, and re-layouts  1.93 us
  transfers between devices with their start and end apart: 18, of which 9 were waited for; matrix products, arithmetic and copies ran while one was open for 0% of the time, Pallas kernels for 21%

profile of v8, /device:TPU:0, one launch (start us, length us, event | category | flops | bytes accessed | tf_op | source)
XLA Modules:
  0.0 54.2 jit_solution(11378234846256141988)
XLA Ops:
  0.0 1.2 %copy-done = bf16[1024,512]{1,0:T(8,128)(2,1)S(1)} copy-done((bf16[1024,512]{1,0:T(8,128)(2,1)S(1)}, bf16[1024,512]{1,0:T(8,128)(2,1)}, u32[]{:S(2)}) %copy-start) | copy-done | bytes 1048600
  1.2 0.7 %copy-done.4 = s32[4,256]{1,0:T(4,128)S(1)} copy-done((s32[4,256]{1,0:T(4,128)S(1)}, s32[4,256]{1,0:T(4,128)}, u32[]{:S(2)}) %copy-start.4) | copy-done | bytes 4120
  2.1 2.4 %collective-permute-start = (bf16[1024,512]{1,0:T(8,128)(2,1)S(1)}, bf16[1024,512]{1,0:T(8,128)(2,1)S(1)}, u32[]{:S(2)}, u32[]{:S(2)}) collective-permute-start(bf16[1024,512]{1,0:T(8,128)(2,1)S(1)} %shard_map.55.refs_1_), channel_id=1, source_target_pairs={{0,8},{8,0},{16,24},{24,16},{1,9},{9,1},{17,25},{25,17},{2,10},{10... | collective-permute-start | bytes 3145736 | tf_op jit(solution)/shard_map/ppermute | solution.py:23
  4.6 2.3 %collective-permute-start.3 = (bf16[4,32,1024]{2,1,0:T(8,128)(2,1)S(1)}, bf16[4,32,1024]{2,1,0:T(8,128)(2,1)S(1)}, u32[]{:S(2)}, u32[]{:S(2)}) collective-permute-start(bf16[4,32,1024]{2,1,0:T(8,128)(2,1)S(1)} %copy-done.2), channel_id=1, source_target_pairs={{0,1},{1,0},{2,3},{3,2},{4,5},{5,4},{6,7},{7,6},{8,9},{9,8},{10,11... | collective-permute-start | bytes 786440 | tf_op jit(solution)/shard_map/ppermute | solution.py:23
  6.9 2.6 %collective-permute-start.4 = (bf16[4,32,1024]{2,1,0:T(8,128)(2,1)S(1)}, bf16[4,32,1024]{2,1,0:T(8,128)(2,1)S(1)}, u32[]{:S(2)}, u32[]{:S(2)}) collective-permute-start(bf16[4,32,1024]{2,1,0:T(8,128)(2,1)S(1)} %copy-done.2), channel_id=1, source_target_pairs={{0,4},{1,5},{2,6},{3,7},{4,0},{5,1},{6,2},{7,3},{8,12},{9,13},{10,... | collective-permute-start | bytes 786440 | tf_op jit(solution)/shard_map/ppermute | solution.py:23
  9.5 1.6 %collective-permute-start.11 = (bf16[4,32,1024]{2,1,0:T(8,128)(2,1)S(1)}, bf16[4,32,1024]{2,1,0:T(8,128)(2,1)S(1)}, u32[]{:S(2)}, u32[]{:S(2)}) collective-permute-start(bf16[4,32,1024]{2,1,0:T(8,128)(2,1)S(1)} %copy-done.2), channel_id=1, source_target_pairs={{0,2},{1,3},{2,0},{3,1},{4,6},{5,7},{6,4},{7,5},{8,10},{9,11},{10,... | collective-permute-start | bytes 786440 | tf_op jit(solution)/shard_map/ppermute | solution.py:23
  11.1 1.4 %shard_map.56.refs_1_ = bf16[32,1536]{1,0:T(8,128)(2,1)S(1)} custom-call(s32[4,8]{1,0:T(4,128)S(1)} %copy-done.5, s32[4,256]{1,0:T(4,128)S(1)} %copy-done.4, bf16[4,32,1024]{2,1,0:T(8,128)(2,1)S(1)} %copy-done.2), custom_call_target="tpu_custom_call" | custom-call | flops 1000 | bytes 1000 | tf_op jit(solution)/shard_map/pallas_call | solution.py:340
  12.5 1.3 %collective-permute-done.1.refs_2_ = bf16[32,1536]{1,0:T(8,128)(2,1)S(1)} collective-permute-done((bf16[32,1536]{1,0:T(8,128)(2,1)S(1)}, bf16[32,1536]{1,0:T(8,128)(2,1)S(1)}, u32[]{:S(2)}, u32[]{:S(2)}) %collective-permute-start.1) | collective-permute-done | bytes 98336 | tf_op jit(solution)/shard_map/ppermute | solution.py:23
  13.8 0.7 %shard_map.57 = bf16[32,1536]{1,0:T(8,128)(2,1)S(1)} custom-call(s32[4,256]{1,0:T(4,128)S(1)} %copy-done.4, bf16[32,1536]{1,0:T(8,128)(2,1)S(1)} %shard_map.56.refs_1_, bf16[32,1536]{1,0:T(8,128)(2,1)S(1)} %collective-permute-done.1.refs_2_), custom_call_target="tpu_custom_call" | custom-call | flops 1000 | bytes 1000 | tf_op jit(solution)/shard_map/pallas_call | solution.py:340
  14.5 1.8 %collective-permute-start.2 = (bf16[32,1536]{1,0:T(8,128)(2,1)S(1)}, bf16[32,1536]{1,0:T(8,128)(2,1)S(1)}, u32[]{:S(2)}, u32[]{:S(2)}) collective-permute-start(bf16[32,1536]{1,0:T(8,128)(2,1)S(1)} %shard_map.57), channel_id=1, source_target_pairs={{0,16},{8,24},{16,0},{24,8},{1,17},{9,25},{17,1},{25,9},{2,18},{10... | collective-permute-start | bytes 294920 | tf_op jit(solution)/shard_map/ppermute | solution.py:23
  16.4 2.8 %shard_map.58 = (bf16[1024,1024]{1,0:T(8,128)(2,1)S(1)}, bf16[1024,512]{1,0:T(8,128)(2,1)S(1)}, f32[8,1024]{1,0:T(8,128)S(1)}) custom-call(s32[4,8]{1,0:T(4,128)S(1)} %copy-done.5, s32[4,256]{1,0:T(4,128)S(1)} %copy-done.4, bf16[1024,512]{1,0:T(8,128)(2,1)S(1)} %copy-done.1), custom_call_target="tpu_custom_call" | custom-call | flops 1000 | bytes 1000 | tf_op jit(solution)/shard_map/pallas_call | solution.py:340
  19.2 0.3 collective-permute-done.2.refs_3_
  19.5 0.7 %shard_map.59 = bf16[32,1536]{1,0:T(8,128)(2,1)S(1)} custom-call(s32[4,256]{1,0:T(4,128)S(1)} %copy-done.4, bf16[32,1536]{1,0:T(8,128)(2,1)S(1)} %shard_map.56.refs_1_, bf16[32,1536]{1,0:T(8,128)(2,1)S(1)} %collective-permute-done.1.refs_2_, bf16[32,1536]{1,0:T(8,128)(2,1)S(1)} %collective-permute-done.2.refs_3_), custom_call_target="tpu_custom_call" | custom-call | flops 1000 | bytes 1000 | tf_op jit(solution)/shard_map/pallas_call | solution.py:340
  20.5 0.7 %collective-permute-start.8 = (bf16[32,1536]{1,0:T(8,128)(2,1)S(1)}, bf16[32,1536]{1,0:T(8,128)(2,1)S(1)}, u32[]{:S(2)}, u32[]{:S(2)}) collective-permute-start(bf16[32,1536]{1,0:T(8,128)(2,1)S(1)} %shard_map.59), channel_id=1, source_target_pairs={{0,2},{1,3},{2,0},{3,1},{4,6},{5,7},{6,4},{7,5},{8,10},{9,11},{10,... | collective-permute-start | bytes 294920 | tf_op jit(solution)/shard_map/ppermute | solution.py:23
  21.2 0.3 collective-permute-done.4.refs_15_
  21.5 1.9 %shard_map.60 = bf16[512,512]{1,0:T(8,128)(2,1)S(1)} custom-call(s32[4,256]{1,0:T(4,128)S(1)} %copy-done.4, bf16[1024,512]{1,0:T(8,128)(2,1)S(1)} %shard_map.55.refs_1_, bf16[1024,512]{1,0:T(8,128)(2,1)S(1)} %collective-permute-done.refs_2_), custom_call_target="tpu_custom_call" | custom-call | flops 1000 | bytes 1000 | tf_op jit(solution)/shard_map/pallas_call | solution.py:340
  23.5 3.2 %collective-permute-start.12 = (bf16[32,1536]{1,0:T(8,128)(2,1)S(1)}, bf16[32,1536]{1,0:T(8,128)(2,1)S(1)}, u32[]{:S(2)}, u32[]{:S(2)}) collective-permute-start(bf16[32,1536]{1,0:T(8,128)(2,1)S(1)} %shard_map.59), channel_id=1, source_target_pairs={{0,4},{1,5},{2,6},{3,7},{4,0},{5,1},{6,2},{7,3},{8,12},{9,13},{10,... | collective-permute-start | bytes 294920 | tf_op jit(solution)/shard_map/ppermute | solution.py:23
  26.7 1.7 %collective-permute-start.5 = (bf16[512,512]{1,0:T(8,128)(2,1)S(1)}, bf16[512,512]{1,0:T(8,128)(2,1)S(1)}, u32[]{:S(2)}, u32[]{:S(2)}) collective-permute-start(bf16[512,512]{1,0:T(8,128)(2,1)S(1)} %shard_map.60), channel_id=1, source_target_pairs={{0,16},{8,24},{16,0},{24,8},{1,17},{9,25},{17,1},{25,9},{2,18},{10... | collective-permute-start | bytes 1572872 | tf_op jit(solution)/shard_map/ppermute | solution.py:23
  28.5 0.5 collective-permute-start.7
  29.0 2.0 %collective-permute-start.9 = (bf16[4,32,1024]{2,1,0:T(8,128)(2,1)S(1)}, bf16[4,32,1024]{2,1,0:T(8,128)(2,1)S(1)}, u32[]{:S(2)}, u32[]{:S(2)}) collective-permute-start(bf16[4,32,1024]{2,1,0:T(8,128)(2,1)S(1)} %collective-permute-done.3.refs_12_), channel_id=1, source_target_pairs={{0,2},{1,3},{2,0},{3,1},{4,6},{5,7},{6,4},{7,5},{8,10},{9,11},{10,... | collective-permute-start | bytes 786440 | tf_op jit(solution)/shard_map/ppermute | solution.py:23
  31.0 0.4 collective-permute-done.12
  31.5 1.1 %collective-permute-start.13 = (bf16[128,1536]{1,0:T(8,128)(2,1)S(1)}, bf16[128,1536]{1,0:T(8,128)(2,1)S(1)}, u32[]{:S(2)}, u32[]{:S(2)}) collective-permute-start(bf16[128,1536]{1,0:T(8,128)(2,1)S(1)} %pad_maximum_fusion.refs_6_), channel_id=1, source_target_pairs={{0,1},{1,0},{2,3},{3,2},{4,5},{5,4},{6,7},{7,6},{8,9},{9,8},{10,11... | collective-permute-start | bytes 1179656 | tf_op jit(solution)/shard_map/ppermute | solution.py:23
  32.6 2.4 %collective-permute-start.15 = (bf16[4,32,1024]{2,1,0:T(8,128)(2,1)S(1)}, bf16[4,32,1024]{2,1,0:T(8,128)(2,1)S(1)}, u32[]{:S(2)}, u32[]{:S(2)}) collective-permute-start(bf16[4,32,1024]{2,1,0:T(8,128)(2,1)S(1)} %copy-done.2), channel_id=1, source_target_pairs={{0,6},{1,7},{2,4},{3,5},{4,2},{5,3},{6,0},{7,1},{8,14},{9,15},{10,... | collective-permute-start | bytes 786440 | tf_op jit(solution)/shard_map/ppermute | solution.py:23
  35.1 2.3 %collective-permute-done.7.refs_16_ = bf16[4,32,1024]{2,1,0:T(8,128)(2,1)S(1)} collective-permute-done((bf16[4,32,1024]{2,1,0:T(8,128)(2,1)S(1)}, bf16[4,32,1024]{2,1,0:T(8,128)(2,1)S(1)}, u32[]{:S(2)}, u32[]{:S(2)}) %collective-permute-start.7) | collective-permute-done | bytes 262176 | tf_op jit(solution)/shard_map/ppermute | solution.py:23
  37.4 5.3 %collective-permute-done.9.refs_14_ = bf16[4,32,1024]{2,1,0:T(8,128)(2,1)S(1)} collective-permute-done((bf16[4,32,1024]{2,1,0:T(8,128)(2,1)S(1)}, bf16[4,32,1024]{2,1,0:T(8,128)(2,1)S(1)}, u32[]{:S(2)}, u32[]{:S(2)}) %collective-permute-start.9) | collective-permute-done | bytes 262176 | tf_op jit(solution)/shard_map/ppermute | solution.py:23
  42.6 0.5 collective-permute-start.14
  43.3 0.9 %collective-permute-start.17 = (bf16[4,32,1024]{2,1,0:T(8,128)(2,1)S(1)}, bf16[4,32,1024]{2,1,0:T(8,128)(2,1)S(1)}, u32[]{:S(2)}, u32[]{:S(2)}) collective-permute-start(bf16[4,32,1024]{2,1,0:T(8,128)(2,1)S(1)} %collective-permute-done.15.refs_17_), channel_id=1, source_target_pairs={{0,1},{1,0},{2,3},{3,2},{4,5},{5,4},{6,7},{7,6},{8,9},{9,8},{10,11... | collective-permute-start | bytes 786440 | tf_op jit(solution)/shard_map/ppermute | solution.py:23
  44.2 0.4 collective-permute-done.10.refs_4_
  44.6 1.9 %shard_map.61 = (bf16[1024,512]{1,0:T(8,128)(2,1)S(1)}, bf16[1024,512]{1,0:T(8,128)(2,1)S(1)}) custom-call(s32[4,256]{1,0:T(4,128)S(1)} %copy-done.4, bf16[1024,512]{1,0:T(8,128)(2,1)S(1)} %shard_map.55.refs_1_, bf16[1024,512]{1,0:T(8,128)(2,1)S(1)} %collective-permute-done.refs_2_, bf16[512,512]{1,0:T(8,128)(2,1)S(1)} %collective-permute-done.5.refs_3_, ...), custom_call_target="tpu_custom_call" | custom-call | flops 1000 | bytes 1000 | tf_op jit(solution)/shard_map/pallas_call | solution.py:340
  46.5 2.0 %shard_map.62 = (bf16[1024,512]{1,0:T(8,128)(2,1)S(1)}, f32[1024,512]{1,0:T(8,128)S(1)}) custom-call(s32[4,256]{1,0:T(4,128)S(1)} %copy-done.4, bf16[1024,512]{1,0:T(8,128)(2,1)S(1)} %get-tuple-element.28.refs_1_, bf16[1024,512]{1,0:T(8,128)(2,1)S(1)} %get-tuple-element.29.refs_2_, bf16[1024,1024]{1,0:T(8,128)(2,1)S(1)} %get-tuple-element.30.refs_3_, ...), custom_call_target="tpu_custom_call" | custom-call | flops 1000 | bytes 1000 | tf_op jit(solution)/shard_map/pallas_call | solution.py:340
  48.5 3.5 %collective-permute-done.17.last = bf16[4,32,1024]{2,1,0:T(8,128)(2,1)S(1)} collective-permute-done((bf16[4,32,1024]{2,1,0:T(8,128)(2,1)S(1)}, bf16[4,32,1024]{2,1,0:T(8,128)(2,1)S(1)}, u32[]{:S(2)}, u32[]{:S(2)}) %collective-permute-start.17) | collective-permute-done | bytes 262176 | tf_op jit(solution)/shard_map/ppermute | solution.py:23
  52.0 2.2 %shard_map.63 = bf16[1024,512]{1,0:T(8,128)(2,1)} custom-call(f32[1024,512]{1,0:T(8,128)S(1)} %get-tuple-element.35.base, f32[8,1024]{1,0:T(8,128)S(1)} %get-tuple-element.22.refs_10_.weight, bf16[1024,512]{1,0:T(8,128)(2,1)S(1)} %get-tuple-element.36.mix, bf16[4,32,1024]{2,1,0:T(8,128)(2,1)S(1)} %collective-permute-done.17.last), custom_call_target="tpu_custom_call" | custom-call | flops 1000 | bytes 1000 | tf_op jit(solution)/shard_map/pallas_call | solution.py:444
  (26 shorter events, 0.8 us)
Async XLA Ops:
  0.0 1.2 %copy-start = (bf16[1024,512]{1,0:T(8,128)(2,1)S(1)}, bf16[1024,512]{1,0:T(8,128)(2,1)}, u32[]{:S(2)}) copy-start(bf16[1024,512]{1,0:T(8,128)(2,1)} %refs_2_.3) | copy-start | bytes 3145732
  1.2 0.7 %copy-start.4 = (s32[4,256]{1,0:T(4,128)S(1)}, s32[4,256]{1,0:T(4,128)}, u32[]{:S(2)}) copy-start(s32[4,256]{1,0:T(4,128)} %refs_0_.14) | copy-start | bytes 12292
  1.9 2.6 %copy-start.2 = (bf16[4,32,1024]{2,1,0:T(8,128)(2,1)S(1)}, bf16[4,32,1024]{2,1,0:T(8,128)(2,1)}, u32[]{:S(2)}) copy-start(bf16[4,32,1024]{2,1,0:T(8,128)(2,1)} %refs_11_.1) | copy-start | bytes 786436
  1.9 9.1 %copy-start.5 = (s32[4,8]{1,0:T(4,128)S(1)}, s32[4,8]{1,0:T(4,128)}, u32[]{:S(2)}) copy-start(s32[4,8]{1,0:T(4,128)} %refs_0_.10) | copy-start | bytes 388
  1.9 14.5 %copy-start.1 = (bf16[1024,512]{1,0:T(8,128)(2,1)S(1)}, bf16[1024,512]{1,0:T(8,128)(2,1)}, u32[]{:S(2)}) copy-start(bf16[1024,512]{1,0:T(8,128)(2,1)} %refs_2_.3) | copy-start | bytes 3145732
  2.1 19.4 %collective-permute-start = (bf16[1024,512]{1,0:T(8,128)(2,1)S(1)}, bf16[1024,512]{1,0:T(8,128)(2,1)S(1)}, u32[]{:S(2)}, u32[]{:S(2)}) collective-permute-start(bf16[1024,512]{1,0:T(8,128)(2,1)S(1)} %shard_map.55.refs_1_), channel_id=1, source_target_pairs={{0,8},{8,0},{16,24},{24,16},{1,9},{9,1},{17,25},{25,17},{2,10},{10... | collective-permute-start | bytes 3145736 | tf_op jit(solution)/shard_map/ppermute | solution.py:23
  4.6 14.9 %collective-permute-start.3 = (bf16[4,32,1024]{2,1,0:T(8,128)(2,1)S(1)}, bf16[4,32,1024]{2,1,0:T(8,128)(2,1)S(1)}, u32[]{:S(2)}, u32[]{:S(2)}) collective-permute-start(bf16[4,32,1024]{2,1,0:T(8,128)(2,1)S(1)} %copy-done.2), channel_id=1, source_target_pairs={{0,1},{1,0},{2,3},{3,2},{4,5},{5,4},{6,7},{7,6},{8,9},{9,8},{10,11... | collective-permute-start | bytes 786440 | tf_op jit(solution)/shard_map/ppermute | solution.py:23
  6.9 14.6 %collective-permute-start.4 = (bf16[4,32,1024]{2,1,0:T(8,128)(2,1)S(1)}, bf16[4,32,1024]{2,1,0:T(8,128)(2,1)S(1)}, u32[]{:S(2)}, u32[]{:S(2)}) collective-permute-start(bf16[4,32,1024]{2,1,0:T(8,128)(2,1)S(1)} %copy-done.2), channel_id=1, source_target_pairs={{0,4},{1,5},{2,6},{3,7},{4,0},{5,1},{6,2},{7,3},{8,12},{9,13},{10,... | collective-permute-start | bytes 786440 | tf_op jit(solution)/shard_map/ppermute | solution.py:23
  9.5 14.0 %collective-permute-start.11 = (bf16[4,32,1024]{2,1,0:T(8,128)(2,1)S(1)}, bf16[4,32,1024]{2,1,0:T(8,128)(2,1)S(1)}, u32[]{:S(2)}, u32[]{:S(2)}) collective-permute-start(bf16[4,32,1024]{2,1,0:T(8,128)(2,1)S(1)} %copy-done.2), channel_id=1, source_target_pairs={{0,2},{1,3},{2,0},{3,1},{4,6},{5,7},{6,4},{7,5},{8,10},{9,11},{10,... | collective-permute-start | bytes 786440 | tf_op jit(solution)/shard_map/ppermute | solution.py:23
  12.4 1.4 %collective-permute-start.1 = (bf16[32,1536]{1,0:T(8,128)(2,1)S(1)}, bf16[32,1536]{1,0:T(8,128)(2,1)S(1)}, u32[]{:S(2)}, u32[]{:S(2)}) collective-permute-start(bf16[32,1536]{1,0:T(8,128)(2,1)S(1)} %shard_map.56.refs_1_), channel_id=1, source_target_pairs={{0,8},{8,0},{16,24},{24,16},{1,9},{9,1},{17,25},{25,17},{2,10},{10... | collective-permute-start | bytes 294920 | tf_op jit(solution)/shard_map/ppermute | solution.py:23
  14.5 4.9 %collective-permute-start.2 = (bf16[32,1536]{1,0:T(8,128)(2,1)S(1)}, bf16[32,1536]{1,0:T(8,128)(2,1)S(1)}, u32[]{:S(2)}, u32[]{:S(2)}) collective-permute-start(bf16[32,1536]{1,0:T(8,128)(2,1)S(1)} %shard_map.57), channel_id=1, source_target_pairs={{0,16},{8,24},{16,0},{24,8},{1,17},{9,25},{17,1},{25,9},{2,18},{10... | collective-permute-start | bytes 294920 | tf_op jit(solution)/shard_map/ppermute | solution.py:23
  20.2 8.2 %collective-permute-start.6 = (bf16[32,1536]{1,0:T(8,128)(2,1)S(1)}, bf16[32,1536]{1,0:T(8,128)(2,1)S(1)}, u32[]{:S(2)}, u32[]{:S(2)}) collective-permute-start(bf16[32,1536]{1,0:T(8,128)(2,1)S(1)} %shard_map.59), channel_id=1, source_target_pairs={{0,6},{1,7},{2,4},{3,5},{4,2},{5,3},{6,0},{7,1},{8,14},{9,15},{10,... | collective-permute-start | bytes 294920 | tf_op jit(solution)/shard_map/ppermute | solution.py:23
  20.5 8.5 %collective-permute-start.8 = (bf16[32,1536]{1,0:T(8,128)(2,1)S(1)}, bf16[32,1536]{1,0:T(8,128)(2,1)S(1)}, u32[]{:S(2)}, u32[]{:S(2)}) collective-permute-start(bf16[32,1536]{1,0:T(8,128)(2,1)S(1)} %shard_map.59), channel_id=1, source_target_pairs={{0,2},{1,3},{2,0},{3,1},{4,6},{5,7},{6,4},{7,5},{8,10},{9,11},{10,... | collective-permute-start | bytes 294920 | tf_op jit(solution)/shard_map/ppermute | solution.py:23
  23.5 23.0 %copy-start.3 = (bf16[4,256,256]{2,1,0:T(8,128)(2,1)S(1)}, bf16[4,256,256]{2,1,0:T(8,128)(2,1)}, u32[]{:S(2)}) copy-start(bf16[4,256,256]{2,1,0:T(8,128)(2,1)} %refs_5_.1) | copy-start | bytes 1572868
  23.5 8.0 %collective-permute-start.12 = (bf16[32,1536]{1,0:T(8,128)(2,1)S(1)}, bf16[32,1536]{1,0:T(8,128)(2,1)S(1)}, u32[]{:S(2)}, u32[]{:S(2)}) collective-permute-start(bf16[32,1536]{1,0:T(8,128)(2,1)S(1)} %shard_map.59), channel_id=1, source_target_pairs={{0,4},{1,5},{2,6},{3,7},{4,0},{5,1},{6,2},{7,3},{8,12},{9,13},{10,... | collective-permute-start | bytes 294920 | tf_op jit(solution)/shard_map/ppermute | solution.py:23
  26.7 15.9 %collective-permute-start.5 = (bf16[512,512]{1,0:T(8,128)(2,1)S(1)}, bf16[512,512]{1,0:T(8,128)(2,1)S(1)}, u32[]{:S(2)}, u32[]{:S(2)}) collective-permute-start(bf16[512,512]{1,0:T(8,128)(2,1)S(1)} %shard_map.60), channel_id=1, source_target_pairs={{0,16},{8,24},{16,0},{24,8},{1,17},{9,25},{17,1},{25,9},{2,18},{10... | collective-permute-start | bytes 1572872 | tf_op jit(solution)/shard_map/ppermute | solution.py:23
  28.5 8.9 %collective-permute-start.7 = (bf16[4,32,1024]{2,1,0:T(8,128)(2,1)S(1)}, bf16[4,32,1024]{2,1,0:T(8,128)(2,1)S(1)}, u32[]{:S(2)}, u32[]{:S(2)}) collective-permute-start(bf16[4,32,1024]{2,1,0:T(8,128)(2,1)S(1)} %collective-permute-done.4.refs_15_), channel_id=1, source_target_pairs={{0,1},{1,0},{2,3},{3,2},{4,5},{5,4},{6,7},{7,6},{8,9},{9,8},{10,11... | collective-permute-start | bytes 786440 | tf_op jit(solution)/shard_map/ppermute | solution.py:23
  29.0 13.6 %collective-permute-start.9 = (bf16[4,32,1024]{2,1,0:T(8,128)(2,1)S(1)}, bf16[4,32,1024]{2,1,0:T(8,128)(2,1)S(1)}, u32[]{:S(2)}, u32[]{:S(2)}) collective-permute-start(bf16[4,32,1024]{2,1,0:T(8,128)(2,1)S(1)} %collective-permute-done.3.refs_12_), channel_id=1, source_target_pairs={{0,2},{1,3},{2,0},{3,1},{4,6},{5,7},{6,4},{7,5},{8,10},{9,11},{10,... | collective-permute-start | bytes 786440 | tf_op jit(solution)/shard_map/ppermute | solution.py:23
  31.5 11.8 %collective-permute-start.13 = (bf16[128,1536]{1,0:T(8,128)(2,1)S(1)}, bf16[128,1536]{1,0:T(8,128)(2,1)S(1)}, u32[]{:S(2)}, u32[]{:S(2)}) collective-permute-start(bf16[128,1536]{1,0:T(8,128)(2,1)S(1)} %pad_maximum_fusion.refs_6_), channel_id=1, source_target_pairs={{0,1},{1,0},{2,3},{3,2},{4,5},{5,4},{6,7},{7,6},{8,9},{9,8},{10,11... | collective-permute-start | bytes 1179656 | tf_op jit(solution)/shard_map/ppermute | solution.py:23
  32.6 10.5 %collective-permute-start.15 = (bf16[4,32,1024]{2,1,0:T(8,128)(2,1)S(1)}, bf16[4,32,1024]{2,1,0:T(8,128)(2,1)S(1)}, u32[]{:S(2)}, u32[]{:S(2)}) collective-permute-start(bf16[4,32,1024]{2,1,0:T(8,128)(2,1)S(1)} %copy-done.2), channel_id=1, source_target_pairs={{0,6},{1,7},{2,4},{3,5},{4,2},{5,3},{6,0},{7,1},{8,14},{9,15},{10,... | collective-permute-start | bytes 786440 | tf_op jit(solution)/shard_map/ppermute | solution.py:23
  42.6 1.9 %collective-permute-start.10 = (bf16[512,512]{1,0:T(8,128)(2,1)S(1)}, bf16[512,512]{1,0:T(8,128)(2,1)S(1)}, u32[]{:S(2)}, u32[]{:S(2)}) collective-permute-start(bf16[512,512]{1,0:T(8,128)(2,1)S(1)} %collective-permute-done.5.refs_3_), channel_id=1, source_target_pairs={{0,8},{8,0},{16,24},{24,16},{1,9},{9,1},{17,25},{25,17},{2,10},{10... | collective-permute-start | bytes 1572872 | tf_op jit(solution)/shard_map/ppermute | solution.py:23
  42.6 3.8 %collective-permute-start.14 = (bf16[128,1536]{1,0:T(8,128)(2,1)S(1)}, bf16[128,1536]{1,0:T(8,128)(2,1)S(1)}, u32[]{:S(2)}, u32[]{:S(2)}) collective-permute-start(bf16[128,1536]{1,0:T(8,128)(2,1)S(1)} %pad_maximum_fusion.refs_6_), channel_id=1, source_target_pairs={{0,8},{8,0},{16,24},{24,16},{1,9},{9,1},{17,25},{25,17},{2,10},{10... | collective-permute-start | bytes 1179656 | tf_op jit(solution)/shard_map/ppermute | solution.py:23
  43.3 3.2 %collective-permute-start.16 = (bf16[128,1536]{1,0:T(8,128)(2,1)S(1)}, bf16[128,1536]{1,0:T(8,128)(2,1)S(1)}, u32[]{:S(2)}, u32[]{:S(2)}) collective-permute-start(bf16[128,1536]{1,0:T(8,128)(2,1)S(1)} %collective-permute-done.13.refs_7_), channel_id=1, source_target_pairs={{0,8},{8,0},{16,24},{24,16},{1,9},{9,1},{17,25},{25,17},{2,10},{10... | collective-permute-start | bytes 1179656 | tf_op jit(solution)/shard_map/ppermute | solution.py:23
  43.3 8.7 %collective-permute-start.17 = (bf16[4,32,1024]{2,1,0:T(8,128)(2,1)S(1)}, bf16[4,32,1024]{2,1,0:T(8,128)(2,1)S(1)}, u32[]{:S(2)}, u32[]{:S(2)}) collective-permute-start(bf16[4,32,1024]{2,1,0:T(8,128)(2,1)S(1)} %collective-permute-done.15.refs_17_), channel_id=1, source_target_pairs={{0,1},{1,0},{2,3},{3,2},{4,5},{5,4},{6,7},{7,6},{8,9},{9,8},{10,11... | collective-permute-start | bytes 786440 | tf_op jit(solution)/shard_map/ppermute | solution.py:23
